TPU v7x, 128 devices: a whole 4x4x4 slice. The times are simulated.
128 devices in a mesh: row: 8 (over z, core), col: 16 (over y, x).
Axes of the slice: x: 4, y: 4, z: 4, core: 2. Of those that a mesh axis runs over, the one named last changes fastest.
Arguments:
- trail_cov: float32 [16384, 16384], P('row', 'col')
- panel_two_rows: float32 [16384, 512], P('row'), may hold values from -0.046875 to 0.046875
- diag_inv_two: float32 [512, 512], replicated
- panel_one_top: float32 [512, 512], replicated, may hold values from -0.25 to 0.25
- panel_one_rows: float32 [16384, 512], P('row'), may hold values from -0.046875 to 0.046875
- diag_inv_one: float32 [512, 512], replicated
- pattern_two: int32 [128], replicated, may hold values 0 or 1
- pattern_one: int32 [132], replicated, may hold values from 0 to 1, as said below
- loadings: bfloat16 [262144, 256], P(('row', 'col')), may hold values from -0.5 to 0.5
- unit_block: int32 [262144, 1], P(('row', 'col')), may hold values from 0 to 127; in each aligned block of 2048 rows (0 to 2047, 2048 to 4095, ...) at most 32 rows name the same one
- block_panel: int32 [128], replicated, may hold values from 0 to 3
- counts: int32 [262144], P(('row', 'col')), may hold values from 0 to 31
- shape_par: float32 [262144], P(('row', 'col')), may hold values from 0.5 to 5
- exposure: float32 [262144], P(('row', 'col')), may hold values from 0.2 to 5
Outputs:
- cov_two: float32 [16384, 512], P(('row', 'col'))
- top_cov: float32 [512, 512], replicated
- cov_one: float32 [16384, 512], P(('row', 'col'))
- diag_two: float32 [512, 512], replicated
- diag_one: float32 [512, 512], replicated
- shape_grad: float32 [262144], P(('row', 'col'))
Inputs may be any that keep to these rules, and one draw needn't show every extreme that they name: `unit_block`: among the histories of one device, no trailing block is named by more than 32 of them, and some block by exactly 32. `pattern_one`: at least one of the first 4 entries is 1.
All inputs are finite; a program needn't handle non-finite values.
Results may differ from a plain program's by a relative error of at most 0.0003.
Values may be sent and summed in bfloat16 or wider, within the bound.
No kernel may reach another device: no remote copies, remote signals or barrier semaphores. Data moves between devices by JAX's collectives and lax.ppermute only.
A program may use at most 192 MiB of HBM per device.

v0:
```python
import jax
import jax.numpy as jnp
from jax import lax
from jax.sharding import PartitionSpec as P

HIGH = lax.Precision.HIGHEST


def spread(block, axis, owner):
    block = jnp.where(lax.axis_index(axis) == owner, block, jnp.zeros_like(block))
    return lax.psum(block, axis)


def matmul(left, right):
    return jnp.dot(left, right, precision=HIGH, preferred_element_type=jnp.float32)


def tmatmul(left, right):
    return lax.dot_general(
        left, right, (((0,), (0,)), ((), ())), precision=HIGH, preferred_element_type=jnp.float32
    )


def row_mask(bits, block_width):
    return jnp.repeat(bits.astype(jnp.float32), block_width)[:, None]


def local(
    trail_cov,
    panel_two_rows,
    diag_inv_two,
    panel_one_top,
    panel_one_rows,
    diag_inv_one,
    pattern_two,
    pattern_one,
    loadings,
    unit_block,
    block_panel,
    counts,
    shape_par,
    exposure,
):
    row_count = lax.axis_size("row")
    col_count = lax.axis_size("col")
    row_index = lax.axis_index("row")
    col_index = lax.axis_index("col")
    ratio = col_count // row_count
    width = diag_inv_two.shape[0]
    block_width = loadings.shape[1] // 2
    top_blocks = width // block_width
    col_span = trail_cov.shape[1]
    owner = row_index * col_count + col_index
    root = col_index // ratio
    offset = col_index % ratio * col_span
    mask_two = row_mask(
        lax.dynamic_slice_in_dim(pattern_two, row_index * col_count, col_count), block_width
    )
    mask_one = row_mask(
        lax.dynamic_slice_in_dim(pattern_one, top_blocks + row_index * col_count, col_count),
        block_width,
    )
    mask_top = row_mask(pattern_one[:top_blocks], block_width)
    norm_two = matmul(mask_two * panel_two_rows, diag_inv_two)
    norm_one = matmul(mask_one * panel_one_rows, diag_inv_one)
    norm_top = matmul(mask_top * panel_one_top, diag_inv_one)
    cols_two = spread(lax.dynamic_slice_in_dim(norm_two, offset, col_span, 0), "row", root)
    cols_one = spread(lax.dynamic_slice_in_dim(norm_one, offset, col_span, 0), "row", root)
    gram_two = tmatmul(diag_inv_two, diag_inv_two)
    gram_one = tmatmul(diag_inv_one, diag_inv_one)
    image_two = lax.psum(matmul(trail_cov, cols_two), "col")
    rows_two = -mask_two * image_two
    diag_two = gram_two - lax.psum(tmatmul(norm_two, rows_two), "row")
    cross = lax.psum(tmatmul(rows_two, norm_one), "row")
    top_cov = -mask_top * (matmul(diag_two, norm_top) + cross)
    image_one = lax.psum(matmul(trail_cov, cols_one), "col")
    rows_one = -mask_one * (matmul(rows_two, norm_top) + image_one)
    diag_one = gram_one - tmatmul(norm_top, top_cov) - lax.psum(tmatmul(norm_one, rows_one), "row")
    cov_two = lax.dynamic_slice_in_dim(rows_two, col_index * block_width, block_width, 0)
    cov_one = lax.dynamic_slice_in_dim(rows_one, col_index * block_width, block_width, 0)
    square = lax.dynamic_slice_in_dim(trail_cov, offset, col_span, 0)
    grid = square.reshape(row_count, block_width, row_count, block_width)
    tiles = jnp.moveaxis(jnp.diagonal(grid, axis1=0, axis2=2), -1, 0)
    held = jnp.where(root == row_index, 1.0, 0.0).astype(jnp.float32) * tiles
    placed = lax.dynamic_update_slice_in_dim(
        jnp.zeros((col_count, block_width, block_width), jnp.float32),
        held,
        col_index % ratio * row_count,
        0,
    )
    own_tile = lax.psum_scatter(placed, "col", scatter_dimension=0, tiled=True)[0]
    panel = block_panel[owner]
    cross_tile = lax.dynamic_slice(cov_one, (0, panel * block_width), (block_width, block_width))
    inner_tile = lax.dynamic_slice(
        diag_one, (panel * block_width, panel * block_width), (block_width, block_width)
    )
    blocks = unit_block[:, 0]
    block_total = row_count * col_count
    capacity = 2 * loadings.shape[0] // block_total
    hits = (blocks[:, None] == jnp.arange(block_total, dtype=jnp.int32)[None, :]).astype(jnp.int32)
    rank = jnp.sum(jnp.cumsum(hits, axis=0) * hits, axis=1) - 1
    slot = blocks * capacity + rank
    packed = (
        jnp.zeros((block_total * capacity, 2 * block_width), jnp.bfloat16).at[slot].set(loadings)
    )
    packed = packed.reshape(block_total, capacity, 2 * block_width)
    flat = lax.all_to_all(packed, ("row", "col"), split_axis=0, concat_axis=0, tiled=True).astype(
        jnp.float32
    )
    front = flat[..., :block_width]
    back = flat[..., block_width:]
    value = jnp.sum(jnp.einsum("skb,bc->skc", front, own_tile, precision=HIGH) * front, axis=-1)
    value = value + 2.0 * jnp.sum(
        jnp.einsum("skb,bc->skc", front, cross_tile, precision=HIGH) * back, axis=-1
    )
    value = value + jnp.sum(
        jnp.einsum("skb,bc->skc", back, inner_tile, precision=HIGH) * back, axis=-1
    )
    returned = lax.all_to_all(value, ("row", "col"), split_axis=0, concat_axis=0, tiled=True)
    variance = returned.reshape(-1)[slot]
    mean = exposure * jnp.exp(0.5 * variance)
    seen = counts.astype(jnp.float32)
    total = shape_par + mean
    shape_grad = (
        lax.digamma(shape_par + seen)
        - lax.digamma(shape_par)
        + jnp.log(shape_par / total)
        + (mean - seen) / total
    )
    return (cov_two, top_cov, cov_one, diag_two, diag_one, shape_grad)


def solution(mesh):
    in_specs = (
        P("row", "col"),
        P("row", None),
        P(),
        P(),
        P("row", None),
        P(),
        P(),
        P(),
        P(("row", "col"), None),
        P(("row", "col"), None),
        P(),
        P(("row", "col")),
        P(("row", "col")),
        P(("row", "col")),
    )
    out_specs = (P(("row", "col"), None), P(), P(("row", "col"), None), P(), P(), P(("row", "col")))
    return jax.shard_map(local, mesh=mesh, in_specs=in_specs, out_specs=out_specs, check_vma=False)
```

profile of v0, /device:TPU:1, one launch (start us, length us, event | category | flops | bytes accessed | tf_op | source)
XLA Modules:
  0.0 512.3 jit_solution(3474837565501168186)
XLA Ops:
  9.0 8.7 %fusion = f32[2048,512]{1,0:T(8,128)S(1)} fusion(f32[512,512]{1,0:T(8,128)S(1)} %copy-done, f32[2048,512]{1,0:T(8,128)} %param.18, f32[2048]{0:T(1024)S(1)} %broadcast_bitcast_fusion), kind=kOutput, calls=%fused_computation.6 | convolution fusion | flops 6443499520 | bytes 9445376 | tf_op jit(solution)/shard_map/dot_general | solution.py:15
  17.7 7.0 %fusion.2 = f32[2048,512]{1,0:T(8,128)S(1)} fusion(f32[512,512]{1,0:T(8,128)S(1)} %copy-done.8, f32[2048,512]{1,0:T(8,128)S(1)} %copy-done.13, f32[2048]{0:T(1024)S(1)} %broadcast_bitcast_fusion.1), kind=kOutput, calls=%fused_computation.8 | convolution fusion | flops 6443499520 | bytes 9445376 | tf_op jit(solution)/shard_map/dot_general | solution.py:15
  28.1 74.7 %all-reduce.12.cloned.1.call-done = (f32[1024,512]{1,0:T(8,128)}, f32[1024,512]{1,0:T(8,128)}) async-done(((f32[1024,512]{1,0:T(8,128)}, f32[1024,512]{1,0:T(8,128)}), (f32[1024,512]{1,0:T(8,128)}, f32[1024,512]{1,0:T(8,128)})) %all-reduce.12.cloned.1.call-update) | async-done | bytes 4194320 | tf_op jit(solution)/shard_map/psum | solution.py:11
  102.8 31.3 %convolution_bitcast_fusion.1 = f32[2048,512]{0,1:T(8,128)} fusion(f32[1024,512]{1,0:T(8,128)} %get-tuple-element.35, f32[2048,1024]{1,0:T(8,128)} %param.14), kind=kOutput, calls=%fused_computation.11 | convolution fusion | flops 12884901888 | bytes 14680064 | tf_op jit(solution)/shard_map/dot_general | solution.py:15
  134.1 17.0 %convolution_bitcast_fusion = f32[2048,512]{1,0:T(8,128)} fusion(f32[1024,512]{1,0:T(8,128)S(1)} %copy-done.16, f32[2048,1024]{1,0:T(8,128)} %param.14), kind=kOutput, calls=%fused_computation.10 | convolution fusion | flops 12884901888 | bytes 14680064 | tf_op jit(solution)/shard_map/dot_general | solution.py:15
  153.4 11.2 %scatter_custom_fusion = bf16[4096,256]{1,0:T(8,128)(2,1)} fusion(s32[2048]{0:T(1024)S(1)} %bitcast.76, bf16[2048,256]{1,0:T(8,128)(2,1)} %param.22, bf16[]{:T(256)} %constant.134.clone.1), kind=kCustom, calls=%fused_computation.33 | custom fusion | bytes 2097664 | tf_op jit(solution)/shard_map/scatter | solution.py:104
  164.7 10.4 %all-to-all-start = ((bf16[128,32,256]{2,1,0:T(8,128)(2,1)}), bf16[128,32,256]{2,1,0:T(8,128)(2,1)}, u32[]{:S(2)}, u32[]{:S(2)}) async-start(bf16[128,32,256]{2,1,0:T(8,128)(2,1)} %bitcast.12), calls=%async_computation | async-start | bytes 4194304 | tf_op jit(solution)/shard_map/all_to_all | solution.py:107
  186.3 3.1 fusion.15
  189.4 127.1 %all-reduce.8.cloned.1.call-done = (f32[2048,512]{0,1:T(8,128)}, f32[2048,512]{1,0:T(8,128)}) async-done(((f32[2048,512]{0,1:T(8,128)}, f32[2048,512]{1,0:T(8,128)}), (f32[2048,512]{0,1:T(8,128)}, f32[2048,512]{1,0:T(8,128)})) %all-reduce.8.cloned.1.call-update) | async-done | bytes 8388624 | tf_op jit(solution)/shard_map/psum | solution.py:71
  320.0 7.8 %fusion.38 = f32[512,512]{1,0:T(8,128)} fusion(f32[2048,512]{0,1:T(8,128)S(1)} %broadcast_multiply_fusion, f32[2048,512]{1,0:T(8,128)S(1)} %copy-done.3), kind=kOutput, calls=%fused_computation.83 | convolution fusion | flops 6442450944 | bytes 9437184 | tf_op jit(solution)/shard_map/dot_general | solution.py:19
  327.8 14.3 %fusion.37 = f32[512,512]{1,0:T(8,128)} fusion(f32[2048,512]{1,0:T(8,128)S(1)} %copy-done.5, f32[2048,512]{0,1:T(8,128)S(1)} %broadcast_multiply_fusion), kind=kOutput, calls=%fused_computation.82 | convolution fusion | flops 6442450944 | bytes 9437184 | tf_op jit(solution)/shard_map/dot_general | solution.py:19
  342.1 7.8 %add_multiply_fusion = f32[2048,512]{1,0:T(8,128)S(1)} fusion(f32[2048,512]{1,0:T(8,128)S(1)} %copy-done.9, f32[2048,512]{0,1:T(8,128)S(1)} %broadcast_multiply_fusion, f32[512,512]{1,0:T(8,128)S(1)} %fusion.15, f32[2048]{0:T(1024)S(1)} %bitcast_negate_fusion), kind=kOutput, calls=%fused_computation.5 | convolution fusion | flops 6444548096 | bytes 13639680 | tf_op jit(solution)/shard_map/dot_general | solution.py:15
  351.9 7.7 %fusion.40 = f32[512,512]{1,0:T(8,128)} fusion(f32[2048,512]{1,0:T(8,128)S(1)} %copy-done.3, f32[2048,512]{1,0:T(8,128)S(1)} %add_multiply_fusion), kind=kOutput, calls=%fused_computation.85 | convolution fusion | flops 6442450944 | bytes 9437184 | tf_op jit(solution)/shard_map/dot_general | solution.py:19
  361.0 3.0 fusion.39
  364.1 4.5 copy.57
  368.6 4.0 convert_element_type.25
  372.6 2.9 fusion.36
  375.6 15.1 %reduce-scatter.4.cloned.1.call-done = f32[1,128,128]{1,2,0:T(8,128)} async-done(((f32[16,128,128]{1,2,0:T(8,128)}), f32[1,128,128]{1,2,0:T(8,128)}) %reduce-scatter.4.cloned.1.call-update) | async-done | bytes 65552
  394.4 2.9 multiply_reduce_fusion.1
  397.3 65.2 %all-reduce.10.cloned.1.call-done = (f32[512,512]{1,0:T(8,128)}, f32[512,512]{1,0:T(8,128)}, f32[512,512]{1,0:T(8,128)}) async-done(((f32[512,512]{1,0:T(8,128)}, f32[512,512]{1,0:T(8,128)}, f32[512,512]{1,0:T(8,128)}), (f32[512,512]{1,0:T(8,128)}, f32[512,512]{1,0:T(8,128)}, f32[512,512]{1,0:T(8,128)})) %all-reduce.10.cloned.1.call-update) | async-done | bytes 3145744 | tf_op jit(solution)/shard_map/psum | solution.py:74
  462.5 3.9 convolution_subtract_fusion.1
  472.3 9.7 %all-to-all-start.1 = ((f32[128,1,32]{2,1,0:T(1,128)}), f32[128,1,32]{2,1,0:T(1,128)S(1)}, u32[]{:S(2)}, u32[]{:S(2)}) async-start(f32[128,1,32]{2,1,0:T(1,128)} %copy.64), calls=%async_computation.1 | async-start | bytes 131072 | tf_op jit(solution)/shard_map/all_to_all | solution.py:119
  484.5 7.1 %all-to-all-done.1 = f32[128,1,32]{2,1,0:T(1,128)S(1)} async-done(((f32[128,1,32]{2,1,0:T(1,128)}), f32[128,1,32]{2,1,0:T(1,128)S(1)}, u32[]{:S(2)}, u32[]{:S(2)}) %all-to-all-start.1) | async-done | bytes 16416 | tf_op jit(solution)/shard_map/all_to_all | solution.py:119
  493.0 11.8 %gather_fusion.1 = f32[2048]{0:T(1024)S(1)} fusion(f32[4096]{0:T(1024)S(1)} %reshape.103, s32[2048]{0:T(1024)S(1)} %broadcast_clamp_fusion), kind=kCustom, calls=%fused_computation.1 | custom fusion | bytes 24576 | tf_op jit(solution)/shard_map/gather | solution.py:120
  (106 shorter events, 38.7 us)
Async XLA Ops:
  7.2 95.6 %all-reduce.12.cloned.1.call-start = ((), (), s32[]{:S(2)}) async-start(), calls=%async_computation.6 | async-start | bytes 8388608 | tf_op jit(solution)/shard_map/psum | solution.py:11
  9.0 8.8 %copy-start.8 = (f32[512,512]{1,0:T(8,128)S(1)}, f32[512,512]{1,0:T(8,128)}, u32[]{:S(2)}) copy-start(f32[512,512]{1,0:T(8,128)} %param.16) | copy-start | bytes 3145732
  9.0 8.8 %copy-start.13 = (f32[2048,512]{1,0:T(8,128)S(1)}, f32[2048,512]{1,0:T(8,128)}, u32[]{:S(2)}) copy-start(f32[2048,512]{1,0:T(8,128)} %param.15) | copy-start | bytes 12582916
  17.7 7.0 %copy-start.2 = (f32[2048,512]{1,0:T(8,128)}, f32[2048,512]{1,0:T(8,128)S(1)}, u32[]{:S(2)}) copy-start(f32[2048,512]{1,0:T(8,128)S(1)} %fusion) | copy-start | bytes 12582916
  28.0 288.5 %all-reduce.8.cloned.1.call-start = ((), (), s32[]{:S(2)}) async-start(), calls=%async_computation.4 | async-start | bytes 16777216 | tf_op jit(solution)/shard_map/psum | solution.py:71
  102.8 31.3 %copy-start.16 = (f32[1024,512]{1,0:T(8,128)S(1)}, f32[1024,512]{1,0:T(8,128)}, u32[]{:S(2)}) copy-start(f32[1024,512]{1,0:T(8,128)} %get-tuple-element.36) | copy-start | bytes 6291460
  164.7 199.4 %all-to-all-start = ((bf16[128,32,256]{2,1,0:T(8,128)(2,1)}), bf16[128,32,256]{2,1,0:T(8,128)(2,1)}, u32[]{:S(2)}, u32[]{:S(2)}) async-start(bf16[128,32,256]{2,1,0:T(8,128)(2,1)} %bitcast.12), calls=%async_computation | async-start | bytes 4194304 | tf_op jit(solution)/shard_map/all_to_all | solution.py:107
  175.0 215.7 %reduce-scatter.4.cloned.1.call-start = ((), (), s32[]{:S(2)}) async-start(), calls=%async_computation.3 | async-start | bytes 1114112
  185.6 276.9 %all-reduce.10.cloned.1.call-start = ((), (), s32[]{:S(2)}) async-start(), calls=%async_computation.5 | async-start | bytes 6291456 | tf_op jit(solution)/shard_map/psum | solution.py:74
  316.5 3.4 copy-start.3
  320.0 22.1 %copy-start.1 = (f32[2048,512]{0,1:T(8,128)}, f32[2048,512]{0,1:T(8,128)S(1)}, u32[]{:S(2)}) copy-start(f32[2048,512]{0,1:T(8,128)S(1)} %broadcast_multiply_fusion) | copy-start | bytes 12582916
  320.0 7.8 %copy-start.5 = (f32[2048,512]{1,0:T(8,128)S(1)}, f32[2048,512]{1,0:T(8,128)}, u32[]{:S(2)}) copy-start(f32[2048,512]{1,0:T(8,128)} %copy-done.4) | copy-start | bytes 12582916
  327.8 14.3 %copy-start.9 = (f32[2048,512]{1,0:T(8,128)S(1)}, f32[2048,512]{1,0:T(8,128)}, u32[]{:S(2)}) copy-start(f32[2048,512]{1,0:T(8,128)} %get-tuple-element.31) | copy-start | bytes 12582916
  351.9 7.8 %copy-start.25 = (s32[128]{0:T(128)S(1)}, s32[128]{0:T(128)}, u32[]{:S(2)}) copy-start(s32[128]{0:T(128)} %param.24) | copy-start | bytes 1540
  462.5 3.9 copy-start.19
  462.5 5.8 %copy-start.10 = (f32[512,512]{1,0:T(8,128)S(1)}, f32[512,512]{1,0:T(8,128)}, u32[]{:S(2)}) copy-start(f32[512,512]{1,0:T(8,128)} %fusion.39) | copy-start | bytes 3145732
  462.5 5.9 %copy-start.18 = (f32[512,512]{1,0:T(8,128)S(1)}, f32[512,512]{1,0:T(8,128)}, u32[]{:S(2)}) copy-start(f32[512,512]{1,0:T(8,128)} %get-tuple-element.34) | copy-start | bytes 3145732
  466.4 3.8 copy-start.15
  466.4 3.8 copy-start.6
  466.4 3.8 copy-start.14
  472.3 19.3 %all-to-all-start.1 = ((f32[128,1,32]{2,1,0:T(1,128)}), f32[128,1,32]{2,1,0:T(1,128)S(1)}, u32[]{:S(2)}, u32[]{:S(2)}) async-start(f32[128,1,32]{2,1,0:T(1,128)} %copy.64), calls=%async_computation.1 | async-start | bytes 131072 | tf_op jit(solution)/shard_map/all_to_all | solution.py:119
  493.0 11.8 %copy-start.21 = (f32[2048]{0:T(1024)S(1)}, f32[2048]{0:T(1024)}, u32[]{:S(2)}) copy-start(f32[2048]{0:T(1024)} %param.26) | copy-start | bytes 24580
  493.0 11.8 %copy-start.22 = (f32[2048]{0:T(1024)S(1)}, f32[2048]{0:T(1024)}, u32[]{:S(2)}) copy-start(f32[2048]{0:T(1024)} %param.27) | copy-start | bytes 24580
  493.0 11.8 %copy-start.23 = (s32[2048]{0:T(1024)S(1)}, s32[2048]{0:T(1024)}, u32[]{:S(2)}) copy-start(s32[2048]{0:T(1024)} %param.25) | copy-start | bytes 24580
  (8 other events, 15.3 us)
Sparse Core Ops, SparseCore 0:
  28.1 74.5 all-reduce.11
  151.3 165.2 all-reduce.7
  320.1 70.5 reduce-scatter.3
  393.7 68.7 all-reduce.9
where the time goes:
time: 520 us; the launch traced here: 512 us
  waiting for transfers between devices  289 us (56%)
  matrix products  122 us (23%)
  local copies, waits for them, and re-layouts  50.7 us (10%)
  starting transfers between devices  20.7 us (4%)
  between operations  15.2 us (3%)
  other arithmetic  14.1 us (3%)
    psum x1, waiting for transfers between devices, local(): image_two = lax.psum(matmul(trail_cov, cols_two), 'col')  127 us
    dot_general x7, matrix products, matmul(): jnp.dot(left, right, precision=HIGH, preferred_element_type=jnp.float32)  76.9 us
    psum x1, waiting for transfers between devices, spread(): return lax.psum(block, axis)  74.7 us
    psum x1, waiting for transfers between devices, local(): cross = lax.psum(tmatmul(rows_two, norm_one), 'row')  65.2 us
    dot_general x6, matrix products, tmatmul(): lax.dot_general(left, right, (((0,), (0,)), ((), ())), precision=HIGH, pr...  38.6 us
    unnamed x5, waiting for transfers between devices  15.2 us
    gather x1, local copies, waits for them, and re-layouts, local(): variance = returned.reshape(-1)[slot]  11.8 us
    scatter x1, local copies, waits for them, and re-layouts, local(): jnp.zeros((block_total * capacity, 2 * block_width), jnp.bfloat16).at[slot]  11.2 us
  transfers between devices with their start and end apart: 6, of which 5 were waited for; matrix products, arithmetic and copies ran while one was open for 18% of the time, Pallas kernels for 0%

commit v1 on v0

v1 whole, which is shorter than its diff:
```python
import functools
import jax
import jax.numpy as jnp
from jax import lax
from jax.experimental import pallas as pl
from jax.experimental.pallas import tpu as pltpu
from jax.sharding import PartitionSpec as P

BOTH = ("row", "col")

LEVELS = 32700.0
STEPS = 64.0
TINY = 1e-33
ROOM = 56 * 1024 * 1024


def split(value):
    head = value.astype(jnp.bfloat16)
    return head, (value - head.astype(jnp.float32)).astype(jnp.bfloat16)


def dot(left, right):
    return jnp.dot(left, right, preferred_element_type=jnp.float32)


def tdot(left, right):
    return lax.dot_general(
        left, right, (((0,), (0,)), ((), ())), preferred_element_type=jnp.float32
    )


def product(left, right, form=dot):
    left_head, left_tail = split(left)
    right_head, right_tail = split(right)
    return form(left_head, right_head) + (form(left_head, right_tail) + form(left_tail, right_head))


def pack(code):
    half = code.shape[-1] // 2
    return code[..., :half] * 65536 + code[..., half:]


def unpack(word):
    low = lax.shift_right_arithmetic(lax.shift_left(word, 16), 16)
    high = lax.shift_right_arithmetic(word - low, 16)
    return jnp.concatenate([high, low], axis=-1).astype(jnp.float32)


def encode(value, out_ref, *at):
    rows = value.shape[0]
    largest = jnp.max(jnp.abs(value), axis=0, keepdims=True)
    step = jnp.ceil(jnp.log2(jnp.maximum(largest, TINY)) * STEPS)
    code = jnp.round(value * (jnp.exp2(step * (-1.0 / STEPS)) * LEVELS))
    code = jnp.clip(code, -32767.0, 32767.0).astype(jnp.int32)
    out_ref[(*at, pl.ds(0, rows), slice(None))] = pack(code)
    head = pack(step.astype(jnp.int32))
    out_ref[(*at, pl.ds(rows, 8), slice(None))] = jnp.broadcast_to(head, (8, head.shape[1]))


def decode(word):
    rows = word.shape[0] - 8
    scale = jnp.exp2(unpack(word[rows : rows + 1]) * (1.0 / STEPS)) * (1.0 / LEVELS)
    return unpack(word[:rows]) * scale


def share_kernel(at_ref, two_ref, one_ref, inv_two_ref, inv_one_ref, out_ref):
    for i, (rows, inv) in enumerate(((two_ref, inv_two_ref), (one_ref, inv_one_ref))):
        keep = at_ref[1 + i].astype(jnp.float32)
        encode(product(keep * rows[...], inv[...]), out_ref, i)


def share(at, panel_two, panel_one, inv_two, inv_one, bw):
    width = inv_two.shape[0]
    rows = pl.BlockSpec((bw, width), lambda i, at: (at[0], 0))
    whole = pl.BlockSpec((width, width), lambda i, at: (0, 0))
    return pl.pallas_call(
        share_kernel,
        out_shape=jax.ShapeDtypeStruct((2, bw + 8, width // 2), jnp.int32),
        grid_spec=pltpu.PrefetchScalarGridSpec(
            num_scalar_prefetch=1,
            grid=(1,),
            in_specs=[rows, rows, whole, whole],
            out_specs=pl.BlockSpec((2, bw + 8, width // 2), lambda i, at: (0, 0, 0)),
        ),
        compiler_params=pltpu.CompilerParams(vmem_limit_bytes=ROOM),
    )(at, panel_two, panel_one, inv_two, inv_one)


def image_kernel(panel, bw, pieces, at_ref, cov_ref, *refs):
    held, (image_ref, code_ref, head_ref, tail_ref) = refs[:pieces], refs[pieces:]

    @pl.when(pl.program_id(0) == 0)
    def _():
        for i, ref in enumerate(held):
            head, tail = split(decode(ref[panel]))
            rows = pl.ds(pl.multiple_of(at_ref[i] * bw, bw), bw)
            head_ref[rows, :] = head
            tail_ref[rows, :] = tail

    cov_head, cov_tail = split(cov_ref[...])
    image = dot(cov_head, head_ref[...]) + (
        dot(cov_head, tail_ref[...]) + dot(cov_tail, head_ref[...])
    )
    image_ref[...] = image
    for i in range(image.shape[0] // bw):
        encode(image[i * bw : (i + 1) * bw], code_ref, i)


def image(at, trail_cov, held, panel, bw, tile=256):
    rows, span = trail_cov.shape
    width = 2 * held[0].shape[-1]
    every = pl.BlockSpec(held[0].shape, lambda i, at: (0, 0, 0))
    return pl.pallas_call(
        functools.partial(image_kernel, panel, bw, len(held)),
        out_shape=[
            jax.ShapeDtypeStruct((rows, width), jnp.float32),
            jax.ShapeDtypeStruct((rows // bw, bw + 8, width // 2), jnp.int32),
        ],
        grid_spec=pltpu.PrefetchScalarGridSpec(
            num_scalar_prefetch=1,
            grid=(rows // tile,),
            in_specs=[pl.BlockSpec((tile, span), lambda i, at: (i, 0))] + [every] * len(held),
            out_specs=[
                pl.BlockSpec((tile, width), lambda i, at: (i, 0)),
                pl.BlockSpec((tile // bw, bw + 8, width // 2), lambda i, at: (i, 0, 0)),
            ],
            scratch_shapes=[pltpu.VMEM((span, width), jnp.bfloat16)] * 2,
        ),
        compiler_params=pltpu.CompilerParams(vmem_limit_bytes=ROOM),
        cost_estimate=pl.CostEstimate(
            flops=6 * rows * span * width, bytes_accessed=4 * rows * (span + width), transcendentals=0
        ),
    )(at, trail_cov, *held)


def sums_kernel(
    bw, bits_two_ref, bits_one_ref, two_ref, one_ref, image_two_ref, image_one_ref,
    inv_two_ref, inv_one_ref, out_ref,
):
    step = pl.program_id(0)

    @pl.when(step == 0)
    def _():
        out_ref[...] = jnp.zeros_like(out_ref)

    count = two_ref.shape[0] // bw

    def masked(ref, bits_ref):
        keep = [
            jnp.full((bw, 1), bits_ref[step * count + i].astype(jnp.float32)) for i in range(count)
        ]
        keep = jnp.concatenate(keep, axis=0)
        return ref[...] * keep, keep

    two, keep_two = masked(two_ref, bits_two_ref)
    one, _ = masked(one_ref, bits_one_ref)
    image_two = split(image_two_ref[...] * keep_two)
    image_one = split(image_one_ref[...])
    two, one = split(two), split(one)
    for i, (left, right) in enumerate(((two, image_two), (one, image_two), (one, image_one))):
        out_ref[i] += tdot(left[0], right[0]) + (tdot(left[0], right[1]) + tdot(left[1], right[0]))

    @pl.when(step == pl.num_programs(0) - 1)
    def _():
        for i, inv in enumerate((inv_two_ref, inv_one_ref, inv_one_ref)):
            out_ref[i] = product(inv[...], out_ref[i], tdot)


def sums(bits_two, bits_one, panel_two, panel_one, image_two, image_one, inv_two, inv_one, bw, tile=256):
    rows, width = panel_two.shape
    part = pl.BlockSpec((tile, width), lambda i, *_: (i, 0))
    whole = pl.BlockSpec((width, width), lambda i, *_: (0, 0))
    return pl.pallas_call(
        functools.partial(sums_kernel, bw),
        out_shape=jax.ShapeDtypeStruct((3, width, width), jnp.float32),
        grid_spec=pltpu.PrefetchScalarGridSpec(
            num_scalar_prefetch=2,
            grid=(rows // tile,),
            in_specs=[part] * 4 + [whole] * 2,
            out_specs=pl.BlockSpec((3, width, width), lambda i, *_: (0, 0, 0)),
        ),
        compiler_params=pltpu.CompilerParams(vmem_limit_bytes=ROOM),
        cost_estimate=pl.CostEstimate(
            flops=18 * rows * width * width, bytes_accessed=16 * rows * width, transcendentals=0
        ),
    )(bits_two, bits_one, panel_two, panel_one, image_two, image_one, inv_two, inv_one)


def rows_kernel(at_ref, two_ref, one_ref, top_ref, cov_two_ref, cov_one_ref, cross_ref):
    count = two_ref.shape[0]

    def total(ref):
        value = decode(ref[0])
        for i in range(1, count):
            value = value + decode(ref[i])
        return value

    cov_two = -at_ref[0].astype(jnp.float32) * total(two_ref)
    cov_two_ref[...] = cov_two
    cov_one = -at_ref[1].astype(jnp.float32) * (product(cov_two, top_ref[...]) + total(one_ref))
    cov_one_ref[...] = cov_one
    bw = cross_ref.shape[1]
    cross_ref[...] = cov_one_ref[:, pl.ds(pl.multiple_of(at_ref[2] * bw, bw), bw)]


def rows(at, part_two, part_one, norm_top, bw):
    width = norm_top.shape[0]
    smem = pl.BlockSpec(memory_space=pltpu.SMEM)
    vmem = pl.BlockSpec(memory_space=pltpu.VMEM)
    return pl.pallas_call(
        rows_kernel,
        out_shape=[jax.ShapeDtypeStruct((bw, n), jnp.float32) for n in (width, width, bw)],
        in_specs=[smem, vmem, vmem, vmem],
        out_specs=[vmem] * 3,
        compiler_params=pltpu.CompilerParams(vmem_limit_bytes=ROOM),
    )(at, part_two, part_one, norm_top)


def small_kernel(at_ref, own_ref, other_ref, gram_ref, top_ref, keep_ref, two_ref, top_cov_ref, one_ref, sums_ref):
    y_count, lanes = own_ref.shape[2], own_ref.shape[-1]
    tall = own_ref.shape[-2]

    for flip, ref in enumerate((own_ref, other_ref)):
        half = lax.rem(at_ref[3] + flip, 2)
        for dz in range(4):
            z = lax.rem(at_ref[2] + 4 - dz, 4)
            for dx in range(4):
                x = lax.rem(at_ref[0] + 4 - dx, 4)
                row = ((half * 4 + z) * 4 + x) * tall
                for dy in range(y_count):
                    y = lax.rem(at_ref[1] + 4 - dy, 4)
                    sums_ref[
                        :,
                        pl.ds(pl.multiple_of(row, tall), tall),
                        pl.ds(pl.multiple_of(y * lanes, lanes), lanes),
                    ] = ref[dz, dx, dy]
    top = top_ref[...]
    two = gram_ref[0] + sums_ref[0]
    two_ref[...] = two
    mixed = sums_ref[1]
    keep = jnp.concatenate(
        [
            jnp.full((top.shape[0] // 4, 1), keep_ref[i].astype(jnp.float32)) for i in range(4)
        ],
        axis=0,
    )
    top_cov = -keep * (product(two, top) - mixed.T)
    top_cov_ref[...] = top_cov
    one_ref[...] = gram_ref[1] + sums_ref[2] - product(top, top_cov, tdot) - product(mixed, top)


def small(at, own, other, gram, norm_top, bits_top):
    width = norm_top.shape[0]
    smem = pl.BlockSpec(memory_space=pltpu.SMEM)
    vmem = pl.BlockSpec(memory_space=pltpu.VMEM)
    return pl.pallas_call(
        small_kernel,
        out_shape=[jax.ShapeDtypeStruct((width, width), jnp.float32)] * 3,
        in_specs=[smem, vmem, vmem, vmem, vmem, smem],
        out_specs=[vmem] * 3,
        scratch_shapes=[pltpu.VMEM((3, width, width), jnp.float32)],
        compiler_params=pltpu.CompilerParams(vmem_limit_bytes=ROOM),
    )(at, own, other, gram, norm_top, bits_top)


def early_kernel(keep_ref, top_rows_ref, inv_two_ref, inv_one_ref, gram_ref, top_ref):
    keep = jnp.concatenate(
        [
            jnp.full((top_rows_ref.shape[0] // 4, 1), keep_ref[i].astype(jnp.float32))
            for i in range(4)
        ],
        axis=0,
    )
    top_ref[...] = product(keep * top_rows_ref[...], inv_one_ref[...])
    gram_ref[0] = product(inv_two_ref[...], inv_two_ref[...], tdot)
    gram_ref[1] = product(inv_one_ref[...], inv_one_ref[...], tdot)


def early(bits_top, panel_top, inv_two, inv_one):
    width = inv_two.shape[0]
    smem = pl.BlockSpec(memory_space=pltpu.SMEM)
    vmem = pl.BlockSpec(memory_space=pltpu.VMEM)
    return pl.pallas_call(
        early_kernel,
        out_shape=[
            jax.ShapeDtypeStruct((2, width, width), jnp.float32),
            jax.ShapeDtypeStruct((width, width), jnp.float32),
        ],
        in_specs=[smem, vmem, vmem, vmem],
        out_specs=[vmem] * 2,
        compiler_params=pltpu.CompilerParams(vmem_limit_bytes=ROOM),
    )(bits_top, panel_top, inv_two, inv_one)


def row_sums(value):
    ones = jnp.ones((8, value.shape[1]), jnp.bfloat16)
    head, tail = split(value)
    form = (((1,), (1,)), ((), ()))
    return lax.dot_general(
        ones, head, form, preferred_element_type=jnp.float32
    ) + lax.dot_general(ones, tail, form, preferred_element_type=jnp.float32)


def forms_kernel(units_ref, tile_ref, cross_ref, out_ref):
    bw = tile_ref.shape[0]
    front, back = units_ref[:, :bw], units_ref[:, bw:]
    middle = jnp.concatenate([*split(tile_ref[...]), *split(2.0 * cross_ref[...])], axis=1)
    both = dot(front, middle)
    value = (both[:, :bw] + both[:, bw : 2 * bw]) * front.astype(jnp.float32)
    value = value + (both[:, 2 * bw : 3 * bw] + both[:, 3 * bw :]) * back.astype(jnp.float32)
    out_ref[...] = row_sums(value)


def forms(units, tile, cross, step=1024):
    count, bw = units.shape[0], tile.shape[0]
    whole = pl.BlockSpec((bw, bw), lambda i: (0, 0))
    return pl.pallas_call(
        forms_kernel,
        out_shape=jax.ShapeDtypeStruct((8, count), jnp.float32),
        grid=(count // step,),
        in_specs=[pl.BlockSpec((step, 2 * bw), lambda i: (i, 0)), whole, whole],
        out_specs=pl.BlockSpec((8, step), lambda i: (0, i)),
        compiler_params=pltpu.CompilerParams(vmem_limit_bytes=ROOM),
    )(units, tile, cross)


def inner_kernel(units_ref, panel_ref, diag_ref, out_ref):
    bw = units_ref.shape[1] // 2
    back = units_ref[:, bw:]
    count = diag_ref.shape[0] // bw
    value = jnp.zeros(back.shape, jnp.float32)
    for p in range(count):
        at = slice(p * bw, (p + 1) * bw)
        both = dot(back, jnp.concatenate(split(diag_ref[at, at]), axis=1))
        value = jnp.where(panel_ref[...] == p, both[:, :bw] + both[:, bw:], value)
    out_ref[...] = row_sums(value * back.astype(jnp.float32))


def inner(units, panel, diag, step=1024):
    count, width = units.shape
    return pl.pallas_call(
        inner_kernel,
        out_shape=jax.ShapeDtypeStruct((8, count), jnp.float32),
        grid=(count // step,),
        in_specs=[
            pl.BlockSpec((step, width), lambda i: (i, 0)),
            pl.BlockSpec((step, 1), lambda i: (i, 0)),
            pl.BlockSpec(diag.shape, lambda i: (0, 0)),
        ],
        out_specs=pl.BlockSpec((8, step), lambda i: (0, i)),
        compiler_params=pltpu.CompilerParams(vmem_limit_bytes=ROOM),
    )(units, panel, diag)


class Ring:
    def __init__(self, axis, size, stride, count=4):
        self.axis, self.size, self.stride, self.count = axis, size, stride, count

    def place(self):
        return lax.axis_index(self.axis) // self.stride % self.count

    def move(self, value, step):
        pairs = []
        for i in range(self.size):
            at = i // self.stride % self.count
            pairs.append((i, i + ((at + step) % self.count - at) * self.stride))
        return lax.ppermute(value, self.axis, pairs)

    def scatter_sum(self, value, axis):
        size = value.shape[axis] // self.count

        def take(step):
            at = (self.place() + step) % self.count * size
            return lax.dynamic_slice_in_dim(value, at, size, axis)

        parts = [self.move(take(step), step) for step in range(1, self.count)]
        total = take(0)
        for part in parts:
            total = total + part
        return total

    def gather(self, value):
        return jnp.stack([value] + [self.move(value, step) for step in range(1, self.count)])


def local(
    trail_cov,
    panel_two_rows,
    diag_inv_two,
    panel_one_top,
    panel_one_rows,
    diag_inv_one,
    pattern_two,
    pattern_one,
    loadings,
    unit_block,
    block_panel,
    counts,
    shape_par,
    exposure,
):
    row_count = lax.axis_size("row")
    col_count = lax.axis_size("col")
    total_count = row_count * col_count
    row_index = lax.axis_index("row")
    col_index = lax.axis_index("col")
    ratio = col_count // row_count
    width = diag_inv_two.shape[0]
    bw = loadings.shape[1] // 2
    top_blocks = width // bw
    owner = row_index * col_count + col_index
    core = Ring("row", row_count, 1, 2)
    ring_z = Ring("row", row_count, 2)
    ring_x = Ring("col", col_count, 1)
    ring_y = Ring("col", col_count, 4)

    bits_two = lax.dynamic_slice_in_dim(pattern_two, row_index * col_count, col_count)
    bits_top = pattern_one[:top_blocks]
    bits_one = lax.dynamic_slice_in_dim(
        pattern_one, top_blocks + row_index * col_count, col_count
    )
    own_two = lax.dynamic_index_in_dim(bits_two, col_index, 0, False)
    own_one = lax.dynamic_index_in_dim(bits_one, col_index, 0, False)

    part = share(
        jnp.stack([col_index, own_two, own_one]),
        panel_two_rows, panel_one_rows, diag_inv_two, diag_inv_one, bw,
    )
    moves = [(i, i % row_count * col_count + i // row_count) for i in range(total_count)]
    part = lax.ppermute(part, BOTH, moves)
    after, before = ring_z.move(part, 1), ring_z.move(part, -1)
    far = jnp.stack([ring_z.move(after[0], 1), ring_z.move(before[1], -1)])
    held, places = [], []
    for step, piece in ((0, part), (1, after), (-1, before), (2, far)):
        at = (ring_z.place() - step) % 4 * 2
        held += [piece, core.move(piece, 1)]
        places += [at + core.place(), at + 1 - core.place()]
    places = jnp.stack(places)

    blocks = unit_block[:, 0]
    capacity = 2 * loadings.shape[0] // total_count
    hits = (blocks[:, None] == jnp.arange(total_count, dtype=jnp.int32)[None, :]).astype(jnp.int32)
    rank = jnp.sum(jnp.cumsum(hits, axis=0) * hits, axis=1) - 1
    slot = blocks * capacity + rank
    packed = jnp.zeros((total_count * capacity, 2 * bw), jnp.bfloat16).at[slot].set(loadings)
    packed = packed.reshape(total_count, capacity, 2 * bw)
    units = lax.all_to_all(packed, BOTH, split_axis=0, concat_axis=0, tiled=True)
    units = units.reshape(total_count * capacity, 2 * bw)

    side = col_index % ratio
    tiles = jnp.stack(
        [
            lax.dynamic_slice(trail_cov, ((side * row_count + j) * bw, j * bw), (bw, bw))
            for j in range(row_count)
        ]
    )
    tiles = jnp.concatenate([jnp.where(side == h, tiles, 0.0) for h in range(ratio)])
    tiles = lax.all_to_all(tiles, "col", split_axis=0, concat_axis=0, tiled=True)
    tile = lax.dynamic_index_in_dim(
        tiles, row_index * ratio + col_index // row_count, 0, keepdims=False
    )

    gram, norm_top = early(bits_top, panel_one_top, diag_inv_two, diag_inv_one)

    image_two, code_two = image(places, trail_cov, held, 0, bw)
    code_two = lax.all_to_all(code_two, "col", split_axis=0, concat_axis=0, tiled=True)
    image_one, code_one = image(places, trail_cov, held, 1, bw)
    code_one = lax.all_to_all(code_one, "col", split_axis=0, concat_axis=0, tiled=True)

    total = sums(
        bits_two, bits_one, panel_two_rows, panel_one_rows, image_two, image_one,
        diag_inv_two, diag_inv_one, bw,
    )
    total = core.scatter_sum(total, 1)
    total = ring_z.scatter_sum(total, 1)
    total = ring_x.scatter_sum(total, 1)
    total = ring_y.scatter_sum(total, 2)
    total = ring_z.gather(ring_x.gather(ring_y.gather(total)))
    spots = jnp.stack([ring_x.place(), ring_y.place(), ring_z.place(), core.place()])
    diag_two, top_cov, diag_one = small(
        spots, total, core.move(total, 1), gram, norm_top, bits_top
    )

    cov_two, cov_one, cross = rows(
        jnp.stack([own_two, own_one, block_panel[owner]]), code_two, code_one, norm_top, bw
    )
    value = forms(units, tile, cross)[0].reshape(total_count, capacity)
    returned = lax.all_to_all(value, BOTH, split_axis=0, concat_axis=0, tiled=True)
    picked = jnp.dot(
        hits.astype(jnp.float32), returned, precision=lax.Precision.HIGHEST,
        preferred_element_type=jnp.float32,
    )
    at_rank = rank[:, None] == jnp.arange(capacity, dtype=jnp.int32)[None, :]
    variance = jnp.sum(jnp.where(at_rank, picked, 0.0), axis=1)
    own_panel = jnp.sum(hits * block_panel[None, :], axis=1, keepdims=True)
    variance = variance + inner(loadings, own_panel, diag_one)[0]

    mean = exposure * jnp.exp(0.5 * variance)
    seen = counts.astype(jnp.float32)
    scale = shape_par + mean
    shape_grad = (
        lax.digamma(shape_par + seen)
        - lax.digamma(shape_par)
        + jnp.log(shape_par / scale)
        + (mean - seen) / scale
    )
    return (cov_two, top_cov, cov_one, diag_two, diag_one, shape_grad)


def solution(mesh):
    in_specs = (
        P("row", "col"),
        P("row", None),
        P(),
        P(),
        P("row", None),
        P(),
        P(),
        P(),
        P(("row", "col"), None),
        P(("row", "col"), None),
        P(),
        P(("row", "col")),
        P(("row", "col")),
        P(("row", "col")),
    )
    out_specs = (P(("row", "col"), None), P(), P(("row", "col"), None), P(), P(), P(("row", "col")))
    return jax.shard_map(local, mesh=mesh, in_specs=in_specs, out_specs=out_specs, check_vma=False)
```

time: 520 us -> 345 us (0.66); the launches traced: 512 us -> 343 us
  waiting for transfers between devices: 289 us -> 106 us
  matrix products: 122 us -> 1.37 us
  starting transfers between devices: 20.7 us -> 103 us
  Pallas kernels: 0 us -> 78.2 us
  between operations: 15.2 us -> 1.46 us
  local copies, waits for them, and re-layouts: 50.7 us -> 39.7 us
    psum x3 -> x0, waiting for transfers between devices: 267 us -> none  [the longest x1 127 us: local(): image_two = lax.psum(matmul(trail_cov, cols_two), 'col')]
    dot_general x16 -> x1, matrix products: 122 us -> 1.37 us  [local(): jnp.dot(hits.astype(jnp.float32), returned, precision=lax.Precision.HIGHE...]
    pallas_call x0 -> x9, Pallas kernels: none -> 78.2 us  [the longest x2 27.9 us: image(): pl.pallas_call(functools.partial(image_kernel, panel, bw, len(held)), out...]
    ppermute x0 -> x29, waiting for transfers between devices: none -> 72.6 us  [the longest x28 71.3 us: move(): return lax.ppermute(value, self.axis, pairs)]
    ppermute x0 -> x29, starting transfers between devices: none -> 65.9 us  [the longest x28 59.9 us: move(): return lax.ppermute(value, self.axis, pairs)]
    all_to_all x2 -> x5, waiting for transfers between devices: 7.05 us -> 33.1 us  [the longest x1 25.5 us: local(): lax.all_to_all(code_one, 'col', split_axis=0, concat_axis=0, tiled=True)]
    all_to_all x2 -> x5, starting transfers between devices: 20.1 us -> 36.9 us  [the longest x1 10.4 us: local(): lax.all_to_all(packed, BOTH, split_axis=0, concat_axis=0, tiled=True)]
    unnamed x5 -> x0, waiting for transfers between devices: 15.2 us -> none
  transfers between devices with their start and end apart: 6 -> 34, of which waited for: 5 -> 12; matrix products, arithmetic and copies ran while one was open for 18% -> 12% of each run, Pallas kernels for 0% -> 19%
where the time goes in v1:
time: 345 us; the launch traced here: 343 us
  waiting for transfers between devices  106 us (31%)
  starting transfers between devices  103 us (30%)
  Pallas kernels  78.2 us (23%)
  local copies, waits for them, and re-layouts  39.7 us (12%)
  other arithmetic  13.6 us (4%)
    ppermute x28, waiting for transfers between devices, move(): return lax.ppermute(value, self.axis, pairs)  71.3 us
    ppermute x28, starting transfers between devices, move(): return lax.ppermute(value, self.axis, pairs)  59.9 us
    pallas_call x2, Pallas kernels, image(): pl.pallas_call(functools.partial(image_kernel, panel, bw, len(held)), out...  27.9 us
    all_to_all x1, waiting for transfers between devices, local(): lax.all_to_all(code_one, 'col', split_axis=0, concat_axis=0, tiled=True)  25.5 us
    pallas_call x1, Pallas kernels, sums(): pl.pallas_call(functools.partial(sums_kernel, bw), out_shape=jax.ShapeDty...  20.2 us
    unnamed x45, local copies, waits for them, and re-layouts  12.4 us
    scatter x1, local copies, waits for them, and re-layouts, local(): jnp.zeros((total_count * capacity, 2 * bw), jnp.bfloat16).at[slot]  11.3 us
    all_to_all x1, starting transfers between devices, local(): lax.all_to_all(packed, BOTH, split_axis=0, concat_axis=0, tiled=True)  10.4 us
  transfers between devices with their start and end apart: 34, of which 12 were waited for; matrix products, arithmetic and copies ran while one was open for 12% of the time, Pallas kernels for 19%

profile of v1, /device:TPU:1, one launch (start us, length us, event | category | flops | bytes accessed | tf_op | source)
XLA Modules:
  0.0 342.8 jit_solution(10600083385719804075)
XLA Ops:
  8.8 6.0 %collective-permute-start = (s32[2,136,256]{2,1,0:T(8,128)}, s32[2,136,256]{2,1,0:T(8,128)S(1)}, u32[]{:S(2)}, u32[]{:S(2)}) collective-permute-start(s32[2,136,256]{2,1,0:T(8,128)} %shard_map.181), channel_id=1, source_target_pairs={{0,0},{1,16},{2,32},{3,48},{4,64},{5,80},{6,96},{7,112},{8,1},{9,1... | collective-permute-start | bytes 835592 | tf_op jit(solution)/shard_map/ppermute | solution.py:430
  18.7 9.2 %collective-permute-start.2 = (s32[2,136,256]{2,1,0:T(8,128)S(1)}, s32[2,136,256]{2,1,0:T(8,128)S(1)}, u32[]{:S(2)}, u32[]{:S(2)}) collective-permute-start(s32[2,136,256]{2,1,0:T(8,128)S(1)} %collective-permute-done.refs_0_), channel_id=1, source_target_pairs={{0,32},{16,48},{32,64},{48,80},{64,96},{80,112},{96,0},{112,16},{1... | collective-permute-start | bytes 835592 | tf_op jit(solution)/shard_map/ppermute | solution.py:367
  40.9 13.6 %collective-permute-start.1 = (s32[2,136,256]{2,1,0:T(8,128)S(1)}, s32[2,136,256]{2,1,0:T(8,128)S(1)}, u32[]{:S(2)}, u32[]{:S(2)}) collective-permute-start(s32[2,136,256]{2,1,0:T(8,128)S(1)} %collective-permute-done.refs_0_), channel_id=1, source_target_pairs={{0,16},{16,0},{32,48},{48,32},{64,80},{80,64},{96,112},{112,96},{1... | collective-permute-start | bytes 835592 | tf_op jit(solution)/shard_map/ppermute | solution.py:367
  56.7 8.7 %all-to-all-start.3 = ((f32[16,128,128]{2,1,0:T(8,128)}), f32[16,128,128]{2,1,0:T(8,128)S(1)}, u32[]{:S(2)}, u32[]{:S(2)}) async-start(f32[16,128,128]{2,1,0:T(8,128)} %pad_maximum_fusion.1), calls=%async_computation.3 | async-start | bytes 2097152 | tf_op jit(solution)/shard_map/all_to_all | solution.py:458
  69.0 13.9 %shard_map.183 = (f32[2048,512]{1,0:T(8,128)}, s32[16,136,256]{2,1,0:T(8,128)}) custom-call(s32[8]{0:T(128)} %stack.145.at_ref, f32[2048,1024]{1,0:T(8,128)} %cov_ref.3, s32[2,136,256]{2,1,0:T(8,128)} %copy-done.12, s32[2,136,256]{2,1,0:T(8,128)} %copy-done.13, s32[2,136,256]{2,1,0:T(8,128)} %copy-done.6, s32[2,136,256]{2,1,0:T(8,128)} %copy-done.14, ...), custom_call_target="tpu_custom_call" | custom-call | flops 6442450944 | bytes 12582912 | tf_op jit(solution)/shard_map/pallas_call | solution.py:113
  82.9 13.9 %shard_map.182 = (f32[2048,512]{1,0:T(8,128)}, s32[16,136,256]{2,1,0:T(8,128)}) custom-call(s32[8]{0:T(128)} %stack.145.at_ref, f32[2048,1024]{1,0:T(8,128)} %cov_ref.3, s32[2,136,256]{2,1,0:T(8,128)} %copy-done.12, s32[2,136,256]{2,1,0:T(8,128)} %copy-done.13, s32[2,136,256]{2,1,0:T(8,128)} %copy-done.6, s32[2,136,256]{2,1,0:T(8,128)} %copy-done.14, ...), custom_call_target="tpu_custom_call" | custom-call | flops 6442450944 | bytes 12582912 | tf_op jit(solution)/shard_map/pallas_call | solution.py:113
  96.9 20.2 %shard_map.186 = f32[3,512,512]{2,1,0:T(8,128)} custom-call(s32[16]{0:T(128)} %dynamic_slice.95.bits_two_ref, s32[16]{0:T(128)} %dynamic_slice.96.bits_one_ref, f32[2048,512]{1,0:T(8,128)} %two_ref.3, f32[2048,512]{1,0:T(8,128)} %one_ref.3, f32[2048,512]{1,0:T(8,128)} %get-tuple-element.22.image_two_ref, f32[2048,512]{1,0:T(8,128)} %get-tuple-element.23.image_one_ref, ...), custom_call_target="tpu_custom_call" | custom-call | flops 9663676416 | bytes 16777216 | tf_op jit(solution)/shard_map/pallas_call | solution.py:173
  121.1 6.8 %all-to-all-start.1 = ((s32[16,136,256]{2,1,0:T(8,128)}), s32[16,136,256]{2,1,0:T(8,128)S(1)}, u32[]{:S(2)}, u32[]{:S(2)}) async-start(s32[16,136,256]{2,1,0:T(8,128)} %get-tuple-element.19), calls=%async_computation.1 | async-start | bytes 4456448 | tf_op jit(solution)/shard_map/all_to_all | solution.py:468
  137.7 25.5 %all-to-all-done.1.one_ref = s32[16,136,256]{2,1,0:T(8,128)S(1)} async-done(((s32[16,136,256]{2,1,0:T(8,128)}), s32[16,136,256]{2,1,0:T(8,128)S(1)}, u32[]{:S(2)}, u32[]{:S(2)}) %all-to-all-start.1) | async-done | bytes 2228256 | tf_op jit(solution)/shard_map/all_to_all | solution.py:468
  164.6 4.4 %all-to-all-start = ((s32[16,136,256]{2,1,0:T(8,128)}), s32[16,136,256]{2,1,0:T(8,128)}, u32[]{:S(2)}, u32[]{:S(2)}) async-start(s32[16,136,256]{2,1,0:T(8,128)} %get-tuple-element.18), calls=%async_computation | async-start | bytes 4456448 | tf_op jit(solution)/shard_map/all_to_all | solution.py:466
  177.0 22.6 %collective-permute-done.13 = f32[3,16,512]{2,1,0:T(8,128)S(1)} collective-permute-done((f32[3,16,512]{2,1,0:T(8,128)S(1)}, f32[3,16,512]{2,1,0:T(8,128)S(1)}, u32[]{:S(2)}, u32[]{:S(2)}) %collective-permute-start.13) | collective-permute-done | bytes 98336 | tf_op jit(solution)/shard_map/ppermute | solution.py:367
  199.7 4.5 %collective-permute-done.14 = f32[3,16,512]{2,1,0:T(8,128)S(1)} collective-permute-done((f32[3,16,512]{2,1,0:T(8,128)S(1)}, f32[3,16,512]{2,1,0:T(8,128)S(1)}, u32[]{:S(2)}, u32[]{:S(2)}) %collective-permute-start.14) | collective-permute-done | bytes 98336 | tf_op jit(solution)/shard_map/ppermute | solution.py:367
  213.7 11.3 %scatter_custom_fusion = bf16[4096,256]{1,0:T(8,128)(2,1)} fusion(s32[2048]{0:T(1024)S(1)} %bitcast.90, bf16[2048,256]{1,0:T(8,128)(2,1)} %units_ref.1, bf16[]{:T(256)} %constant.374.clone.1), kind=kCustom, calls=%fused_computation.9 | custom fusion | bytes 2097664 | tf_op jit(solution)/shard_map/scatter | solution.py:445
  225.0 10.4 %all-to-all-start.2 = ((bf16[128,32,256]{2,1,0:T(8,128)(2,1)}), bf16[128,32,256]{2,1,0:T(8,128)(2,1)S(1)}, u32[]{:S(2)}, u32[]{:S(2)}) async-start(bf16[128,32,256]{2,1,0:T(8,128)(2,1)} %bitcast.36), calls=%async_computation.2 | async-start | bytes 4194304 | tf_op jit(solution)/shard_map/all_to_all | solution.py:447
  240.5 22.2 %collective-permute-done.22 = f32[4,3,16,128]{3,2,1,0:T(8,128)S(1)} collective-permute-done((f32[4,3,16,128]{3,2,1,0:T(8,128)S(1)}, f32[4,3,16,128]{3,2,1,0:T(8,128)S(1)}, u32[]{:S(2)}, u32[]{:S(2)}) %collective-permute-start.22) | collective-permute-done | bytes 98336 | tf_op jit(solution)/shard_map/ppermute | solution.py:367
  270.4 6.5 %collective-permute-done.25 = f32[4,4,3,16,128]{4,3,2,1,0:T(8,128)S(1)} collective-permute-done((f32[4,4,3,16,128]{4,3,2,1,0:T(8,128)S(1)}, f32[4,4,3,16,128]{4,3,2,1,0:T(8,128)S(1)}, u32[]{:S(2)}, u32[]{:S(2)}) %collective-permute-start.25) | collective-permute-done | bytes 393248 | tf_op jit(solution)/shard_map/ppermute | solution.py:367
  276.9 9.3 %collective-permute-done.26 = f32[4,4,3,16,128]{4,3,2,1,0:T(8,128)S(1)} collective-permute-done((f32[4,4,3,16,128]{4,3,2,1,0:T(8,128)S(1)}, f32[4,4,3,16,128]{4,3,2,1,0:T(8,128)S(1)}, u32[]{:S(2)}, u32[]{:S(2)}) %collective-permute-start.26) | collective-permute-done | bytes 393248 | tf_op jit(solution)/shard_map/ppermute | solution.py:367
  290.4 5.9 %shard_map.184 = (f32[2,512,512]{2,1,0:T(8,128)}, f32[512,512]{1,0:T(8,128)}) custom-call(s32[4]{0:T(128)} %slice.23.keep_ref, f32[512,512]{1,0:T(8,128)} %top_rows_ref.1, f32[512,512]{1,0:T(8,128)} %inv_two_ref.5, f32[512,512]{1,0:T(8,128)} %inv_one_ref.5), custom_call_target="tpu_custom_call" | custom-call | tf_op jit(solution)/shard_map/pallas_call | solution.py:283
  300.3 5.0 %shard_map.185 = (f32[128,512]{1,0:T(8,128)}, f32[128,512]{1,0:T(8,128)}, f32[128,128]{1,0:T(8,128)}) custom-call(s32[3]{0:T(128)} %pad_add_fusion.1.at_ref, s32[16,136,256]{2,1,0:T(8,128)} %all-to-all-done.two_ref, s32[16,136,256]{2,1,0:T(8,128)} %copy-done, f32[512,512]{1,0:T(8,128)} %get-tuple-element.20.top_ref), custom_call_target="tpu_custom_call" | custom-call | tf_op jit(solution)/shard_map/pallas_call | solution.py:210
  306.7 4.6 %shard_map.188 = f32[8,4096]{1,0:T(8,128)} custom-call(bf16[4096,256]{1,0:T(8,128)(2,1)} %bitcast.70, f32[128,128]{1,0:T(8,128)} %dynamic-slice_bitcast_fusion.tile_ref, f32[128,128]{1,0:T(8,128)} %get-tuple-element.29.cross_ref), custom_call_target="tpu_custom_call" | custom-call | tf_op jit(solution)/shard_map/pallas_call | solution.py:317
  313.0 6.6 %all-to-all-start.4 = ((f32[128,1,32]{2,1,0:T(1,128)}), f32[128,1,32]{2,1,0:T(1,128)S(1)}, u32[]{:S(2)}, u32[]{:S(2)}) async-start(f32[128,1,32]{2,1,0:T(1,128)} %bitcast.47), calls=%async_computation.4 | async-start | bytes 131072 | tf_op jit(solution)/shard_map/all_to_all | solution.py:488
  321.5 7.6 %all-to-all-done.4 = f32[128,1,32]{2,1,0:T(1,128)S(1)} async-done(((f32[128,1,32]{2,1,0:T(1,128)}), f32[128,1,32]{2,1,0:T(1,128)S(1)}, u32[]{:S(2)}, u32[]{:S(2)}) %all-to-all-start.4) | async-done | bytes 16416 | tf_op jit(solution)/shard_map/all_to_all | solution.py:488
  330.4 6.7 %shard_map.187 = (f32[512,512]{1,0:T(8,128)}, f32[512,512]{1,0:T(8,128)}, f32[512,512]{1,0:T(8,128)}) custom-call(s32[4]{0:T(128)} %pad_add_fusion.3.at_ref, f32[4,4,4,3,16,128]{5,4,3,2,1,0:T(8,128)} %pad_maximum_fusion.own_ref, f32[4,4,4,3,16,128]{5,4,3,2,1,0:T(8,128)} %collective-permute-done.28.other_ref, f32[2,512,512]{2,1,0:T(8,128)} %get-tuple-element.24.gram_ref, ...), custom_call_target="tpu_custom_call" | custom-call | tf_op jit(solution)/shard_map/pallas_call | solution.py:256
  337.2 4.0 %shard_map.189 = f32[8,2048]{1,0:T(8,128)} custom-call(bf16[2048,256]{1,0:T(8,128)(2,1)} %units_ref.1, s32[2048,1]{1,0:T(8,128)} %copy.27.panel_ref, f32[512,512]{1,0:T(8,128)} %get-tuple-element.16.diag_ref), custom_call_target="tpu_custom_call" | custom-call | tf_op jit(solution)/shard_map/pallas_call | solution.py:341
  (143 shorter events, 91.8 us)
Async XLA Ops:
  18.7 17.4 %collective-permute-start.2 = (s32[2,136,256]{2,1,0:T(8,128)S(1)}, s32[2,136,256]{2,1,0:T(8,128)S(1)}, u32[]{:S(2)}, u32[]{:S(2)}) collective-permute-start(s32[2,136,256]{2,1,0:T(8,128)S(1)} %collective-permute-done.refs_0_), channel_id=1, source_target_pairs={{0,32},{16,48},{32,64},{48,80},{64,96},{80,112},{96,0},{112,16},{1... | collective-permute-start | bytes 835592 | tf_op jit(solution)/shard_map/ppermute | solution.py:367
  36.1 18.9 %collective-permute-start.6 = (s32[136,256]{1,0:T(8,128)S(1)}, s32[136,256]{1,0:T(8,128)S(1)}, u32[]{:S(2)}, u32[]{:S(2)}) collective-permute-start(s32[136,256]{1,0:T(8,128)S(1)} %slice_bitcast_fusion.1), channel_id=1, source_target_pairs={{0,32},{16,48},{32,64},{48,80},{64,96},{80,112},{96,0},{112,16},{1... | collective-permute-start | bytes 417800 | tf_op jit(solution)/shard_map/ppermute | solution.py:367
  38.4 16.6 %collective-permute-start.7 = (s32[136,256]{1,0:T(8,128)S(1)}, s32[136,256]{1,0:T(8,128)S(1)}, u32[]{:S(2)}, u32[]{:S(2)}) collective-permute-start(s32[136,256]{1,0:T(8,128)S(1)} %slice_bitcast_fusion), channel_id=1, source_target_pairs={{0,96},{16,112},{32,0},{48,16},{64,32},{80,48},{96,64},{112,80},{1... | collective-permute-start | bytes 417800 | tf_op jit(solution)/shard_map/ppermute | solution.py:367
  40.9 26.5 %collective-permute-start.1 = (s32[2,136,256]{2,1,0:T(8,128)S(1)}, s32[2,136,256]{2,1,0:T(8,128)S(1)}, u32[]{:S(2)}, u32[]{:S(2)}) collective-permute-start(s32[2,136,256]{2,1,0:T(8,128)S(1)} %collective-permute-done.refs_0_), channel_id=1, source_target_pairs={{0,16},{16,0},{32,48},{48,32},{64,80},{80,64},{96,112},{112,96},{1... | collective-permute-start | bytes 835592 | tf_op jit(solution)/shard_map/ppermute | solution.py:367
  56.7 63.5 %all-to-all-start.3 = ((f32[16,128,128]{2,1,0:T(8,128)}), f32[16,128,128]{2,1,0:T(8,128)S(1)}, u32[]{:S(2)}, u32[]{:S(2)}) async-start(f32[16,128,128]{2,1,0:T(8,128)} %pad_maximum_fusion.1), calls=%async_computation.3 | async-start | bytes 2097152 | tf_op jit(solution)/shard_map/all_to_all | solution.py:458
  121.1 42.1 %all-to-all-start.1 = ((s32[16,136,256]{2,1,0:T(8,128)}), s32[16,136,256]{2,1,0:T(8,128)S(1)}, u32[]{:S(2)}, u32[]{:S(2)}) async-start(s32[16,136,256]{2,1,0:T(8,128)} %get-tuple-element.19), calls=%async_computation.1 | async-start | bytes 4456448 | tf_op jit(solution)/shard_map/all_to_all | solution.py:468
  133.2 36.3 %collective-permute-start.10 = (f32[3,64,512]{2,1,0:T(8,128)}, f32[3,64,512]{2,1,0:T(8,128)}, u32[]{:S(2)}, u32[]{:S(2)}) collective-permute-start(f32[3,64,512]{2,1,0:T(8,128)} %get-tuple-element.32), channel_id=1, source_target_pairs={{0,32},{16,48},{32,64},{48,80},{64,96},{80,112},{96,0},{112,16},{1... | collective-permute-start | bytes 1179656 | tf_op jit(solution)/shard_map/ppermute | solution.py:367
  134.2 35.3 %collective-permute-start.11 = (f32[3,64,512]{2,1,0:T(8,128)}, f32[3,64,512]{2,1,0:T(8,128)}, u32[]{:S(2)}, u32[]{:S(2)}) collective-permute-start(f32[3,64,512]{2,1,0:T(8,128)} %get-tuple-element.34), channel_id=1, source_target_pairs={{0,64},{16,80},{32,96},{48,112},{64,0},{80,16},{96,32},{112,48},{1... | collective-permute-start | bytes 1179656 | tf_op jit(solution)/shard_map/ppermute | solution.py:367
  137.6 31.9 %collective-permute-start.12 = (f32[3,64,512]{2,1,0:T(8,128)}, f32[3,64,512]{2,1,0:T(8,128)}, u32[]{:S(2)}, u32[]{:S(2)}) collective-permute-start(f32[3,64,512]{2,1,0:T(8,128)} %get-tuple-element.33), channel_id=1, source_target_pairs={{0,96},{16,112},{32,0},{48,16},{64,32},{80,48},{96,64},{112,80},{1... | collective-permute-start | bytes 1179656 | tf_op jit(solution)/shard_map/ppermute | solution.py:367
  164.6 60.4 %all-to-all-start = ((s32[16,136,256]{2,1,0:T(8,128)}), s32[16,136,256]{2,1,0:T(8,128)}, u32[]{:S(2)}, u32[]{:S(2)}) async-start(s32[16,136,256]{2,1,0:T(8,128)} %get-tuple-element.18), calls=%async_computation | async-start | bytes 4456448 | tf_op jit(solution)/shard_map/all_to_all | solution.py:466
  171.1 28.5 %collective-permute-start.13 = (f32[3,16,512]{2,1,0:T(8,128)S(1)}, f32[3,16,512]{2,1,0:T(8,128)S(1)}, u32[]{:S(2)}, u32[]{:S(2)}) collective-permute-start(f32[3,16,512]{2,1,0:T(8,128)S(1)} %get-tuple-element.39), channel_id=1, source_target_pairs={{0,1},{1,2},{2,3},{3,0},{4,5},{5,6},{6,7},{7,4},{8,9},{9,10},{10,1... | collective-permute-start | bytes 294920 | tf_op jit(solution)/shard_map/ppermute | solution.py:367
  172.4 31.8 %collective-permute-start.14 = (f32[3,16,512]{2,1,0:T(8,128)S(1)}, f32[3,16,512]{2,1,0:T(8,128)S(1)}, u32[]{:S(2)}, u32[]{:S(2)}) collective-permute-start(f32[3,16,512]{2,1,0:T(8,128)S(1)} %get-tuple-element.41), channel_id=1, source_target_pairs={{0,2},{1,3},{2,0},{3,1},{4,6},{5,7},{6,4},{7,5},{8,10},{9,11},{10,... | collective-permute-start | bytes 294920 | tf_op jit(solution)/shard_map/ppermute | solution.py:367
  174.8 29.4 %collective-permute-start.15 = (f32[3,16,512]{2,1,0:T(8,128)S(1)}, f32[3,16,512]{2,1,0:T(8,128)S(1)}, u32[]{:S(2)}, u32[]{:S(2)}) collective-permute-start(f32[3,16,512]{2,1,0:T(8,128)S(1)} %get-tuple-element.40), channel_id=1, source_target_pairs={{0,3},{1,0},{2,1},{3,2},{4,7},{5,4},{6,5},{7,6},{8,11},{9,8},{10,9... | collective-permute-start | bytes 294920 | tf_op jit(solution)/shard_map/ppermute | solution.py:367
  209.6 25.8 %collective-permute-start.19 = (f32[3,16,128]{2,1,0:T(8,128)S(1)}, f32[3,16,128]{2,1,0:T(8,128)S(1)}, u32[]{:S(2)}, u32[]{:S(2)}) collective-permute-start(f32[3,16,128]{2,1,0:T(8,128)S(1)} %add_add_fusion.2), channel_id=1, source_target_pairs={{0,4},{1,5},{2,6},{3,7},{4,8},{5,9},{6,10},{7,11},{8,12},{9,13},{1... | collective-permute-start | bytes 73736 | tf_op jit(solution)/shard_map/ppermute | solution.py:367
  210.5 24.9 %collective-permute-start.20 = (f32[3,16,128]{2,1,0:T(8,128)S(1)}, f32[3,16,128]{2,1,0:T(8,128)S(1)}, u32[]{:S(2)}, u32[]{:S(2)}) collective-permute-start(f32[3,16,128]{2,1,0:T(8,128)S(1)} %add_add_fusion.2), channel_id=1, source_target_pairs={{0,8},{1,9},{2,10},{3,11},{4,12},{5,13},{6,14},{7,15},{8,0},{9,1},... | collective-permute-start | bytes 73736 | tf_op jit(solution)/shard_map/ppermute | solution.py:367
  213.7 21.8 %collective-permute-start.21 = (f32[3,16,128]{2,1,0:T(8,128)S(1)}, f32[3,16,128]{2,1,0:T(8,128)S(1)}, u32[]{:S(2)}, u32[]{:S(2)}) collective-permute-start(f32[3,16,128]{2,1,0:T(8,128)S(1)} %add_add_fusion.2), channel_id=1, source_target_pairs={{0,12},{1,13},{2,14},{3,15},{4,0},{5,1},{6,2},{7,3},{8,4},{9,5},{1... | collective-permute-start | bytes 73736 | tf_op jit(solution)/shard_map/ppermute | solution.py:367
  225.0 80.3 %all-to-all-start.2 = ((bf16[128,32,256]{2,1,0:T(8,128)(2,1)}), bf16[128,32,256]{2,1,0:T(8,128)(2,1)S(1)}, u32[]{:S(2)}, u32[]{:S(2)}) async-start(bf16[128,32,256]{2,1,0:T(8,128)(2,1)} %bitcast.36), calls=%async_computation.2 | async-start | bytes 4194304 | tf_op jit(solution)/shard_map/all_to_all | solution.py:447
  235.5 27.2 %collective-permute-start.22 = (f32[4,3,16,128]{3,2,1,0:T(8,128)S(1)}, f32[4,3,16,128]{3,2,1,0:T(8,128)S(1)}, u32[]{:S(2)}, u32[]{:S(2)}) collective-permute-start(f32[4,3,16,128]{3,2,1,0:T(8,128)S(1)} %get-tuple-element.43), channel_id=1, source_target_pairs={{0,1},{1,2},{2,3},{3,0},{4,5},{5,6},{6,7},{7,4},{8,9},{9,10},{10,1... | collective-permute-start | bytes 294920 | tf_op jit(solution)/shard_map/ppermute | solution.py:367
  236.9 28.2 %collective-permute-start.23 = (f32[4,3,16,128]{3,2,1,0:T(8,128)S(1)}, f32[4,3,16,128]{3,2,1,0:T(8,128)S(1)}, u32[]{:S(2)}, u32[]{:S(2)}) collective-permute-start(f32[4,3,16,128]{3,2,1,0:T(8,128)S(1)} %get-tuple-element.43), channel_id=1, source_target_pairs={{0,2},{1,3},{2,0},{3,1},{4,6},{5,7},{6,4},{7,5},{8,10},{9,11},{10,... | collective-permute-start | bytes 294920 | tf_op jit(solution)/shard_map/ppermute | solution.py:367
  239.3 25.8 %collective-permute-start.24 = (f32[4,3,16,128]{3,2,1,0:T(8,128)S(1)}, f32[4,3,16,128]{3,2,1,0:T(8,128)S(1)}, u32[]{:S(2)}, u32[]{:S(2)}) collective-permute-start(f32[4,3,16,128]{3,2,1,0:T(8,128)S(1)} %get-tuple-element.43), channel_id=1, source_target_pairs={{0,3},{1,0},{2,1},{3,2},{4,7},{5,4},{6,5},{7,6},{8,11},{9,8},{10,9... | collective-permute-start | bytes 294920 | tf_op jit(solution)/shard_map/ppermute | solution.py:367
  266.6 19.7 %collective-permute-start.26 = (f32[4,4,3,16,128]{4,3,2,1,0:T(8,128)S(1)}, f32[4,4,3,16,128]{4,3,2,1,0:T(8,128)S(1)}, u32[]{:S(2)}, u32[]{:S(2)}) collective-permute-start(f32[4,4,3,16,128]{4,3,2,1,0:T(8,128)S(1)} %get-tuple-element.38), channel_id=1, source_target_pairs={{0,64},{16,80},{32,96},{48,112},{64,0},{80,16},{96,32},{112,48},{1... | collective-permute-start | bytes 1179656 | tf_op jit(solution)/shard_map/ppermute | solution.py:367
  269.5 16.7 %collective-permute-start.27 = (f32[4,4,3,16,128]{4,3,2,1,0:T(8,128)S(1)}, f32[4,4,3,16,128]{4,3,2,1,0:T(8,128)S(1)}, u32[]{:S(2)}, u32[]{:S(2)}) collective-permute-start(f32[4,4,3,16,128]{4,3,2,1,0:T(8,128)S(1)} %get-tuple-element.38), channel_id=1, source_target_pairs={{0,96},{16,112},{32,0},{48,16},{64,32},{80,48},{96,64},{112,80},{1... | collective-permute-start | bytes 1179656 | tf_op jit(solution)/shard_map/ppermute | solution.py:367
  287.6 42.8 %collective-permute-start.28 = (f32[4,4,4,3,16,128]{5,4,3,2,1,0:T(8,128)}, f32[4,4,4,3,16,128]{5,4,3,2,1,0:T(8,128)}, u32[]{:S(2)}, u32[]{:S(2)}) collective-permute-start(f32[4,4,4,3,16,128]{5,4,3,2,1,0:T(8,128)} %pad_maximum_fusion.own_ref), channel_id=1, source_target_pairs={{0,16},{16,0},{32,48},{48,32},{64,80},{80,64},{96,112},{112,96},{1... | collective-permute-start | bytes 4718600 | tf_op jit(solution)/shard_map/ppermute | solution.py:367
  313.0 16.1 %all-to-all-start.4 = ((f32[128,1,32]{2,1,0:T(1,128)}), f32[128,1,32]{2,1,0:T(1,128)S(1)}, u32[]{:S(2)}, u32[]{:S(2)}) async-start(f32[128,1,32]{2,1,0:T(1,128)} %bitcast.47), calls=%async_computation.4 | async-start | bytes 131072 | tf_op jit(solution)/shard_map/all_to_all | solution.py:488
  (29 other events, 225.2 us)

commit v2 on v1

--- a/solution.py
+++ b/solution.py
@@ -12,6 +12,7 @@
 STEPS = 64.0
 TINY = 1e-33
 ROOM = 56 * 1024 * 1024
+LIGHT = pl.CostEstimate(flops=1, bytes_accessed=1, transcendentals=0)
 
 
 def split(value):
@@ -106,7 +107,7 @@
         encode(image[i * bw : (i + 1) * bw], code_ref, i)
 
 
-def image(at, trail_cov, held, panel, bw, tile=256):
+def image(at, trail_cov, held, panel, bw, tile=512):
     rows, span = trail_cov.shape
     width = 2 * held[0].shape[-1]
     every = pl.BlockSpec(held[0].shape, lambda i, at: (0, 0, 0))
@@ -127,9 +128,7 @@
             scratch_shapes=[pltpu.VMEM((span, width), jnp.bfloat16)] * 2,
         ),
         compiler_params=pltpu.CompilerParams(vmem_limit_bytes=ROOM),
-        cost_estimate=pl.CostEstimate(
-            flops=6 * rows * span * width, bytes_accessed=4 * rows * (span + width), transcendentals=0
-        ),
+        cost_estimate=LIGHT,
     )(at, trail_cov, *held)
 
 
@@ -166,7 +165,7 @@
             out_ref[i] = product(inv[...], out_ref[i], tdot)
 
 
-def sums(bits_two, bits_one, panel_two, panel_one, image_two, image_one, inv_two, inv_one, bw, tile=256):
+def sums(bits_two, bits_one, panel_two, panel_one, image_two, image_one, inv_two, inv_one, bw, tile=512):
     rows, width = panel_two.shape
     part = pl.BlockSpec((tile, width), lambda i, *_: (i, 0))
     whole = pl.BlockSpec((width, width), lambda i, *_: (0, 0))
@@ -180,9 +179,7 @@
             out_specs=pl.BlockSpec((3, width, width), lambda i, *_: (0, 0, 0)),
         ),
         compiler_params=pltpu.CompilerParams(vmem_limit_bytes=ROOM),
-        cost_estimate=pl.CostEstimate(
-            flops=18 * rows * width * width, bytes_accessed=16 * rows * width, transcendentals=0
-        ),
+        cost_estimate=LIGHT,
     )(bits_two, bits_one, panel_two, panel_one, image_two, image_one, inv_two, inv_one)
 
 
@@ -381,6 +378,21 @@
 
     def gather(self, value):
         return jnp.stack([value] + [self.move(value, step) for step in range(1, self.count)])
+
+
+def spread_plan(row_count, col_count):
+    plan = []
+    for r in range(row_count):
+        z = r // 2
+        first = col_count // row_count * r
+        for c in range(col_count):
+            x, y = c % 4, c // 4
+            x_first = first % 4
+            side = 0 if x in (x_first, (x_first - 1) % 4) else 1
+            half = 0 if x in (x_first, (x_first + 1) % 4) else 1
+            j = y % 4 * 2 + half
+            plan.append((side * row_count + j, j * col_count + first + side))
+    return plan
 
 
 def local(
@@ -422,49 +434,62 @@
     own_two = lax.dynamic_index_in_dim(bits_two, col_index, 0, False)
     own_one = lax.dynamic_index_in_dim(bits_one, col_index, 0, False)
 
+    spread = spread_plan(row_count, col_count)
+    chosen = jnp.array([block for block, _ in spread], jnp.int32)[owner]
     part = share(
-        jnp.stack([col_index, own_two, own_one]),
+        jnp.stack([chosen, bits_two[chosen], bits_one[chosen]]),
         panel_two_rows, panel_one_rows, diag_inv_two, diag_inv_one, bw,
     )
-    moves = [(i, i % row_count * col_count + i // row_count) for i in range(total_count)]
-    part = lax.ppermute(part, BOTH, moves)
-    after, before = ring_z.move(part, 1), ring_z.move(part, -1)
-    far = jnp.stack([ring_z.move(after[0], 1), ring_z.move(before[1], -1)])
+    blocks, side = unit_block[:, 0], col_index % ratio
+    part, blocks, side = lax.optimization_barrier((part, blocks, side))
+    part = lax.ppermute(part, BOTH, [(i, j) for i, (_, j) in enumerate(spread)])
     held, places = [], []
-    for step, piece in ((0, part), (1, after), (-1, before), (2, far)):
+    for step in range(4):
+        piece = ring_z.move(part, step) if step else part
         at = (ring_z.place() - step) % 4 * 2
         held += [piece, core.move(piece, 1)]
         places += [at + core.place(), at + 1 - core.place()]
     places = jnp.stack(places)
 
-    blocks = unit_block[:, 0]
+    tiles = jnp.stack(
+        [
+            lax.dynamic_slice(trail_cov, ((side * row_count + j) * bw, j * bw), (bw, bw))
+            for j in range(row_count)
+        ]
+    )
+    at = col_index % row_count
+    pairs = [
+        (r * col_count + ratio * r + h, r * col_count + h * row_count)
+        for r in range(row_count)
+        for h in range(ratio)
+    ]
+    tiles = lax.ppermute(tiles, BOTH, pairs)
+    half = row_count // 2
+    while half:
+        pairs = [(c, c + half) for c in range(0, col_count, 2 * half)]
+        handed = lax.ppermute(tiles[half:], "col", pairs)
+        tiles = jnp.where(at // half % 2 == 1, handed, tiles[:half])
+        half //= 2
+    tile = tiles[0]
+
     capacity = 2 * loadings.shape[0] // total_count
     hits = (blocks[:, None] == jnp.arange(total_count, dtype=jnp.int32)[None, :]).astype(jnp.int32)
     rank = jnp.sum(jnp.cumsum(hits, axis=0) * hits, axis=1) - 1
     slot = blocks * capacity + rank
     packed = jnp.zeros((total_count * capacity, 2 * bw), jnp.bfloat16).at[slot].set(loadings)
     packed = packed.reshape(total_count, capacity, 2 * bw)
+    packed, held[2] = lax.optimization_barrier((packed, held[2]))
     units = lax.all_to_all(packed, BOTH, split_axis=0, concat_axis=0, tiled=True)
     units = units.reshape(total_count * capacity, 2 * bw)
 
-    side = col_index % ratio
-    tiles = jnp.stack(
-        [
-            lax.dynamic_slice(trail_cov, ((side * row_count + j) * bw, j * bw), (bw, bw))
-            for j in range(row_count)
-        ]
-    )
-    tiles = jnp.concatenate([jnp.where(side == h, tiles, 0.0) for h in range(ratio)])
-    tiles = lax.all_to_all(tiles, "col", split_axis=0, concat_axis=0, tiled=True)
-    tile = lax.dynamic_index_in_dim(
-        tiles, row_index * ratio + col_index // row_count, 0, keepdims=False
-    )
-
     gram, norm_top = early(bits_top, panel_one_top, diag_inv_two, diag_inv_one)
+    places, norm_top = lax.optimization_barrier((places, norm_top))
 
     image_two, code_two = image(places, trail_cov, held, 0, bw)
+    code_two, units = lax.optimization_barrier((code_two, units))
     code_two = lax.all_to_all(code_two, "col", split_axis=0, concat_axis=0, tiled=True)
     image_one, code_one = image(places, trail_cov, held, 1, bw)
+    code_one, code_two = lax.optimization_barrier((code_one, code_two))
     code_one = lax.all_to_all(code_one, "col", split_axis=0, concat_axis=0, tiled=True)
 
     total = sums(
@@ -475,17 +500,19 @@
     total = ring_z.scatter_sum(total, 1)
     total = ring_x.scatter_sum(total, 1)
     total = ring_y.scatter_sum(total, 2)
-    total = ring_z.gather(ring_x.gather(ring_y.gather(total)))
-    spots = jnp.stack([ring_x.place(), ring_y.place(), ring_z.place(), core.place()])
-    diag_two, top_cov, diag_one = small(
-        spots, total, core.move(total, 1), gram, norm_top, bits_top
-    )
-
+    total, code_one = lax.optimization_barrier((total, code_one))
+    total = ring_x.gather(ring_y.gather(total))
     cov_two, cov_one, cross = rows(
         jnp.stack([own_two, own_one, block_panel[owner]]), code_two, code_one, norm_top, bw
     )
     value = forms(units, tile, cross)[0].reshape(total_count, capacity)
+    total, value = lax.optimization_barrier((total, value))
     returned = lax.all_to_all(value, BOTH, split_axis=0, concat_axis=0, tiled=True)
+    total = ring_z.gather(total)
+    total, returned = lax.optimization_barrier((total, returned))
+    other = core.move(total, 1)
+    spots = jnp.stack([ring_x.place(), ring_y.place(), ring_z.place(), core.place()])
+    diag_two, top_cov, diag_one = small(spots, total, other, gram, norm_top, bits_top)
     picked = jnp.dot(
         hits.astype(jnp.float32), returned, precision=lax.Precision.HIGHEST,
         preferred_element_type=jnp.float32,

time: 345 us -> 295 us (0.86)
  waiting for transfers between devices: 106 us -> 71.1 us
  starting transfers between devices: 103 us -> 87.2 us
  local copies, waits for them, and re-layouts: 39.7 us -> 43.7 us
    ppermute x28 -> x27, starting transfers between devices: 59.9 us -> 30.8 us  [move(): return lax.ppermute(value, self.axis, pairs)]
    all_to_all x1, waiting for transfers between devices: 25.5 us -> 0.01 us  [local(): lax.all_to_all(code_one, 'col', split_axis=0, concat_axis=0, tiled=True)]
    ppermute x28 -> x27, waiting for transfers between devices: 71.3 us -> 56 us  [move(): return lax.ppermute(value, self.axis, pairs)]
    ppermute x1 -> x5, waiting for transfers between devices: 1.28 us -> 11.1 us  [the longest x3 7.09 us: local(): handed = lax.ppermute(tiles[half:], 'col', pairs)]
    all_to_all x1 -> x0, starting transfers between devices: 8.65 us -> none  [local(): lax.all_to_all(tiles, 'col', split_axis=0, concat_axis=0, tiled=True)]
    all_to_all x1, starting transfers between devices: 6.55 us -> 13 us  [local(): lax.all_to_all(value, BOTH, split_axis=0, concat_axis=0, tiled=True)]
    ppermute x1 -> x5, starting transfers between devices: 6.03 us -> 12.3 us  [the longest x3 5.83 us: local(): handed = lax.ppermute(tiles[half:], 'col', pairs)]
    all_to_all x1, starting transfers between devices: 10.4 us -> 16.6 us  [local(): lax.all_to_all(packed, BOTH, split_axis=0, concat_axis=0, tiled=True)]
  transfers between devices with their start and end apart: 34 -> 36, of which waited for: 12 -> 12; matrix products, arithmetic and copies ran while one was open for 12% -> 14% of each run, Pallas kernels for 19% -> 20%
where the time goes in v2:
time: 295 us; the launch traced here: 294 us
  starting transfers between devices  87.2 us (30%)
  Pallas kernels  74.9 us (25%)
  waiting for transfers between devices  71.1 us (24%)
  local copies, waits for them, and re-layouts  43.7 us (15%)
  other arithmetic  12.1 us (4%)
  between operations  3.19 us (1%)
    ppermute x27, waiting for transfers between devices, move(): return lax.ppermute(value, self.axis, pairs)  56 us
    ppermute x27, starting transfers between devices, move(): return lax.ppermute(value, self.axis, pairs)  30.8 us
    pallas_call x2, Pallas kernels, image(): pl.pallas_call(functools.partial(image_kernel, panel, bw, len(held)), out...  24.9 us
    pallas_call x1, Pallas kernels, sums(): pl.pallas_call(functools.partial(sums_kernel, bw), out_shape=jax.ShapeDty...  19.7 us
    all_to_all x1, starting transfers between devices, local(): lax.all_to_all(packed, BOTH, split_axis=0, concat_axis=0, tiled=True)  16.6 us
    unnamed x41, local copies, waits for them, and re-layouts  15.3 us
    all_to_all x1, starting transfers between devices, local(): lax.all_to_all(value, BOTH, split_axis=0, concat_axis=0, tiled=True)  13 us
    scatter x1, local copies, waits for them, and re-layouts, local(): jnp.zeros((total_count * capacity, 2 * bw), jnp.bfloat16).at[slot]  11.3 us
  transfers between devices with their start and end apart: 36, of which 12 were waited for; matrix products, arithmetic and copies ran while one was open for 14% of the time, Pallas kernels for 20%

profile of v2, /device:TPU:1, one launch (start us, length us, event | category | flops | bytes accessed | tf_op | source)
XLA Modules:
  0.0 293.7 jit_solution(11958251127034931875)
XLA Ops:
  7.8 4.5 %pad_add_fusion = (s32[3]{0:T(128)}, s32[3]{0:T(128)}) fusion(s32[1]{0:T(128)} %dynamic_slice.103, s32[1]{0:T(128)} %get-tuple-element.80, s32[1]{0:T(128)} %get-tuple-element.82, s32[1]{0:T(128)} %get-tuple-element.79, s32[1]{0:T(128)} %get-tuple-element.81, s32[1]{0:T(128)} %dynamic_slice.104), kind=kLoop, calls=%fused_computation.66 | loop fusion | flops 12 | bytes 48 | tf_op jit(solution)/shard_map/stack | solution.py:506
  16.2 5.2 %collective-permute-start = (s32[2,136,256]{2,1,0:T(8,128)}, s32[2,136,256]{2,1,0:T(8,128)S(1)}, u32[]{:S(2)}, u32[]{:S(2)}) collective-permute-start(s32[2,136,256]{2,1,0:T(8,128)} %shard_map.191), channel_id=1, source_target_pairs={{0,0},{1,1},{2,17},{3,16},{4,32},{5,33},{6,49},{7,48},{8,64},{9,65... | collective-permute-start | bytes 835592 | tf_op jit(solution)/shard_map/ppermute | solution.py:445
  22.3 4.0 %collective-permute-done.refs_0_ = s32[2,136,256]{2,1,0:T(8,128)S(1)} collective-permute-done((s32[2,136,256]{2,1,0:T(8,128)}, s32[2,136,256]{2,1,0:T(8,128)S(1)}, u32[]{:S(2)}, u32[]{:S(2)}) %collective-permute-start) | collective-permute-done | bytes 278560 | tf_op jit(solution)/shard_map/ppermute | solution.py:445
  26.4 4.5 %collective-permute-start.2 = (s32[2,136,256]{2,1,0:T(8,128)S(1)}, s32[2,136,256]{2,1,0:T(8,128)S(1)}, u32[]{:S(2)}, u32[]{:S(2)}) collective-permute-start(s32[2,136,256]{2,1,0:T(8,128)S(1)} %collective-permute-done.refs_0_), channel_id=1, source_target_pairs={{0,32},{16,48},{32,64},{48,80},{64,96},{80,112},{96,0},{112,16},{1... | collective-permute-start | bytes 835592 | tf_op jit(solution)/shard_map/ppermute | solution.py:364
  32.0 11.3 %scatter_custom_fusion = bf16[4096,256]{1,0:T(8,128)(2,1)} fusion(s32[2048]{0:T(1024)S(1)} %get-tuple-element.78, bf16[2048,256]{1,0:T(8,128)(2,1)} %units_ref.1, bf16[]{:T(256)} %constant.386.clone.1), kind=kCustom, calls=%fused_computation.14 | custom fusion | bytes 2097664 | tf_op jit(solution)/shard_map/scatter | solution.py:479
  43.3 16.6 %all-to-all-start = ((bf16[128,32,256]{2,1,0:T(8,128)(2,1)}), bf16[128,32,256]{2,1,0:T(8,128)(2,1)S(1)}, u32[]{:S(2)}, u32[]{:S(2)}) async-start(bf16[128,32,256]{2,1,0:T(8,128)(2,1)} %bitcast.64), calls=%async_computation | async-start | bytes 4194304 | tf_op jit(solution)/shard_map/all_to_all | solution.py:482
  65.0 27.2 %collective-permute-done.4.refs_4_ = s32[2,136,256]{2,1,0:T(8,128)S(1)} collective-permute-done((s32[2,136,256]{2,1,0:T(8,128)S(1)}, s32[2,136,256]{2,1,0:T(8,128)S(1)}, u32[]{:S(2)}, u32[]{:S(2)}) %collective-permute-start.4) | collective-permute-done | bytes 278560 | tf_op jit(solution)/shard_map/ppermute | solution.py:364
  92.9 4.2 %collective-permute-done.6.refs_6_ = s32[2,136,256]{2,1,0:T(8,128)S(1)} collective-permute-done((s32[2,136,256]{2,1,0:T(8,128)S(1)}, s32[2,136,256]{2,1,0:T(8,128)S(1)}, u32[]{:S(2)}, u32[]{:S(2)}) %collective-permute-start.6) | collective-permute-done | bytes 278560 | tf_op jit(solution)/shard_map/ppermute | solution.py:364
  98.2 5.9 %shard_map.190 = (f32[2,512,512]{2,1,0:T(8,128)}, f32[512,512]{1,0:T(8,128)}) custom-call(s32[4]{0:T(128)} %slice.33.keep_ref, f32[512,512]{1,0:T(8,128)} %top_rows_ref.1, f32[512,512]{1,0:T(8,128)} %inv_two_ref.5, f32[512,512]{1,0:T(8,128)} %inv_one_ref.5), custom_call_target="tpu_custom_call" | custom-call | tf_op jit(solution)/shard_map/pallas_call | solution.py:280
  104.7 12.5 %shard_map.193 = (f32[2048,512]{1,0:T(8,128)}, s32[16,136,256]{2,1,0:T(8,128)}) custom-call(s32[8]{0:T(128)} %stack.131.at_ref, f32[2048,1024]{1,0:T(8,128)} %cov_ref.3, s32[2,136,256]{2,1,0:T(8,128)} %copy-done.6, s32[2,136,256]{2,1,0:T(8,128)} %collective-permute-done.1.refs_1_, s32[2,136,256]{2,1,0:T(8,128)} %copy-done.7, ...), custom_call_target="tpu_custom_call" | custom-call | flops 1 | bytes 1 | tf_op jit(solution)/shard_map/pallas_call | solution.py:114
  118.5 5.8 %all-to-all-start.1 = ((s32[16,136,256]{2,1,0:T(8,128)}), s32[16,136,256]{2,1,0:T(8,128)S(1)}, u32[]{:S(2)}, u32[]{:S(2)}) async-start(s32[16,136,256]{2,1,0:T(8,128)} %get-tuple-element.43), calls=%async_computation.1 | async-start | bytes 4456448 | tf_op jit(solution)/shard_map/all_to_all | solution.py:490
  125.5 12.5 %shard_map.192 = (f32[2048,512]{1,0:T(8,128)}, s32[16,136,256]{2,1,0:T(8,128)}) custom-call(s32[8]{0:T(128)} %stack.131.at_ref, f32[2048,1024]{1,0:T(8,128)} %cov_ref.3, s32[2,136,256]{2,1,0:T(8,128)} %copy-done.6, s32[2,136,256]{2,1,0:T(8,128)} %collective-permute-done.1.refs_1_, s32[2,136,256]{2,1,0:T(8,128)} %copy-done.7, ...), custom_call_target="tpu_custom_call" | custom-call | flops 1 | bytes 1 | tf_op jit(solution)/shard_map/pallas_call | solution.py:114
  138.0 19.7 %shard_map.194 = f32[3,512,512]{2,1,0:T(8,128)} custom-call(s32[16]{0:T(128)} %dynamic_slice.109.bits_two_ref, s32[16]{0:T(128)} %dynamic_slice.110.bits_one_ref, f32[2048,512]{1,0:T(8,128)} %two_ref.3, f32[2048,512]{1,0:T(8,128)} %one_ref.3, f32[2048,512]{1,0:T(8,128)} %get-tuple-element.45.image_two_ref, f32[2048,512]{1,0:T(8,128)} %get-tuple-element.46.image_one_ref, ...), custom_call_target="tpu_custom_call" | custom-call | flops 1 | bytes 1 | tf_op jit(solution)/shard_map/pallas_call | solution.py:172
  175.3 8.6 %all-to-all-start.2 = ((s32[16,136,256]{2,1,0:T(8,128)}), s32[16,136,256]{2,1,0:T(8,128)}, u32[]{:S(2)}, u32[]{:S(2)}) async-start(s32[16,136,256]{2,1,0:T(8,128)} %get-tuple-element.47), calls=%async_computation.2 | async-start | bytes 4456448 | tf_op jit(solution)/shard_map/all_to_all | solution.py:493
  201.4 8.3 %collective-permute-done.9 = f32[3,64,512]{2,1,0:T(8,128)S(1)} collective-permute-done((f32[3,64,512]{2,1,0:T(8,128)S(1)}, f32[3,64,512]{2,1,0:T(8,128)S(1)}, u32[]{:S(2)}, u32[]{:S(2)}) %collective-permute-start.9) | collective-permute-done | bytes 393248 | tf_op jit(solution)/shard_map/ppermute | solution.py:364
  214.7 7.1 %collective-permute-done.25 = f32[4,128,128]{2,1,0:T(8,128)S(1)} collective-permute-done((f32[4,128,128]{2,1,0:T(8,128)S(1)}, f32[4,128,128]{2,1,0:T(8,128)S(1)}, u32[]{:S(2)}, u32[]{:S(2)}) %collective-permute-start.25) | collective-permute-done | bytes 262176 | tf_op jit(solution)/shard_map/ppermute | solution.py:470
  224.3 4.0 %collective-permute-start.16 = (f32[3,16,128]{2,1,0:T(8,128)S(1)}, f32[3,16,128]{2,1,0:T(8,128)S(1)}, u32[]{:S(2)}, u32[]{:S(2)}) collective-permute-start(f32[3,16,128]{2,1,0:T(8,128)S(1)} %get-tuple-element.76), channel_id=1, source_target_pairs={{0,8},{1,9},{2,10},{3,11},{4,12},{5,13},{6,14},{7,15},{8,0},{9,1},... | collective-permute-start | bytes 73736 | tf_op jit(solution)/shard_map/ppermute | solution.py:364
  234.4 5.0 %shard_map.195 = (f32[128,512]{1,0:T(8,128)}, f32[128,512]{1,0:T(8,128)}, f32[128,128]{1,0:T(8,128)}) custom-call(s32[3]{0:T(128)} %get-tuple-element.83.at_ref, s32[16,136,256]{2,1,0:T(8,128)} %copy-done.1, s32[16,136,256]{2,1,0:T(8,128)} %all-to-all-done.2.one_ref, f32[512,512]{1,0:T(8,128)} %get-tuple-element.49.top_ref), custom_call_target="tpu_custom_call" | custom-call | tf_op jit(solution)/shard_map/pallas_call | solution.py:207
  239.4 4.6 %shard_map.196 = f32[8,4096]{1,0:T(8,128)} custom-call(bf16[4096,256]{1,0:T(8,128)(2,1)} %bitcast.63, f32[128,128]{1,0:T(8,128)} %fusion.10.tile_ref, f32[128,128]{1,0:T(8,128)} %get-tuple-element.54.cross_ref), custom_call_target="tpu_custom_call" | custom-call | tf_op jit(solution)/shard_map/pallas_call | solution.py:314
  253.3 13.0 %all-to-all-start.3 = ((f32[128,1,32]{2,1,0:T(1,128)}), f32[128,1,32]{2,1,0:T(1,128)S(1)}, u32[]{:S(2)}, u32[]{:S(2)}) async-start(f32[128,1,32]{2,1,0:T(1,128)} %bitcast.42), calls=%async_computation.3 | async-start | bytes 131072 | tf_op jit(solution)/shard_map/all_to_all | solution.py:510
  266.3 5.3 %collective-permute-done.28 = f32[4,4,3,16,128]{4,3,2,1,0:T(8,128)S(1)} collective-permute-done((f32[4,4,3,16,128]{4,3,2,1,0:T(8,128)S(1)}, f32[4,4,3,16,128]{4,3,2,1,0:T(8,128)S(1)}, u32[]{:S(2)}, u32[]{:S(2)}) %collective-permute-start.28) | collective-permute-done | bytes 393248 | tf_op jit(solution)/shard_map/ppermute | solution.py:364
  271.8 4.0 %all-to-all-done.3 = f32[128,1,32]{2,1,0:T(1,128)S(1)} async-done(((f32[128,1,32]{2,1,0:T(1,128)}), f32[128,1,32]{2,1,0:T(1,128)S(1)}, u32[]{:S(2)}, u32[]{:S(2)}) %all-to-all-start.3) | async-done | bytes 16416 | tf_op jit(solution)/shard_map/all_to_all | solution.py:510
  281.3 6.7 %shard_map.197 = (f32[512,512]{1,0:T(8,128)}, f32[512,512]{1,0:T(8,128)}, f32[512,512]{1,0:T(8,128)}) custom-call(s32[4]{0:T(128)} %pad_add_fusion.2.at_ref, f32[4,4,4,3,16,128]{5,4,3,2,1,0:T(8,128)} %copy-done.4, f32[4,4,4,3,16,128]{5,4,3,2,1,0:T(8,128)} %copy-done.5, f32[2,512,512]{2,1,0:T(8,128)} %get-tuple-element.58.gram_ref, ...), custom_call_target="tpu_custom_call" | custom-call | tf_op jit(solution)/shard_map/pallas_call | solution.py:253
  288.0 4.0 %shard_map.198 = f32[8,2048]{1,0:T(8,128)} custom-call(bf16[2048,256]{1,0:T(8,128)(2,1)} %units_ref.1, s32[2048,1]{1,0:T(8,128)} %copy.27.panel_ref, f32[512,512]{1,0:T(8,128)} %get-tuple-element.33.diag_ref), custom_call_target="tpu_custom_call" | custom-call | tf_op jit(solution)/shard_map/pallas_call | solution.py:338
  (142 shorter events, 85.8 us)
Async XLA Ops:
  26.4 16.9 %collective-permute-start.2 = (s32[2,136,256]{2,1,0:T(8,128)S(1)}, s32[2,136,256]{2,1,0:T(8,128)S(1)}, u32[]{:S(2)}, u32[]{:S(2)}) collective-permute-start(s32[2,136,256]{2,1,0:T(8,128)S(1)} %collective-permute-done.refs_0_), channel_id=1, source_target_pairs={{0,32},{16,48},{32,64},{48,80},{64,96},{80,112},{96,0},{112,16},{1... | collective-permute-start | bytes 835592 | tf_op jit(solution)/shard_map/ppermute | solution.py:364
  43.3 73.8 %all-to-all-start = ((bf16[128,32,256]{2,1,0:T(8,128)(2,1)}), bf16[128,32,256]{2,1,0:T(8,128)(2,1)S(1)}, u32[]{:S(2)}, u32[]{:S(2)}) async-start(bf16[128,32,256]{2,1,0:T(8,128)(2,1)} %bitcast.64), calls=%async_computation | async-start | bytes 4194304 | tf_op jit(solution)/shard_map/all_to_all | solution.py:482
  60.0 32.2 %collective-permute-start.4 = (s32[2,136,256]{2,1,0:T(8,128)S(1)}, s32[2,136,256]{2,1,0:T(8,128)S(1)}, u32[]{:S(2)}, u32[]{:S(2)}) collective-permute-start(s32[2,136,256]{2,1,0:T(8,128)S(1)} %collective-permute-done.refs_0_), channel_id=1, source_target_pairs={{0,64},{16,80},{32,96},{48,112},{64,0},{80,16},{96,32},{112,48},{1... | collective-permute-start | bytes 835592 | tf_op jit(solution)/shard_map/ppermute | solution.py:364
  63.4 33.8 %collective-permute-start.6 = (s32[2,136,256]{2,1,0:T(8,128)S(1)}, s32[2,136,256]{2,1,0:T(8,128)S(1)}, u32[]{:S(2)}, u32[]{:S(2)}) collective-permute-start(s32[2,136,256]{2,1,0:T(8,128)S(1)} %collective-permute-done.refs_0_), channel_id=1, source_target_pairs={{0,96},{16,112},{32,0},{48,16},{64,32},{80,48},{96,64},{112,80},{1... | collective-permute-start | bytes 835592 | tf_op jit(solution)/shard_map/ppermute | solution.py:364
  64.0 40.7 %collective-permute-start.1 = (s32[2,136,256]{2,1,0:T(8,128)S(1)}, s32[2,136,256]{2,1,0:T(8,128)}, u32[]{:S(2)}, u32[]{:S(2)}) collective-permute-start(s32[2,136,256]{2,1,0:T(8,128)S(1)} %collective-permute-done.refs_0_), channel_id=1, source_target_pairs={{0,16},{16,0},{32,48},{48,32},{64,80},{80,64},{96,112},{112,96},{1... | collective-permute-start | bytes 835592 | tf_op jit(solution)/shard_map/ppermute | solution.py:364
  64.9 39.8 %collective-permute-start.3 = (s32[2,136,256]{2,1,0:T(8,128)S(1)}, s32[2,136,256]{2,1,0:T(8,128)}, u32[]{:S(2)}, u32[]{:S(2)}) collective-permute-start(s32[2,136,256]{2,1,0:T(8,128)S(1)} %collective-permute-done.2.refs_2_), channel_id=1, source_target_pairs={{0,16},{16,0},{32,48},{48,32},{64,80},{80,64},{96,112},{112,96},{1... | collective-permute-start | bytes 835592 | tf_op jit(solution)/shard_map/ppermute | solution.py:364
  92.2 12.5 %collective-permute-start.5 = (s32[2,136,256]{2,1,0:T(8,128)S(1)}, s32[2,136,256]{2,1,0:T(8,128)}, u32[]{:S(2)}, u32[]{:S(2)}) collective-permute-start(s32[2,136,256]{2,1,0:T(8,128)S(1)} %collective-permute-done.4.refs_4_), channel_id=1, source_target_pairs={{0,16},{16,0},{32,48},{48,32},{64,80},{80,64},{96,112},{112,96},{1... | collective-permute-start | bytes 835592 | tf_op jit(solution)/shard_map/ppermute | solution.py:364
  118.5 55.4 %all-to-all-start.1 = ((s32[16,136,256]{2,1,0:T(8,128)}), s32[16,136,256]{2,1,0:T(8,128)S(1)}, u32[]{:S(2)}, u32[]{:S(2)}) async-start(s32[16,136,256]{2,1,0:T(8,128)} %get-tuple-element.43), calls=%async_computation.1 | async-start | bytes 4456448 | tf_op jit(solution)/shard_map/all_to_all | solution.py:490
  160.4 23.5 %collective-permute-start.8 = (f32[3,256,512]{2,1,0:T(8,128)}, f32[3,256,512]{2,1,0:T(8,128)}, u32[]{:S(2)}, u32[]{:S(2)}) collective-permute-start(f32[3,256,512]{2,1,0:T(8,128)} %constant_dynamic-slice_fusion.9), channel_id=1, source_target_pairs={{0,16},{16,0},{32,48},{48,32},{64,80},{80,64},{96,112},{112,96},{1... | collective-permute-start | bytes 4718600 | tf_op jit(solution)/shard_map/ppermute | solution.py:364
  172.5 18.5 %collective-permute-start.24 = (f32[8,128,128]{2,1,0:T(8,128)}, f32[8,128,128]{2,1,0:T(8,128)}, u32[]{:S(2)}, u32[]{:S(2)}) collective-permute-start(f32[8,128,128]{2,1,0:T(8,128)} %bitcast_dynamic-update-slice_fusion), channel_id=1, source_target_pairs={{0,0},{1,8},{18,16},{19,24},{36,32},{37,40},{54,48},{55,56},{72,64... | collective-permute-start | bytes 1572872 | tf_op jit(solution)/shard_map/ppermute | solution.py:466
  175.3 56.9 %all-to-all-start.2 = ((s32[16,136,256]{2,1,0:T(8,128)}), s32[16,136,256]{2,1,0:T(8,128)}, u32[]{:S(2)}, u32[]{:S(2)}) async-start(s32[16,136,256]{2,1,0:T(8,128)} %get-tuple-element.47), calls=%async_computation.2 | async-start | bytes 4456448 | tf_op jit(solution)/shard_map/all_to_all | solution.py:493
  187.0 11.1 %collective-permute-start.11 = (f32[3,64,512]{2,1,0:T(8,128)S(1)}, f32[3,64,512]{2,1,0:T(8,128)S(1)}, u32[]{:S(2)}, u32[]{:S(2)}) collective-permute-start(f32[3,64,512]{2,1,0:T(8,128)S(1)} %get-tuple-element.67), channel_id=1, source_target_pairs={{0,96},{16,112},{32,0},{48,16},{64,32},{80,48},{96,64},{112,80},{1... | collective-permute-start | bytes 1179656 | tf_op jit(solution)/shard_map/ppermute | solution.py:364
  188.7 12.7 %collective-permute-start.10 = (f32[3,64,512]{2,1,0:T(8,128)S(1)}, f32[3,64,512]{2,1,0:T(8,128)S(1)}, u32[]{:S(2)}, u32[]{:S(2)}) collective-permute-start(f32[3,64,512]{2,1,0:T(8,128)S(1)} %get-tuple-element.68), channel_id=1, source_target_pairs={{0,64},{16,80},{32,96},{48,112},{64,0},{80,16},{96,32},{112,48},{1... | collective-permute-start | bytes 1179656 | tf_op jit(solution)/shard_map/ppermute | solution.py:364
  190.3 19.4 %collective-permute-start.9 = (f32[3,64,512]{2,1,0:T(8,128)S(1)}, f32[3,64,512]{2,1,0:T(8,128)S(1)}, u32[]{:S(2)}, u32[]{:S(2)}) collective-permute-start(f32[3,64,512]{2,1,0:T(8,128)S(1)} %get-tuple-element.66), channel_id=1, source_target_pairs={{0,32},{16,48},{32,64},{48,80},{64,96},{80,112},{96,0},{112,16},{1... | collective-permute-start | bytes 1179656 | tf_op jit(solution)/shard_map/ppermute | solution.py:364
  192.0 29.8 %collective-permute-start.25 = (f32[4,128,128]{2,1,0:T(8,128)S(1)}, f32[4,128,128]{2,1,0:T(8,128)S(1)}, u32[]{:S(2)}, u32[]{:S(2)}) collective-permute-start(f32[4,128,128]{2,1,0:T(8,128)S(1)} %slice.46), channel_id=1, source_target_pairs={{0,4},{8,12},{16,20},{24,28},{32,36},{40,44},{48,52},{56,60},{64,6... | collective-permute-start | bytes 786440 | tf_op jit(solution)/shard_map/ppermute | solution.py:470
  210.9 13.2 %collective-permute-start.14 = (f32[3,16,512]{2,1,0:T(8,128)S(1)}, f32[3,16,512]{2,1,0:T(8,128)S(1)}, u32[]{:S(2)}, u32[]{:S(2)}) collective-permute-start(f32[3,16,512]{2,1,0:T(8,128)S(1)} %get-tuple-element.70), channel_id=1, source_target_pairs={{0,3},{1,0},{2,1},{3,2},{4,7},{5,4},{6,5},{7,6},{8,11},{9,8},{10,9... | collective-permute-start | bytes 294920 | tf_op jit(solution)/shard_map/ppermute | solution.py:364
  213.6 10.6 %collective-permute-start.13 = (f32[3,16,512]{2,1,0:T(8,128)S(1)}, f32[3,16,512]{2,1,0:T(8,128)S(1)}, u32[]{:S(2)}, u32[]{:S(2)}) collective-permute-start(f32[3,16,512]{2,1,0:T(8,128)S(1)} %get-tuple-element.71), channel_id=1, source_target_pairs={{0,2},{1,3},{2,0},{3,1},{4,6},{5,7},{6,4},{7,5},{8,10},{9,11},{10,... | collective-permute-start | bytes 294920 | tf_op jit(solution)/shard_map/ppermute | solution.py:364
  232.2 11.8 %collective-permute-start.20 = (f32[3,16,128]{2,1,0:T(8,128)S(1)}, f32[3,16,128]{2,1,0:T(8,128)S(1)}, u32[]{:S(2)}, u32[]{:S(2)}) collective-permute-start(f32[3,16,128]{2,1,0:T(8,128)S(1)} %add_add_fusion.2), channel_id=1, source_target_pairs={{0,12},{1,13},{2,14},{3,15},{4,0},{5,1},{6,2},{7,3},{8,4},{9,5},{1... | collective-permute-start | bytes 73736 | tf_op jit(solution)/shard_map/ppermute | solution.py:364
  232.4 11.6 %collective-permute-start.19 = (f32[3,16,128]{2,1,0:T(8,128)S(1)}, f32[3,16,128]{2,1,0:T(8,128)S(1)}, u32[]{:S(2)}, u32[]{:S(2)}) collective-permute-start(f32[3,16,128]{2,1,0:T(8,128)S(1)} %add_add_fusion.2), channel_id=1, source_target_pairs={{0,8},{1,9},{2,10},{3,11},{4,12},{5,13},{6,14},{7,15},{8,0},{9,1},... | collective-permute-start | bytes 73736 | tf_op jit(solution)/shard_map/ppermute | solution.py:364
  233.4 10.6 %collective-permute-start.18 = (f32[3,16,128]{2,1,0:T(8,128)S(1)}, f32[3,16,128]{2,1,0:T(8,128)S(1)}, u32[]{:S(2)}, u32[]{:S(2)}) collective-permute-start(f32[3,16,128]{2,1,0:T(8,128)S(1)} %add_add_fusion.2), channel_id=1, source_target_pairs={{0,4},{1,5},{2,6},{3,7},{4,8},{5,9},{6,10},{7,11},{8,12},{9,13},{1... | collective-permute-start | bytes 73736 | tf_op jit(solution)/shard_map/ppermute | solution.py:364
  251.2 15.1 %collective-permute-start.30 = (f32[4,4,3,16,128]{4,3,2,1,0:T(8,128)S(1)}, f32[4,4,3,16,128]{4,3,2,1,0:T(8,128)S(1)}, u32[]{:S(2)}, u32[]{:S(2)}) collective-permute-start(f32[4,4,3,16,128]{4,3,2,1,0:T(8,128)S(1)} %pad_maximum_fusion.1), channel_id=1, source_target_pairs={{0,96},{16,112},{32,0},{48,16},{64,32},{80,48},{96,64},{112,80},{1... | collective-permute-start | bytes 1179656 | tf_op jit(solution)/shard_map/ppermute | solution.py:364
  251.7 14.6 %collective-permute-start.29 = (f32[4,4,3,16,128]{4,3,2,1,0:T(8,128)S(1)}, f32[4,4,3,16,128]{4,3,2,1,0:T(8,128)S(1)}, u32[]{:S(2)}, u32[]{:S(2)}) collective-permute-start(f32[4,4,3,16,128]{4,3,2,1,0:T(8,128)S(1)} %pad_maximum_fusion.1), channel_id=1, source_target_pairs={{0,64},{16,80},{32,96},{48,112},{64,0},{80,16},{96,32},{112,48},{1... | collective-permute-start | bytes 1179656 | tf_op jit(solution)/shard_map/ppermute | solution.py:364
  253.3 18.4 %collective-permute-start.28 = (f32[4,4,3,16,128]{4,3,2,1,0:T(8,128)S(1)}, f32[4,4,3,16,128]{4,3,2,1,0:T(8,128)S(1)}, u32[]{:S(2)}, u32[]{:S(2)}) collective-permute-start(f32[4,4,3,16,128]{4,3,2,1,0:T(8,128)S(1)} %pad_maximum_fusion.1), channel_id=1, source_target_pairs={{0,32},{16,48},{32,64},{48,80},{64,96},{80,112},{96,0},{112,16},{1... | collective-permute-start | bytes 1179656 | tf_op jit(solution)/shard_map/ppermute | solution.py:364
  253.3 22.5 %all-to-all-start.3 = ((f32[128,1,32]{2,1,0:T(1,128)}), f32[128,1,32]{2,1,0:T(1,128)S(1)}, u32[]{:S(2)}, u32[]{:S(2)}) async-start(f32[128,1,32]{2,1,0:T(1,128)} %bitcast.42), calls=%async_computation.3 | async-start | bytes 131072 | tf_op jit(solution)/shard_map/all_to_all | solution.py:510
  (29 other events, 267.6 us)

commit v3 on v2

--- a/solution.py
+++ b/solution.py
@@ -64,68 +64,100 @@
     return unpack(word[:rows]) * scale
 
 
-def share_kernel(at_ref, two_ref, one_ref, inv_two_ref, inv_one_ref, out_ref):
-    for i, (rows, inv) in enumerate(((two_ref, inv_two_ref), (one_ref, inv_one_ref))):
-        keep = at_ref[1 + i].astype(jnp.float32)
-        encode(product(keep * rows[...], inv[...]), out_ref, i)
-
-
-def share(at, panel_two, panel_one, inv_two, inv_one, bw):
+def chosen(row, col):
+    first = lax.rem(2 * row, 4)
+    x, y = lax.rem(col, 4), col // 4
+    here = (x == first) | (x == lax.rem(first + 3, 4))
+    left = (x == first) | (x == first + 1)
+    return jnp.where(here, 0, 8) + 2 * y + jnp.where(left, 0, 1)
+
+
+def share_kernel(at_ref, bits_two_ref, bits_one_ref, two_ref, one_ref, inv_two_ref, inv_one_ref, out_ref):
+    block = 16 * at_ref[0] + chosen(at_ref[0], at_ref[1])
+    skip = bits_one_ref.shape[0] - bits_two_ref.shape[0]
+    keep_two = bits_two_ref[block].astype(jnp.float32)
+    keep_one = bits_one_ref[skip + block].astype(jnp.float32)
+    encode(product(keep_two * two_ref[...], inv_two_ref[...]), out_ref, 0)
+    encode(product(keep_one * one_ref[...], inv_one_ref[...]), out_ref, 1)
+
+
+def share(at, bits_two, bits_one, panel_two, panel_one, inv_two, inv_one, bw):
     width = inv_two.shape[0]
-    rows = pl.BlockSpec((bw, width), lambda i, at: (at[0], 0))
-    whole = pl.BlockSpec((width, width), lambda i, at: (0, 0))
+    rows = pl.BlockSpec((bw, width), lambda i, at, *_: (chosen(at[0], at[1]), 0))
+    whole = pl.BlockSpec((width, width), lambda i, *_: (0, 0))
     return pl.pallas_call(
         share_kernel,
         out_shape=jax.ShapeDtypeStruct((2, bw + 8, width // 2), jnp.int32),
         grid_spec=pltpu.PrefetchScalarGridSpec(
-            num_scalar_prefetch=1,
+            num_scalar_prefetch=3,
             grid=(1,),
             in_specs=[rows, rows, whole, whole],
-            out_specs=pl.BlockSpec((2, bw + 8, width // 2), lambda i, at: (0, 0, 0)),
+            out_specs=pl.BlockSpec((2, bw + 8, width // 2), lambda i, *_: (0, 0, 0)),
         ),
         compiler_params=pltpu.CompilerParams(vmem_limit_bytes=ROOM),
-    )(at, panel_two, panel_one, inv_two, inv_one)
-
-
-def image_kernel(panel, bw, pieces, at_ref, cov_ref, *refs):
-    held, (image_ref, code_ref, head_ref, tail_ref) = refs[:pieces], refs[pieces:]
+        cost_estimate=LIGHT,
+    )(at, bits_two, bits_one, panel_two, panel_one, inv_two, inv_one)
+
+
+def tiles_kernel(at_ref, tile_ref, out_ref):
+    out_ref[0] = tile_ref[...]
+
+
+def tiles_of(at, trail_cov, count, bw):
+    return pl.pallas_call(
+        tiles_kernel,
+        out_shape=jax.ShapeDtypeStruct((count, bw, bw), jnp.float32),
+        grid_spec=pltpu.PrefetchScalarGridSpec(
+            num_scalar_prefetch=1,
+            grid=(count,),
+            in_specs=[pl.BlockSpec((bw, bw), lambda j, at: (lax.rem(at[1], 2) * count + j, j))],
+            out_specs=pl.BlockSpec((1, bw, bw), lambda j, at: (j, 0, 0)),
+        ),
+        cost_estimate=LIGHT,
+    )(at, trail_cov)
+
+
+def image_kernel(bw, pieces, at_ref, cov_ref, *refs):
+    held, (two_ref, one_ref, code_ref, head_ref, tail_ref) = refs[:pieces], refs[pieces:]
+    width = two_ref.shape[1]
 
     @pl.when(pl.program_id(0) == 0)
     def _():
+        z, core = at_ref[0] // 2, lax.rem(at_ref[0], 2)
         for i, ref in enumerate(held):
-            head, tail = split(decode(ref[panel]))
-            rows = pl.ds(pl.multiple_of(at_ref[i] * bw, bw), bw)
-            head_ref[rows, :] = head
-            tail_ref[rows, :] = tail
+            block = lax.rem(z + 4 - i // 2, 4) * 2 + lax.rem(core + i, 2)
+            rows = pl.ds(pl.multiple_of(block * bw, bw), bw)
+            for panel in range(2):
+                head, tail = split(decode(ref[panel]))
+                head_ref[rows, panel * width : (panel + 1) * width] = head
+                tail_ref[rows, panel * width : (panel + 1) * width] = tail
 
     cov_head, cov_tail = split(cov_ref[...])
-    image = dot(cov_head, head_ref[...]) + (
-        dot(cov_head, tail_ref[...]) + dot(cov_tail, head_ref[...])
-    )
-    image_ref[...] = image
-    for i in range(image.shape[0] // bw):
-        encode(image[i * bw : (i + 1) * bw], code_ref, i)
-
-
-def image(at, trail_cov, held, panel, bw, tile=512):
+    for panel, image_ref in enumerate((two_ref, one_ref)):
+        at = slice(panel * width, (panel + 1) * width)
+        image = dot(cov_head, head_ref[:, at]) + (
+            dot(cov_head, tail_ref[:, at]) + dot(cov_tail, head_ref[:, at])
+        )
+        image_ref[...] = image
+        for i in range(image.shape[0] // bw):
+            encode(image[i * bw : (i + 1) * bw], code_ref, i, panel)
+
+
+def image(at, trail_cov, held, bw, tile=512):
     rows, span = trail_cov.shape
     width = 2 * held[0].shape[-1]
     every = pl.BlockSpec(held[0].shape, lambda i, at: (0, 0, 0))
     return pl.pallas_call(
-        functools.partial(image_kernel, panel, bw, len(held)),
-        out_shape=[
-            jax.ShapeDtypeStruct((rows, width), jnp.float32),
-            jax.ShapeDtypeStruct((rows // bw, bw + 8, width // 2), jnp.int32),
-        ],
+        functools.partial(image_kernel, bw, len(held)),
+        out_shape=[jax.ShapeDtypeStruct((rows, width), jnp.float32)] * 2
+        + [jax.ShapeDtypeStruct((rows // bw, 2, bw + 8, width // 2), jnp.int32)],
         grid_spec=pltpu.PrefetchScalarGridSpec(
             num_scalar_prefetch=1,
             grid=(rows // tile,),
             in_specs=[pl.BlockSpec((tile, span), lambda i, at: (i, 0))] + [every] * len(held),
-            out_specs=[
-                pl.BlockSpec((tile, width), lambda i, at: (i, 0)),
-                pl.BlockSpec((tile // bw, bw + 8, width // 2), lambda i, at: (i, 0, 0)),
-            ],
-            scratch_shapes=[pltpu.VMEM((span, width), jnp.bfloat16)] * 2,
+            out_specs=[pl.BlockSpec((tile, width), lambda i, at: (i, 0))] * 2
+            + [pl.BlockSpec((tile // bw, 2, bw + 8, width // 2), lambda i, at: (i, 0, 0, 0))],
+            scratch_shapes=[pltpu.VMEM((span, 2 * width), jnp.bfloat16)] * 2,
         ),
         compiler_params=pltpu.CompilerParams(vmem_limit_bytes=ROOM),
         cost_estimate=LIGHT,
@@ -133,7 +165,7 @@
 
 
 def sums_kernel(
-    bw, bits_two_ref, bits_one_ref, two_ref, one_ref, image_two_ref, image_one_ref,
+    bw, at_ref, bits_two_ref, bits_one_ref, two_ref, one_ref, image_two_ref, image_one_ref,
     inv_two_ref, inv_one_ref, out_ref,
 ):
     step = pl.program_id(0)
@@ -143,16 +175,18 @@
         out_ref[...] = jnp.zeros_like(out_ref)
 
     count = two_ref.shape[0] // bw
-
-    def masked(ref, bits_ref):
+    first = 16 * at_ref[0] + step * count
+    skip = bits_one_ref.shape[0] - bits_two_ref.shape[0]
+
+    def masked(ref, bits_ref, base):
         keep = [
-            jnp.full((bw, 1), bits_ref[step * count + i].astype(jnp.float32)) for i in range(count)
+            jnp.full((bw, 1), bits_ref[base + i].astype(jnp.float32)) for i in range(count)
         ]
         keep = jnp.concatenate(keep, axis=0)
         return ref[...] * keep, keep
 
-    two, keep_two = masked(two_ref, bits_two_ref)
-    one, _ = masked(one_ref, bits_one_ref)
+    two, keep_two = masked(two_ref, bits_two_ref, first)
+    one, _ = masked(one_ref, bits_one_ref, skip + first)
     image_two = split(image_two_ref[...] * keep_two)
     image_one = split(image_one_ref[...])
     two, one = split(two), split(one)
@@ -165,7 +199,7 @@
             out_ref[i] = product(inv[...], out_ref[i], tdot)
 
 
-def sums(bits_two, bits_one, panel_two, panel_one, image_two, image_one, inv_two, inv_one, bw, tile=512):
+def sums(at, bits_two, bits_one, panel_two, panel_one, image_two, image_one, inv_two, inv_one, bw, tile=512):
     rows, width = panel_two.shape
     part = pl.BlockSpec((tile, width), lambda i, *_: (i, 0))
     whole = pl.BlockSpec((width, width), lambda i, *_: (0, 0))
@@ -173,59 +207,66 @@
         functools.partial(sums_kernel, bw),
         out_shape=jax.ShapeDtypeStruct((3, width, width), jnp.float32),
         grid_spec=pltpu.PrefetchScalarGridSpec(
-            num_scalar_prefetch=2,
+            num_scalar_prefetch=3,
             grid=(rows // tile,),
             in_specs=[part] * 4 + [whole] * 2,
             out_specs=pl.BlockSpec((3, width, width), lambda i, *_: (0, 0, 0)),
         ),
         compiler_params=pltpu.CompilerParams(vmem_limit_bytes=ROOM),
         cost_estimate=LIGHT,
-    )(bits_two, bits_one, panel_two, panel_one, image_two, image_one, inv_two, inv_one)
-
-
-def rows_kernel(at_ref, two_ref, one_ref, top_ref, cov_two_ref, cov_one_ref, cross_ref):
-    count = two_ref.shape[0]
-
-    def total(ref):
-        value = decode(ref[0])
+    )(at, bits_two, bits_one, panel_two, panel_one, image_two, image_one, inv_two, inv_one)
+
+
+def rows_kernel(at_ref, bits_two_ref, bits_one_ref, panel_ref, code_ref, top_ref, cov_two_ref, cov_one_ref, cross_ref):
+    count = code_ref.shape[0]
+    block = 16 * at_ref[0] + at_ref[1]
+    skip = bits_one_ref.shape[0] - bits_two_ref.shape[0]
+    keep_two = bits_two_ref[block].astype(jnp.float32)
+    keep_one = bits_one_ref[skip + block].astype(jnp.float32)
+
+    def total(panel):
+        value = decode(code_ref[0, panel])
         for i in range(1, count):
-            value = value + decode(ref[i])
+            value = value + decode(code_ref[i, panel])
         return value
 
-    cov_two = -at_ref[0].astype(jnp.float32) * total(two_ref)
+    cov_two = -keep_two * total(0)
     cov_two_ref[...] = cov_two
-    cov_one = -at_ref[1].astype(jnp.float32) * (product(cov_two, top_ref[...]) + total(one_ref))
+    cov_one = -keep_one * (product(cov_two, top_ref[...]) + total(1))
     cov_one_ref[...] = cov_one
     bw = cross_ref.shape[1]
-    cross_ref[...] = cov_one_ref[:, pl.ds(pl.multiple_of(at_ref[2] * bw, bw), bw)]
-
-
-def rows(at, part_two, part_one, norm_top, bw):
+    cross_ref[...] = cov_one_ref[:, pl.ds(pl.multiple_of(panel_ref[block] * bw, bw), bw)]
+
+
+def rows(at, bits_two, bits_one, panel, code, norm_top, bw):
     width = norm_top.shape[0]
     smem = pl.BlockSpec(memory_space=pltpu.SMEM)
     vmem = pl.BlockSpec(memory_space=pltpu.VMEM)
     return pl.pallas_call(
         rows_kernel,
         out_shape=[jax.ShapeDtypeStruct((bw, n), jnp.float32) for n in (width, width, bw)],
-        in_specs=[smem, vmem, vmem, vmem],
+        in_specs=[smem] * 4 + [vmem] * 2,
         out_specs=[vmem] * 3,
         compiler_params=pltpu.CompilerParams(vmem_limit_bytes=ROOM),
-    )(at, part_two, part_one, norm_top)
+        cost_estimate=LIGHT,
+    )(at, bits_two, bits_one, panel, code, norm_top)
 
 
 def small_kernel(at_ref, own_ref, other_ref, gram_ref, top_ref, keep_ref, two_ref, top_cov_ref, one_ref, sums_ref):
     y_count, lanes = own_ref.shape[2], own_ref.shape[-1]
     tall = own_ref.shape[-2]
 
+    own_z, own_core = at_ref[0] // 2, lax.rem(at_ref[0], 2)
+    own_x, own_y = lax.rem(at_ref[1], 4), at_ref[1] // 4
     for flip, ref in enumerate((own_ref, other_ref)):
-        half = lax.rem(at_ref[3] + flip, 2)
+        half = lax.rem(own_core + flip, 2)
         for dz in range(4):
-            z = lax.rem(at_ref[2] + 4 - dz, 4)
+            z = lax.rem(own_z + 4 - dz, 4)
             for dx in range(4):
-                x = lax.rem(at_ref[0] + 4 - dx, 4)
+                x = lax.rem(own_x + 4 - dx, 4)
                 row = ((half * 4 + z) * 4 + x) * tall
                 for dy in range(y_count):
-                    y = lax.rem(at_ref[1] + 4 - dy, 4)
+                    y = lax.rem(own_y + 4 - dy, 4)
                     sums_ref[
                         :,
                         pl.ds(pl.multiple_of(row, tall), tall),
@@ -257,6 +298,7 @@
         out_specs=[vmem] * 3,
         scratch_shapes=[pltpu.VMEM((3, width, width), jnp.float32)],
         compiler_params=pltpu.CompilerParams(vmem_limit_bytes=ROOM),
+        cost_estimate=LIGHT,
     )(at, own, other, gram, norm_top, bits_top)
 
 
@@ -286,6 +328,7 @@
         in_specs=[smem, vmem, vmem, vmem],
         out_specs=[vmem] * 2,
         compiler_params=pltpu.CompilerParams(vmem_limit_bytes=ROOM),
+        cost_estimate=LIGHT,
     )(bits_top, panel_top, inv_two, inv_one)
 
 
@@ -318,6 +361,7 @@
         in_specs=[pl.BlockSpec((step, 2 * bw), lambda i: (i, 0)), whole, whole],
         out_specs=pl.BlockSpec((8, step), lambda i: (0, i)),
         compiler_params=pltpu.CompilerParams(vmem_limit_bytes=ROOM),
+        cost_estimate=LIGHT,
     )(units, tile, cross)
 
 
@@ -346,6 +390,7 @@
         ],
         out_specs=pl.BlockSpec((8, step), lambda i: (0, i)),
         compiler_params=pltpu.CompilerParams(vmem_limit_bytes=ROOM),
+        cost_estimate=LIGHT,
     )(units, panel, diag)
 
 
@@ -380,19 +425,15 @@
         return jnp.stack([value] + [self.move(value, step) for step in range(1, self.count)])
 
 
-def spread_plan(row_count, col_count):
-    plan = []
+def spread_pairs(row_count, col_count):
+    pairs = []
     for r in range(row_count):
-        z = r // 2
-        first = col_count // row_count * r
         for c in range(col_count):
-            x, y = c % 4, c // 4
-            x_first = first % 4
-            side = 0 if x in (x_first, (x_first - 1) % 4) else 1
-            half = 0 if x in (x_first, (x_first + 1) % 4) else 1
-            j = y % 4 * 2 + half
-            plan.append((side * row_count + j, j * col_count + first + side))
-    return plan
+            first, x, y = 2 * r % 4, c % 4, c // 4
+            side = 0 if x in (first, (first + 3) % 4) else 1
+            j = 2 * y + (0 if x in (first, first + 1) else 1)
+            pairs.append((r * col_count + c, j * col_count + 2 * r + side))
+    return pairs
 
 
 def local(
@@ -420,44 +461,27 @@
     width = diag_inv_two.shape[0]
     bw = loadings.shape[1] // 2
     top_blocks = width // bw
-    owner = row_index * col_count + col_index
     core = Ring("row", row_count, 1, 2)
     ring_z = Ring("row", row_count, 2)
     ring_x = Ring("col", col_count, 1)
     ring_y = Ring("col", col_count, 4)
 
-    bits_two = lax.dynamic_slice_in_dim(pattern_two, row_index * col_count, col_count)
+    at = jnp.stack([row_index, col_index]).astype(jnp.int32)
     bits_top = pattern_one[:top_blocks]
-    bits_one = lax.dynamic_slice_in_dim(
-        pattern_one, top_blocks + row_index * col_count, col_count
-    )
-    own_two = lax.dynamic_index_in_dim(bits_two, col_index, 0, False)
-    own_one = lax.dynamic_index_in_dim(bits_one, col_index, 0, False)
-
-    spread = spread_plan(row_count, col_count)
-    chosen = jnp.array([block for block, _ in spread], jnp.int32)[owner]
+
     part = share(
-        jnp.stack([chosen, bits_two[chosen], bits_one[chosen]]),
-        panel_two_rows, panel_one_rows, diag_inv_two, diag_inv_one, bw,
-    )
-    blocks, side = unit_block[:, 0], col_index % ratio
-    part, blocks, side = lax.optimization_barrier((part, blocks, side))
-    part = lax.ppermute(part, BOTH, [(i, j) for i, (_, j) in enumerate(spread)])
-    held, places = [], []
+        at, pattern_two, pattern_one, panel_two_rows, panel_one_rows, diag_inv_two, diag_inv_one, bw
+    )
+    blocks = unit_block[:, 0]
+    part, blocks = lax.optimization_barrier((part, blocks))
+    part = lax.ppermute(part, BOTH, spread_pairs(row_count, col_count))
+    held = []
     for step in range(4):
         piece = ring_z.move(part, step) if step else part
-        at = (ring_z.place() - step) % 4 * 2
         held += [piece, core.move(piece, 1)]
-        places += [at + core.place(), at + 1 - core.place()]
-    places = jnp.stack(places)
-
-    tiles = jnp.stack(
-        [
-            lax.dynamic_slice(trail_cov, ((side * row_count + j) * bw, j * bw), (bw, bw))
-            for j in range(row_count)
-        ]
-    )
-    at = col_index % row_count
+
+    tiles = tiles_of(at, trail_cov, row_count, bw)
+    turn = col_index % row_count
     pairs = [
         (r * col_count + ratio * r + h, r * col_count + h * row_count)
         for r in range(row_count)
@@ -468,7 +492,7 @@
     while half:
         pairs = [(c, c + half) for c in range(0, col_count, 2 * half)]
         handed = lax.ppermute(tiles[half:], "col", pairs)
-        tiles = jnp.where(at // half % 2 == 1, handed, tiles[:half])
+        tiles = jnp.where(turn // half % 2 == 1, handed, tiles[:half])
         half //= 2
     tile = tiles[0]
 
@@ -478,49 +502,47 @@
     slot = blocks * capacity + rank
     packed = jnp.zeros((total_count * capacity, 2 * bw), jnp.bfloat16).at[slot].set(loadings)
     packed = packed.reshape(total_count, capacity, 2 * bw)
-    packed, held[2] = lax.optimization_barrier((packed, held[2]))
+    packed, held[2], held[4], held[6] = lax.optimization_barrier((packed, held[2], held[4], held[6]))
     units = lax.all_to_all(packed, BOTH, split_axis=0, concat_axis=0, tiled=True)
     units = units.reshape(total_count * capacity, 2 * bw)
 
+    image_two, image_one, code = image(at, trail_cov, held, bw)
+    code, units = lax.optimization_barrier((code, units))
+    code = lax.all_to_all(code, "col", split_axis=0, concat_axis=0, tiled=True)
+
+    total = sums(
+        at, pattern_two, pattern_one, panel_two_rows, panel_one_rows, image_two, image_one,
+        diag_inv_two, diag_inv_one, bw,
+    )
+    bits_top, total = lax.optimization_barrier((bits_top, total))
     gram, norm_top = early(bits_top, panel_one_top, diag_inv_two, diag_inv_one)
-    places, norm_top = lax.optimization_barrier((places, norm_top))
-
-    image_two, code_two = image(places, trail_cov, held, 0, bw)
-    code_two, units = lax.optimization_barrier((code_two, units))
-    code_two = lax.all_to_all(code_two, "col", split_axis=0, concat_axis=0, tiled=True)
-    image_one, code_one = image(places, trail_cov, held, 1, bw)
-    code_one, code_two = lax.optimization_barrier((code_one, code_two))
-    code_one = lax.all_to_all(code_one, "col", split_axis=0, concat_axis=0, tiled=True)
-
-    total = sums(
-        bits_two, bits_one, panel_two_rows, panel_one_rows, image_two, image_one,
-        diag_inv_two, diag_inv_one, bw,
-    )
     total = core.scatter_sum(total, 1)
     total = ring_z.scatter_sum(total, 1)
+    total, norm_top = lax.optimization_barrier((total, norm_top))
     total = ring_x.scatter_sum(total, 1)
     total = ring_y.scatter_sum(total, 2)
-    total, code_one = lax.optimization_barrier((total, code_one))
-    total = ring_x.gather(ring_y.gather(total))
+    total, tile = lax.optimization_barrier((total, tile))
+    total = ring_y.gather(total)
+    total = ring_x.gather(total)
+    total, code = lax.optimization_barrier((total, code))
+    total = ring_z.gather(total)
     cov_two, cov_one, cross = rows(
-        jnp.stack([own_two, own_one, block_panel[owner]]), code_two, code_one, norm_top, bw
+        at, pattern_two, pattern_one, block_panel, code, norm_top, bw
     )
     value = forms(units, tile, cross)[0].reshape(total_count, capacity)
-    total, value = lax.optimization_barrier((total, value))
     returned = lax.all_to_all(value, BOTH, split_axis=0, concat_axis=0, tiled=True)
-    total = ring_z.gather(total)
-    total, returned = lax.optimization_barrier((total, returned))
     other = core.move(total, 1)
-    spots = jnp.stack([ring_x.place(), ring_y.place(), ring_z.place(), core.place()])
-    diag_two, top_cov, diag_one = small(spots, total, other, gram, norm_top, bits_top)
+    diag_two, top_cov, diag_one = small(at, total, other, gram, norm_top, bits_top)
+    own_panel = jnp.sum(hits * block_panel[None, :], axis=1, keepdims=True)
+    within = inner(loadings, own_panel, diag_one)[0]
+    within, returned = lax.optimization_barrier((within, returned))
     picked = jnp.dot(
         hits.astype(jnp.float32), returned, precision=lax.Precision.HIGHEST,
         preferred_element_type=jnp.float32,
     )
     at_rank = rank[:, None] == jnp.arange(capacity, dtype=jnp.int32)[None, :]
     variance = jnp.sum(jnp.where(at_rank, picked, 0.0), axis=1)
-    own_panel = jnp.sum(hits * block_panel[None, :], axis=1, keepdims=True)
-    variance = variance + inner(loadings, own_panel, diag_one)[0]
+    variance = variance + within
 
     mean = exposure * jnp.exp(0.5 * variance)
     seen = counts.astype(jnp.float32)

time: 295 us -> 283 us (0.959)
  waiting for transfers between devices: 71.1 us -> 102 us
  local copies, waits for them, and re-layouts: 43.7 us -> 23.7 us
  starting transfers between devices: 87.2 us -> 70.5 us
  other arithmetic: 12.1 us -> 7.63 us
    ppermute x1, waiting for transfers between devices: 0.01 us -> 65.5 us  [local(): tiles = lax.ppermute(tiles, BOTH, pairs)]
    ppermute x27, waiting for transfers between devices: 56 us -> 32.1 us  [move(): return lax.ppermute(value, self.axis, pairs)]
    unnamed x41 -> x32, local copies, waits for them, and re-layouts: 15.3 us -> 3.74 us
    all_to_all x1, starting transfers between devices: 13 us -> 4.21 us  [local(): lax.all_to_all(value, BOTH, split_axis=0, concat_axis=0, tiled=True)]
    all_to_all x2 -> x1, starting transfers between devices: 14.4 us -> 6.03 us  [local(): code = lax.all_to_all(code, 'col', split_axis=0, concat_axis=0, tiled=True)]
    ppermute x3, waiting for transfers between devices: 7.09 us -> 0.01 us  [local(): handed = lax.ppermute(tiles[half:], 'col', pairs)]
    dynamic_slice x6 -> x0, local copies, waits for them, and re-layouts: 6.32 us -> none  [the longest x1 1.34 us: local(): bits_one[chosen]]
    all_to_all x1, starting transfers between devices: 16.6 us -> 10.6 us  [local(): lax.all_to_all(packed, BOTH, split_axis=0, concat_axis=0, tiled=True)]
  transfers between devices with their start and end apart: 36 -> 35, of which waited for: 12 -> 20; matrix products, arithmetic and copies ran while one was open for 14% -> 9% of each run, Pallas kernels for 20% -> 26%
where the time goes in v3:
time: 283 us; the launch traced here: 282 us
  waiting for transfers between devices  102 us (36%)
  Pallas kernels  75.8 us (27%)
  starting transfers between devices  70.5 us (25%)
  local copies, waits for them, and re-layouts  23.7 us (8%)
  other arithmetic  7.63 us (3%)
    ppermute x1, waiting for transfers between devices, local(): tiles = lax.ppermute(tiles, BOTH, pairs)  65.5 us
    ppermute x27, starting transfers between devices, move(): return lax.ppermute(value, self.axis, pairs)  36.5 us
    ppermute x27, waiting for transfers between devices, move(): return lax.ppermute(value, self.axis, pairs)  32.1 us
    pallas_call x1, Pallas kernels, image(): pl.pallas_call(functools.partial(image_kernel, bw, len(held)), out_shape=...  19.9 us
    pallas_call x1, Pallas kernels, sums(): pl.pallas_call(functools.partial(sums_kernel, bw), out_shape=jax.ShapeDty...  19.9 us
    scatter x1, local copies, waits for them, and re-layouts, local(): jnp.zeros((total_count * capacity, 2 * bw), jnp.bfloat16).at[slot]  11.3 us
    all_to_all x1, starting transfers between devices, local(): lax.all_to_all(packed, BOTH, split_axis=0, concat_axis=0, tiled=True)  10.6 us
    ppermute x3, starting transfers between devices, local(): handed = lax.ppermute(tiles[half:], 'col', pairs)  6.71 us
  transfers between devices with their start and end apart: 35, of which 20 were waited for; matrix products, arithmetic and copies ran while one was open for 9% of the time, Pallas kernels for 26%

profile of v3, /device:TPU:1, one launch (start us, length us, event | category | flops | bytes accessed | tf_op | source)
XLA Modules:
  0.0 281.8 jit_solution(10833663419875608313)
XLA Ops:
  1.2 4.0 %shard_map.181 = s32[2,136,256]{2,1,0:T(8,128)} custom-call(s32[2]{0:T(128)} %pad_add_fusion.at_ref, s32[128]{0:T(128)} %bits_two_ref.5, s32[132]{0:T(256)} %bits_one_ref.5, f32[2048,512]{1,0:T(8,128)} %two_ref.3, f32[2048,512]{1,0:T(8,128)} %one_ref.3, f32[512,512]{1,0:T(8,128)} %inv_two_ref.5, f32[512,512]{1,0:T(8,128)} %inv_one_ref.5), custom_call_target="tpu_custom_call" | custom-call | flops 1 | bytes 1 | tf_op jit(solution)/shard_map/pallas_call | solution.py:88
  5.2 5.2 %collective-permute-start = (s32[2,136,256]{2,1,0:T(8,128)}, s32[2,136,256]{2,1,0:T(8,128)S(1)}, u32[]{:S(2)}, u32[]{:S(2)}) collective-permute-start(s32[2,136,256]{2,1,0:T(8,128)} %shard_map.181), channel_id=1, source_target_pairs={{0,0},{1,1},{2,17},{3,16},{4,32},{5,33},{6,49},{7,48},{8,64},{9,65... | collective-permute-start | bytes 835592 | tf_op jit(solution)/shard_map/ppermute | solution.py:477
  11.4 4.0 %collective-permute-done.refs_0_ = s32[2,136,256]{2,1,0:T(8,128)S(1)} collective-permute-done((s32[2,136,256]{2,1,0:T(8,128)}, s32[2,136,256]{2,1,0:T(8,128)S(1)}, u32[]{:S(2)}, u32[]{:S(2)}) %collective-permute-start) | collective-permute-done | bytes 278560 | tf_op jit(solution)/shard_map/ppermute | solution.py:477
  15.4 4.6 %collective-permute-start.2 = (s32[2,136,256]{2,1,0:T(8,128)S(1)}, s32[2,136,256]{2,1,0:T(8,128)S(1)}, u32[]{:S(2)}, u32[]{:S(2)}) collective-permute-start(s32[2,136,256]{2,1,0:T(8,128)S(1)} %collective-permute-done.refs_0_), channel_id=1, source_target_pairs={{0,32},{16,48},{32,64},{48,80},{64,96},{80,112},{96,0},{112,16},{1... | collective-permute-start | bytes 835592 | tf_op jit(solution)/shard_map/ppermute | solution.py:409
  20.0 7.3 %collective-permute-start.3 = (s32[2,136,256]{2,1,0:T(8,128)S(1)}, s32[2,136,256]{2,1,0:T(8,128)S(1)}, u32[]{:S(2)}, u32[]{:S(2)}) collective-permute-start(s32[2,136,256]{2,1,0:T(8,128)S(1)} %collective-permute-done.refs_0_), channel_id=1, source_target_pairs={{0,64},{16,80},{32,96},{48,112},{64,0},{80,16},{96,32},{112,48},{1... | collective-permute-start | bytes 835592 | tf_op jit(solution)/shard_map/ppermute | solution.py:409
  30.1 11.3 %scatter_custom_fusion = bf16[4096,256]{1,0:T(8,128)(2,1)} fusion(s32[2048]{0:T(1024)S(1)} %get-tuple-element.78, bf16[2048,256]{1,0:T(8,128)(2,1)} %units_ref.1, bf16[]{:T(256)} %constant.252.clone.1), kind=kCustom, calls=%fused_computation.14 | custom fusion | bytes 2097664 | tf_op jit(solution)/shard_map/scatter | solution.py:503
  41.4 10.6 %all-to-all-start = ((bf16[128,32,256]{2,1,0:T(8,128)(2,1)}), bf16[128,32,256]{2,1,0:T(8,128)(2,1)S(1)}, u32[]{:S(2)}, u32[]{:S(2)}) async-start(bf16[128,32,256]{2,1,0:T(8,128)(2,1)} %bitcast.35), calls=%async_computation | async-start | bytes 4194304 | tf_op jit(solution)/shard_map/all_to_all | solution.py:506
  55.7 19.9 %shard_map.182 = (f32[2048,512]{1,0:T(8,128)}, f32[2048,512]{1,0:T(8,128)}, s32[16,2,136,256]{3,2,1,0:T(8,128)}) custom-call(s32[2]{0:T(128)} %pad_add_fusion.at_ref, f32[2048,1024]{1,0:T(8,128)} %tile_ref.1, s32[2,136,256]{2,1,0:T(8,128)} %copy-done.5, s32[2,136,256]{2,1,0:T(8,128)} %copy-done.9, s32[2,136,256]{2,1,0:T(8,128)} %copy-done.6, ...), custom_call_target="tpu_custom_call" | custom-call | flops 1 | bytes 1 | tf_op jit(solution)/shard_map/pallas_call | solution.py:150
  75.6 19.9 %shard_map.183 = f32[3,512,512]{2,1,0:T(8,128)} custom-call(s32[2]{0:T(128)} %pad_add_fusion.at_ref, s32[128]{0:T(128)} %bits_two_ref.5, s32[132]{0:T(256)} %bits_one_ref.5, f32[2048,512]{1,0:T(8,128)} %two_ref.3, f32[2048,512]{1,0:T(8,128)} %one_ref.3, f32[2048,512]{1,0:T(8,128)} %get-tuple-element.40.image_two_ref, ...), custom_call_target="tpu_custom_call" | custom-call | flops 1 | bytes 1 | tf_op jit(solution)/shard_map/pallas_call | solution.py:206
  99.9 6.0 %all-to-all-start.1 = ((s32[16,2,136,256]{3,2,1,0:T(8,128)}), s32[16,2,136,256]{3,2,1,0:T(8,128)}, u32[]{:S(2)}, u32[]{:S(2)}) async-start(s32[16,2,136,256]{3,2,1,0:T(8,128)} %get-tuple-element.49), calls=%async_computation.1 | async-start | bytes 8912896 | tf_op jit(solution)/shard_map/all_to_all | solution.py:511
  105.9 5.7 %shard_map.185 = f32[8,128,128]{2,1,0:T(8,128)} custom-call(s32[2]{0:T(128)} %pad_add_fusion.at_ref, f32[2048,1024]{1,0:T(8,128)} %tile_ref.1), custom_call_target="tpu_custom_call" | custom-call | flops 1 | bytes 1 | tf_op jit(solution)/shard_map/pallas_call | solution.py:107
  113.0 65.5 %collective-permute-done.18 = f32[8,128,128]{2,1,0:T(8,128)} collective-permute-done((f32[8,128,128]{2,1,0:T(8,128)}, f32[8,128,128]{2,1,0:T(8,128)}, u32[]{:S(2)}, u32[]{:S(2)}) %collective-permute-start.18) | collective-permute-done | bytes 524320 | tf_op jit(solution)/shard_map/ppermute | solution.py:490
  184.5 3.9 %collective-permute-start.11 = (f32[3,64,512]{2,1,0:T(8,128)S(1)}, f32[3,64,512]{2,1,0:T(8,128)S(1)}, u32[]{:S(2)}, u32[]{:S(2)}) collective-permute-start(f32[3,64,512]{2,1,0:T(8,128)S(1)} %get-tuple-element.67), channel_id=1, source_target_pairs={{0,96},{16,112},{32,0},{48,16},{64,32},{80,48},{96,64},{112,80},{1... | collective-permute-start | bytes 1179656 | tf_op jit(solution)/shard_map/ppermute | solution.py:409
  193.4 6.0 %shard_map.184 = (f32[2,512,512]{2,1,0:T(8,128)}, f32[512,512]{1,0:T(8,128)}) custom-call(s32[4]{0:T(128)} %slice.33.keep_ref, f32[512,512]{1,0:T(8,128)} %top_rows_ref.1, f32[512,512]{1,0:T(8,128)} %inv_two_ref.5, f32[512,512]{1,0:T(8,128)} %inv_one_ref.5), custom_call_target="tpu_custom_call" | custom-call | flops 1 | bytes 1 | tf_op jit(solution)/shard_map/pallas_call | solution.py:322
  203.5 3.2 %collective-permute-start.21 = (f32[1,128,128]{2,1,0:T(8,128)S(1)}, f32[1,128,128]{2,1,0:T(8,128)S(1)}, u32[]{:S(2)}, u32[]{:S(2)}) collective-permute-start(f32[1,128,128]{2,1,0:T(8,128)S(1)} %slice.50), channel_id=1, source_target_pairs={{0,1},{2,3},{4,5},{6,7},{8,9},{10,11},{12,13},{14,15},{16,17},{18,... | collective-permute-start | bytes 196616 | tf_op jit(solution)/shard_map/ppermute | solution.py:494
  216.4 3.1 %collective-permute-done.23 = f32[3,16,128]{2,1,0:T(8,128)S(1)} collective-permute-done((f32[3,16,128]{2,1,0:T(8,128)S(1)}, f32[3,16,128]{2,1,0:T(8,128)S(1)}, u32[]{:S(2)}, u32[]{:S(2)}) %collective-permute-start.23) | collective-permute-done | bytes 24608 | tf_op jit(solution)/shard_map/ppermute | solution.py:409
  229.7 4.9 %collective-permute-done.30 = f32[4,4,3,16,128]{4,3,2,1,0:T(8,128)S(1)} collective-permute-done((f32[4,4,3,16,128]{4,3,2,1,0:T(8,128)S(1)}, f32[4,4,3,16,128]{4,3,2,1,0:T(8,128)S(1)}, u32[]{:S(2)}, u32[]{:S(2)}) %collective-permute-start.30) | collective-permute-done | bytes 393248 | tf_op jit(solution)/shard_map/ppermute | solution.py:409
  236.6 8.9 %collective-permute-done.28 = f32[4,4,3,16,128]{4,3,2,1,0:T(8,128)S(1)} collective-permute-done((f32[4,4,3,16,128]{4,3,2,1,0:T(8,128)S(1)}, f32[4,4,3,16,128]{4,3,2,1,0:T(8,128)S(1)}, u32[]{:S(2)}, u32[]{:S(2)}) %collective-permute-start.28) | collective-permute-done | bytes 393248 | tf_op jit(solution)/shard_map/ppermute | solution.py:409
  245.6 4.4 %collective-permute-start.31 = (f32[4,4,4,3,16,128]{5,4,3,2,1,0:T(8,128)S(1)}, f32[4,4,4,3,16,128]{5,4,3,2,1,0:T(8,128)S(1)}, u32[]{:S(2)}, u32[]{:S(2)}) collective-permute-start(f32[4,4,4,3,16,128]{5,4,3,2,1,0:T(8,128)S(1)} %pad_maximum_fusion.own_ref), channel_id=1, source_target_pairs={{0,16},{16,0},{32,48},{48,32},{64,80},{80,64},{96,112},{112,96},{1... | collective-permute-start | bytes 4718600 | tf_op jit(solution)/shard_map/ppermute | solution.py:409
  250.0 5.0 %shard_map.186 = (f32[128,512]{1,0:T(8,128)}, f32[128,512]{1,0:T(8,128)}, f32[128,128]{1,0:T(8,128)}) custom-call(s32[2]{0:T(128)} %pad_add_fusion.at_ref, s32[128]{0:T(128)} %bits_two_ref.5, s32[132]{0:T(256)} %bits_one_ref.5, s32[128]{0:T(128)} %panel_ref.1, s32[16,2,136,256]{3,2,1,0:T(8,128)} %all-to-all-done.1.code_ref, f32[512,512]{1,0:T(8,128)} %get-tuple-element.51.top_ref), custom_call_target="tpu_custom_call" | custom-call | flops 1 | bytes 1 | tf_op jit(solution)/shard_map/pallas_call | solution.py:245
  255.1 4.6 %shard_map.189 = f32[8,4096]{1,0:T(8,128)} custom-call(bf16[4096,256]{1,0:T(8,128)(2,1)} %bitcast.34, f32[128,128]{1,0:T(8,128)} %fusion.10.tile_ref, f32[128,128]{1,0:T(8,128)} %get-tuple-element.61.cross_ref), custom_call_target="tpu_custom_call" | custom-call | flops 1 | bytes 1 | tf_op jit(solution)/shard_map/pallas_call | solution.py:357
  261.3 4.2 %all-to-all-start.2 = ((f32[128,1,32]{2,1,0:T(1,128)}), f32[128,1,32]{2,1,0:T(1,128)S(1)}, u32[]{:S(2)}, u32[]{:S(2)}) async-start(f32[128,1,32]{2,1,0:T(1,128)} %bitcast.24), calls=%async_computation.2 | async-start | bytes 131072 | tf_op jit(solution)/shard_map/all_to_all | solution.py:533
  268.1 6.7 %shard_map.187 = (f32[512,512]{1,0:T(8,128)}, f32[512,512]{1,0:T(8,128)}, f32[512,512]{1,0:T(8,128)}) custom-call(s32[2]{0:T(128)} %pad_add_fusion.at_ref, f32[4,4,4,3,16,128]{5,4,3,2,1,0:T(8,128)} %copy-done.3, f32[4,4,4,3,16,128]{5,4,3,2,1,0:T(8,128)} %copy-done.4, f32[2,512,512]{2,1,0:T(8,128)} %get-tuple-element.54.gram_ref, ...), custom_call_target="tpu_custom_call" | custom-call | flops 1 | bytes 1 | tf_op jit(solution)/shard_map/pallas_call | solution.py:294
  274.8 4.0 %shard_map.188 = f32[8,2048]{1,0:T(8,128)} custom-call(bf16[2048,256]{1,0:T(8,128)(2,1)} %units_ref.1, s32[2048,1]{1,0:T(8,128)} %copy.25.panel_ref, f32[512,512]{1,0:T(8,128)} %get-tuple-element.33.diag_ref), custom_call_target="tpu_custom_call" | custom-call | flops 1 | bytes 1 | tf_op jit(solution)/shard_map/pallas_call | solution.py:382
  (122 shorter events, 57.7 us)
Async XLA Ops:
  5.2 10.2 %collective-permute-start = (s32[2,136,256]{2,1,0:T(8,128)}, s32[2,136,256]{2,1,0:T(8,128)S(1)}, u32[]{:S(2)}, u32[]{:S(2)}) collective-permute-start(s32[2,136,256]{2,1,0:T(8,128)} %shard_map.181), channel_id=1, source_target_pairs={{0,0},{1,1},{2,17},{3,16},{4,32},{5,33},{6,49},{7,48},{8,64},{9,65... | collective-permute-start | bytes 835592 | tf_op jit(solution)/shard_map/ppermute | solution.py:477
  15.4 26.0 %collective-permute-start.2 = (s32[2,136,256]{2,1,0:T(8,128)S(1)}, s32[2,136,256]{2,1,0:T(8,128)S(1)}, u32[]{:S(2)}, u32[]{:S(2)}) collective-permute-start(s32[2,136,256]{2,1,0:T(8,128)S(1)} %collective-permute-done.refs_0_), channel_id=1, source_target_pairs={{0,32},{16,48},{32,64},{48,80},{64,96},{80,112},{96,0},{112,16},{1... | collective-permute-start | bytes 835592 | tf_op jit(solution)/shard_map/ppermute | solution.py:409
  20.0 21.4 %collective-permute-start.3 = (s32[2,136,256]{2,1,0:T(8,128)S(1)}, s32[2,136,256]{2,1,0:T(8,128)S(1)}, u32[]{:S(2)}, u32[]{:S(2)}) collective-permute-start(s32[2,136,256]{2,1,0:T(8,128)S(1)} %collective-permute-done.refs_0_), channel_id=1, source_target_pairs={{0,64},{16,80},{32,96},{48,112},{64,0},{80,16},{96,32},{112,48},{1... | collective-permute-start | bytes 835592 | tf_op jit(solution)/shard_map/ppermute | solution.py:409
  27.3 14.1 %collective-permute-start.4 = (s32[2,136,256]{2,1,0:T(8,128)S(1)}, s32[2,136,256]{2,1,0:T(8,128)S(1)}, u32[]{:S(2)}, u32[]{:S(2)}) collective-permute-start(s32[2,136,256]{2,1,0:T(8,128)S(1)} %collective-permute-done.refs_0_), channel_id=1, source_target_pairs={{0,96},{16,112},{32,0},{48,16},{64,32},{80,48},{96,64},{112,80},{1... | collective-permute-start | bytes 835592 | tf_op jit(solution)/shard_map/ppermute | solution.py:409
  41.4 57.1 %all-to-all-start = ((bf16[128,32,256]{2,1,0:T(8,128)(2,1)}), bf16[128,32,256]{2,1,0:T(8,128)(2,1)S(1)}, u32[]{:S(2)}, u32[]{:S(2)}) async-start(bf16[128,32,256]{2,1,0:T(8,128)(2,1)} %bitcast.35), calls=%async_computation | async-start | bytes 4194304 | tf_op jit(solution)/shard_map/all_to_all | solution.py:506
  98.2 83.3 %collective-permute-start.8 = (f32[3,256,512]{2,1,0:T(8,128)}, f32[3,256,512]{2,1,0:T(8,128)}, u32[]{:S(2)}, u32[]{:S(2)}) collective-permute-start(f32[3,256,512]{2,1,0:T(8,128)} %constant_dynamic-slice_fusion.9), channel_id=1, source_target_pairs={{0,16},{16,0},{32,48},{48,32},{64,80},{80,64},{96,112},{112,96},{1... | collective-permute-start | bytes 4718600 | tf_op jit(solution)/shard_map/ppermute | solution.py:409
  99.9 128.0 %all-to-all-start.1 = ((s32[16,2,136,256]{3,2,1,0:T(8,128)}), s32[16,2,136,256]{3,2,1,0:T(8,128)}, u32[]{:S(2)}, u32[]{:S(2)}) async-start(s32[16,2,136,256]{3,2,1,0:T(8,128)} %get-tuple-element.49), calls=%async_computation.1 | async-start | bytes 8912896 | tf_op jit(solution)/shard_map/all_to_all | solution.py:511
  111.6 66.9 %collective-permute-start.18 = (f32[8,128,128]{2,1,0:T(8,128)}, f32[8,128,128]{2,1,0:T(8,128)}, u32[]{:S(2)}, u32[]{:S(2)}) collective-permute-start(f32[8,128,128]{2,1,0:T(8,128)} %shard_map.185), channel_id=1, source_target_pairs={{0,0},{1,8},{18,16},{19,24},{36,32},{37,40},{54,48},{55,56},{72,64... | collective-permute-start | bytes 1572872 | tf_op jit(solution)/shard_map/ppermute | solution.py:490
  179.5 11.4 %collective-permute-start.19 = (f32[4,128,128]{2,1,0:T(8,128)S(1)}, f32[4,128,128]{2,1,0:T(8,128)}, u32[]{:S(2)}, u32[]{:S(2)}) collective-permute-start(f32[4,128,128]{2,1,0:T(8,128)S(1)} %slice.46), channel_id=1, source_target_pairs={{0,4},{8,12},{16,20},{24,28},{32,36},{40,44},{48,52},{56,60},{64,6... | collective-permute-start | bytes 786440 | tf_op jit(solution)/shard_map/ppermute | solution.py:494
  184.5 14.9 %collective-permute-start.11 = (f32[3,64,512]{2,1,0:T(8,128)S(1)}, f32[3,64,512]{2,1,0:T(8,128)S(1)}, u32[]{:S(2)}, u32[]{:S(2)}) collective-permute-start(f32[3,64,512]{2,1,0:T(8,128)S(1)} %get-tuple-element.67), channel_id=1, source_target_pairs={{0,96},{16,112},{32,0},{48,16},{64,32},{80,48},{96,64},{112,80},{1... | collective-permute-start | bytes 1179656 | tf_op jit(solution)/shard_map/ppermute | solution.py:409
  188.4 11.0 %collective-permute-start.10 = (f32[3,64,512]{2,1,0:T(8,128)S(1)}, f32[3,64,512]{2,1,0:T(8,128)S(1)}, u32[]{:S(2)}, u32[]{:S(2)}) collective-permute-start(f32[3,64,512]{2,1,0:T(8,128)S(1)} %get-tuple-element.68), channel_id=1, source_target_pairs={{0,64},{16,80},{32,96},{48,112},{64,0},{80,16},{96,32},{112,48},{1... | collective-permute-start | bytes 1179656 | tf_op jit(solution)/shard_map/ppermute | solution.py:409
  190.1 10.6 %collective-permute-start.9 = (f32[3,64,512]{2,1,0:T(8,128)S(1)}, f32[3,64,512]{2,1,0:T(8,128)S(1)}, u32[]{:S(2)}, u32[]{:S(2)}) collective-permute-start(f32[3,64,512]{2,1,0:T(8,128)S(1)} %get-tuple-element.66), channel_id=1, source_target_pairs={{0,32},{16,48},{32,64},{48,80},{64,96},{80,112},{96,0},{112,16},{1... | collective-permute-start | bytes 1179656 | tf_op jit(solution)/shard_map/ppermute | solution.py:409
  191.9 11.6 %collective-permute-start.20 = (f32[2,128,128]{2,1,0:T(8,128)S(1)}, f32[2,128,128]{2,1,0:T(8,128)S(1)}, u32[]{:S(2)}, u32[]{:S(2)}) collective-permute-start(f32[2,128,128]{2,1,0:T(8,128)S(1)} %slice.48), channel_id=1, source_target_pairs={{0,2},{4,6},{8,10},{12,14},{16,18},{20,22},{24,26},{28,30},{32,34}... | collective-permute-start | bytes 393224 | tf_op jit(solution)/shard_map/ppermute | solution.py:494
  202.0 5.2 %collective-permute-start.13 = (f32[3,16,512]{2,1,0:T(8,128)S(1)}, f32[3,16,512]{2,1,0:T(8,128)S(1)}, u32[]{:S(2)}, u32[]{:S(2)}) collective-permute-start(f32[3,16,512]{2,1,0:T(8,128)S(1)} %get-tuple-element.71), channel_id=1, source_target_pairs={{0,2},{1,3},{2,0},{3,1},{4,6},{5,7},{6,4},{7,5},{8,10},{9,11},{10,... | collective-permute-start | bytes 294920 | tf_op jit(solution)/shard_map/ppermute | solution.py:409
  202.1 6.2 %collective-permute-start.12 = (f32[3,16,512]{2,1,0:T(8,128)S(1)}, f32[3,16,512]{2,1,0:T(8,128)S(1)}, u32[]{:S(2)}, u32[]{:S(2)}) collective-permute-start(f32[3,16,512]{2,1,0:T(8,128)S(1)} %get-tuple-element.69), channel_id=1, source_target_pairs={{0,1},{1,2},{2,3},{3,0},{4,5},{5,6},{6,7},{7,4},{8,9},{9,10},{10,1... | collective-permute-start | bytes 294920 | tf_op jit(solution)/shard_map/ppermute | solution.py:409
  203.5 6.4 %collective-permute-start.21 = (f32[1,128,128]{2,1,0:T(8,128)S(1)}, f32[1,128,128]{2,1,0:T(8,128)S(1)}, u32[]{:S(2)}, u32[]{:S(2)}) collective-permute-start(f32[1,128,128]{2,1,0:T(8,128)S(1)} %slice.50), channel_id=1, source_target_pairs={{0,1},{2,3},{4,5},{6,7},{8,9},{10,11},{12,13},{14,15},{16,17},{18,... | collective-permute-start | bytes 196616 | tf_op jit(solution)/shard_map/ppermute | solution.py:494
  208.6 5.0 %collective-permute-start.15 = (f32[3,16,128]{2,1,0:T(8,128)S(1)}, f32[3,16,128]{2,1,0:T(8,128)S(1)}, u32[]{:S(2)}, u32[]{:S(2)}) collective-permute-start(f32[3,16,128]{2,1,0:T(8,128)S(1)} %get-tuple-element.74), channel_id=1, source_target_pairs={{0,4},{1,5},{2,6},{3,7},{4,8},{5,9},{6,10},{7,11},{8,12},{9,13},{1... | collective-permute-start | bytes 73736 | tf_op jit(solution)/shard_map/ppermute | solution.py:409
  221.8 5.1 %collective-permute-start.26 = (f32[4,3,16,128]{3,2,1,0:T(8,128)S(1)}, f32[4,3,16,128]{3,2,1,0:T(8,128)S(1)}, u32[]{:S(2)}, u32[]{:S(2)}) collective-permute-start(f32[4,3,16,128]{3,2,1,0:T(8,128)S(1)} %get-tuple-element.73), channel_id=1, source_target_pairs={{0,2},{1,3},{2,0},{3,1},{4,6},{5,7},{6,4},{7,5},{8,10},{9,11},{10,... | collective-permute-start | bytes 294920 | tf_op jit(solution)/shard_map/ppermute | solution.py:409
  222.3 5.5 %collective-permute-start.25 = (f32[4,3,16,128]{3,2,1,0:T(8,128)S(1)}, f32[4,3,16,128]{3,2,1,0:T(8,128)S(1)}, u32[]{:S(2)}, u32[]{:S(2)}) collective-permute-start(f32[4,3,16,128]{3,2,1,0:T(8,128)S(1)} %get-tuple-element.73), channel_id=1, source_target_pairs={{0,1},{1,2},{2,3},{3,0},{4,5},{5,6},{6,7},{7,4},{8,9},{9,10},{10,1... | collective-permute-start | bytes 294920 | tf_op jit(solution)/shard_map/ppermute | solution.py:409
  227.9 6.7 %collective-permute-start.30 = (f32[4,4,3,16,128]{4,3,2,1,0:T(8,128)S(1)}, f32[4,4,3,16,128]{4,3,2,1,0:T(8,128)S(1)}, u32[]{:S(2)}, u32[]{:S(2)}) collective-permute-start(f32[4,4,3,16,128]{4,3,2,1,0:T(8,128)S(1)} %pad_maximum_fusion.1), channel_id=1, source_target_pairs={{0,96},{16,112},{32,0},{48,16},{64,32},{80,48},{96,64},{112,80},{1... | collective-permute-start | bytes 1179656 | tf_op jit(solution)/shard_map/ppermute | solution.py:409
  228.3 8.2 %collective-permute-start.29 = (f32[4,4,3,16,128]{4,3,2,1,0:T(8,128)S(1)}, f32[4,4,3,16,128]{4,3,2,1,0:T(8,128)S(1)}, u32[]{:S(2)}, u32[]{:S(2)}) collective-permute-start(f32[4,4,3,16,128]{4,3,2,1,0:T(8,128)S(1)} %pad_maximum_fusion.1), channel_id=1, source_target_pairs={{0,64},{16,80},{32,96},{48,112},{64,0},{80,16},{96,32},{112,48},{1... | collective-permute-start | bytes 1179656 | tf_op jit(solution)/shard_map/ppermute | solution.py:409
  229.5 15.9 %collective-permute-start.28 = (f32[4,4,3,16,128]{4,3,2,1,0:T(8,128)S(1)}, f32[4,4,3,16,128]{4,3,2,1,0:T(8,128)S(1)}, u32[]{:S(2)}, u32[]{:S(2)}) collective-permute-start(f32[4,4,3,16,128]{4,3,2,1,0:T(8,128)S(1)} %pad_maximum_fusion.1), channel_id=1, source_target_pairs={{0,32},{16,48},{32,64},{48,80},{64,96},{80,112},{96,0},{112,16},{1... | collective-permute-start | bytes 1179656 | tf_op jit(solution)/shard_map/ppermute | solution.py:409
  245.6 21.3 %collective-permute-start.31 = (f32[4,4,4,3,16,128]{5,4,3,2,1,0:T(8,128)S(1)}, f32[4,4,4,3,16,128]{5,4,3,2,1,0:T(8,128)S(1)}, u32[]{:S(2)}, u32[]{:S(2)}) collective-permute-start(f32[4,4,4,3,16,128]{5,4,3,2,1,0:T(8,128)S(1)} %pad_maximum_fusion.own_ref), channel_id=1, source_target_pairs={{0,16},{16,0},{32,48},{48,32},{64,80},{80,64},{96,112},{112,96},{1... | collective-permute-start | bytes 4718600 | tf_op jit(solution)/shard_map/ppermute | solution.py:409
  261.3 18.3 %all-to-all-start.2 = ((f32[128,1,32]{2,1,0:T(1,128)}), f32[128,1,32]{2,1,0:T(1,128)S(1)}, u32[]{:S(2)}, u32[]{:S(2)}) async-start(f32[128,1,32]{2,1,0:T(1,128)} %bitcast.24), calls=%async_computation.2 | async-start | bytes 131072 | tf_op jit(solution)/shard_map/all_to_all | solution.py:533
  (27 other events, 256.7 us)

commit v4 on v3

--- a/solution.py
+++ b/solution.py
@@ -47,15 +47,15 @@
     return jnp.concatenate([high, low], axis=-1).astype(jnp.float32)
 
 
-def encode(value, out_ref, *at):
+def encode(value, out_ref, *at, first=0):
     rows = value.shape[0]
     largest = jnp.max(jnp.abs(value), axis=0, keepdims=True)
     step = jnp.ceil(jnp.log2(jnp.maximum(largest, TINY)) * STEPS)
     code = jnp.round(value * (jnp.exp2(step * (-1.0 / STEPS)) * LEVELS))
     code = jnp.clip(code, -32767.0, 32767.0).astype(jnp.int32)
-    out_ref[(*at, pl.ds(0, rows), slice(None))] = pack(code)
+    out_ref[(*at, pl.ds(first, rows), slice(None))] = pack(code)
     head = pack(step.astype(jnp.int32))
-    out_ref[(*at, pl.ds(rows, 8), slice(None))] = jnp.broadcast_to(head, (8, head.shape[1]))
+    out_ref[(*at, pl.ds(first + rows, 8), slice(None))] = jnp.broadcast_to(head, (8, head.shape[1]))
 
 
 def decode(word):
@@ -99,22 +99,28 @@
     )(at, bits_two, bits_one, panel_two, panel_one, inv_two, inv_one)
 
 
-def tiles_kernel(at_ref, tile_ref, out_ref):
-    out_ref[0] = tile_ref[...]
-
-
-def tiles_of(at, trail_cov, count, bw):
-    return pl.pallas_call(
-        tiles_kernel,
-        out_shape=jax.ShapeDtypeStruct((count, bw, bw), jnp.float32),
-        grid_spec=pltpu.PrefetchScalarGridSpec(
-            num_scalar_prefetch=1,
-            grid=(count,),
-            in_specs=[pl.BlockSpec((bw, bw), lambda j, at: (lax.rem(at[1], 2) * count + j, j))],
-            out_specs=pl.BlockSpec((1, bw, bw), lambda j, at: (j, 0, 0)),
-        ),
-        cost_estimate=LIGHT,
-    )(at, trail_cov)
+def encode_tile(tile, out_ref, block, first):
+    bw = tile.shape[0]
+    largest = jnp.max(jnp.abs(tile), axis=0, keepdims=True)
+    step = jnp.ceil(jnp.log2(jnp.maximum(largest, TINY)) * STEPS)
+    code = jnp.round(tile * (jnp.exp2(step * (-1.0 / STEPS)) * LEVELS))
+    code = pack(jnp.clip(code, -32767.0, 32767.0).astype(jnp.int32))
+    tall, wide = bw // 4, bw // 2
+    out_ref[block, pl.ds(first, tall), :] = jnp.concatenate(
+        [code[i * tall : (i + 1) * tall] for i in range(4)], axis=1
+    )
+    head = jnp.broadcast_to(pack(step.astype(jnp.int32)), (8, wide))
+    out_ref[block, pl.ds(first + tall, 8), :] = jnp.concatenate([head] * 4, axis=1)
+
+
+def decode_tile(word, bw):
+    tall, wide = bw // 4, bw // 2
+    code = jnp.concatenate(
+        [word[:tall, i * wide : (i + 1) * wide] for i in range(4)]
+        + [word[tall : tall + 8, :wide]],
+        axis=0,
+    )
+    return decode(code)
 
 
 def image_kernel(bw, pieces, at_ref, cov_ref, *refs):
@@ -140,23 +146,32 @@
         )
         image_ref[...] = image
         for i in range(image.shape[0] // bw):
-            encode(image[i * bw : (i + 1) * bw], code_ref, i, panel)
+            encode(image[i * bw : (i + 1) * bw], code_ref, i, first=panel * (bw + 8))
+
+    for i in range(cov_ref.shape[0] // bw):
+        block = pl.program_id(0) * (cov_ref.shape[0] // bw) + i
+
+        @pl.when(at_ref[1] == 2 * at_ref[0] + block // pieces)
+        def _():
+            columns = pl.ds(pl.multiple_of(lax.rem(block, pieces) * bw, bw), bw)
+            encode_tile(cov_ref[i * bw : (i + 1) * bw, columns], code_ref, i, 2 * (bw + 8))
 
 
 def image(at, trail_cov, held, bw, tile=512):
     rows, span = trail_cov.shape
     width = 2 * held[0].shape[-1]
+    tall = 2 * (bw + 8) + bw // 4 + 8
     every = pl.BlockSpec(held[0].shape, lambda i, at: (0, 0, 0))
     return pl.pallas_call(
         functools.partial(image_kernel, bw, len(held)),
         out_shape=[jax.ShapeDtypeStruct((rows, width), jnp.float32)] * 2
-        + [jax.ShapeDtypeStruct((rows // bw, 2, bw + 8, width // 2), jnp.int32)],
+        + [jax.ShapeDtypeStruct((rows // bw, tall, width // 2), jnp.int32)],
         grid_spec=pltpu.PrefetchScalarGridSpec(
             num_scalar_prefetch=1,
             grid=(rows // tile,),
             in_specs=[pl.BlockSpec((tile, span), lambda i, at: (i, 0))] + [every] * len(held),
             out_specs=[pl.BlockSpec((tile, width), lambda i, at: (i, 0))] * 2
-            + [pl.BlockSpec((tile // bw, 2, bw + 8, width // 2), lambda i, at: (i, 0, 0, 0))],
+            + [pl.BlockSpec((tile // bw, tall, width // 2), lambda i, at: (i, 0, 0))],
             scratch_shapes=[pltpu.VMEM((span, 2 * width), jnp.bfloat16)] * 2,
         ),
         compiler_params=pltpu.CompilerParams(vmem_limit_bytes=ROOM),
@@ -166,13 +181,13 @@
 
 def sums_kernel(
     bw, at_ref, bits_two_ref, bits_one_ref, two_ref, one_ref, image_two_ref, image_one_ref,
-    inv_two_ref, inv_one_ref, out_ref,
+    inv_two_ref, inv_one_ref, keep_ref, give_ref, sums_ref,
 ):
     step = pl.program_id(0)
 
     @pl.when(step == 0)
     def _():
-        out_ref[...] = jnp.zeros_like(out_ref)
+        sums_ref[...] = jnp.zeros_like(sums_ref)
 
     count = two_ref.shape[0] // bw
     first = 16 * at_ref[0] + step * count
@@ -191,50 +206,150 @@
     image_one = split(image_one_ref[...])
     two, one = split(two), split(one)
     for i, (left, right) in enumerate(((two, image_two), (one, image_two), (one, image_one))):
-        out_ref[i] += tdot(left[0], right[0]) + (tdot(left[0], right[1]) + tdot(left[1], right[0]))
+        sums_ref[i] += tdot(left[0], right[0]) + (tdot(left[0], right[1]) + tdot(left[1], right[0]))
 
     @pl.when(step == pl.num_programs(0) - 1)
     def _():
+        half = keep_ref.shape[1]
+        core = lax.rem(at_ref[0], 2)
         for i, inv in enumerate((inv_two_ref, inv_one_ref, inv_one_ref)):
-            out_ref[i] = product(inv[...], out_ref[i], tdot)
+            sums_ref[i] = product(inv[...], sums_ref[i], tdot)
+            keep_ref[i] = sums_ref[i, pl.ds(pl.multiple_of(core * half, half), half), :]
+            give_ref[i] = sums_ref[i, pl.ds(pl.multiple_of((1 - core) * half, half), half), :]
 
 
 def sums(at, bits_two, bits_one, panel_two, panel_one, image_two, image_one, inv_two, inv_one, bw, tile=512):
     rows, width = panel_two.shape
     part = pl.BlockSpec((tile, width), lambda i, *_: (i, 0))
     whole = pl.BlockSpec((width, width), lambda i, *_: (0, 0))
+    half = (3, width // 2, width)
     return pl.pallas_call(
         functools.partial(sums_kernel, bw),
-        out_shape=jax.ShapeDtypeStruct((3, width, width), jnp.float32),
+        out_shape=[jax.ShapeDtypeStruct(half, jnp.float32)] * 2,
         grid_spec=pltpu.PrefetchScalarGridSpec(
             num_scalar_prefetch=3,
             grid=(rows // tile,),
             in_specs=[part] * 4 + [whole] * 2,
-            out_specs=pl.BlockSpec((3, width, width), lambda i, *_: (0, 0, 0)),
+            out_specs=[pl.BlockSpec(half, lambda i, *_: (0, 0, 0))] * 2,
+            scratch_shapes=[pltpu.VMEM((3, width, width), jnp.float32)],
         ),
         compiler_params=pltpu.CompilerParams(vmem_limit_bytes=ROOM),
         cost_estimate=LIGHT,
     )(at, bits_two, bits_one, panel_two, panel_one, image_two, image_one, inv_two, inv_one)
 
 
-def rows_kernel(at_ref, bits_two_ref, bits_one_ref, panel_ref, code_ref, top_ref, cov_two_ref, cov_one_ref, cross_ref):
-    count = code_ref.shape[0]
+def call(kernel, at, inputs, shapes):
+    vmem = pl.BlockSpec(memory_space=pltpu.VMEM)
+    return pl.pallas_call(
+        kernel,
+        out_shape=[jax.ShapeDtypeStruct(*shape) for shape in shapes],
+        in_specs=[pl.BlockSpec(memory_space=pltpu.SMEM)] + [vmem] * len(inputs),
+        out_specs=[vmem] * len(shapes),
+        compiler_params=pltpu.CompilerParams(vmem_limit_bytes=ROOM),
+        cost_estimate=LIGHT,
+    )(at, *inputs)
+
+
+def part_of(place, step, size):
+    return pl.ds(pl.multiple_of(lax.rem(place + step, 4) * size, size), size)
+
+
+def fold_z_kernel(at_ref, own_ref, got_ref, mine_ref, *code_refs):
+    size = mine_ref.shape[1]
+    for step, ref in enumerate((mine_ref, *code_refs)):
+        at = part_of(at_ref[0] // 2, step, size)
+        for i in range(3):
+            value = own_ref[i, at, :] + got_ref[i, at, :]
+            if step:
+                encode(value, ref, i)
+            else:
+                ref[i] = value
+
+
+def fold_z(at, own, got):
+    count, size, width = own.shape[0], own.shape[1] // 4, own.shape[2]
+    return call(
+        fold_z_kernel, at, [own, got],
+        [((count, size, width), jnp.float32)] + [((count, size + 8, width // 2), jnp.int32)] * 3,
+    )
+
+
+def fold_x_kernel(at_ref, own_ref, *refs):
+    codes, outs, total_ref = refs[:3], refs[3:7], refs[7]
+    size = outs[0].shape[1]
+    for i in range(3):
+        value = own_ref[i]
+        for ref in codes:
+            value = value + decode(ref[i])
+        total_ref[i] = value
+    for step, ref in enumerate(outs):
+        ref[...] = total_ref[:, part_of(lax.rem(at_ref[1], 4), step, size), :]
+
+
+def fold_x(at, own, codes):
+    count, size, width = own.shape
+    part, whole = ((count, size // 4, width), jnp.float32), ((count, size, width), jnp.float32)
+    return call(fold_x_kernel, at, [own, *codes], [part] * 4 + [whole])[:4]
+
+
+def fold_y_kernel(at_ref, *refs):
+    parts, outs, total_ref = refs[:4], refs[4:8], refs[8]
+    total_ref[...] = (parts[0][...] + parts[1][...]) + (parts[2][...] + parts[3][...])
+    size = outs[0].shape[2]
+    for step, ref in enumerate(outs):
+        ref[...] = total_ref[:, :, part_of(at_ref[1] // 4, step, size)]
+
+
+def fold_y(at, parts):
+    count, size, width = parts[0].shape
+    part, whole = ((count, size, width // 4), jnp.float32), ((count, size, width), jnp.float32)
+    return call(fold_y_kernel, at, parts, [part] * 4 + [whole])[:4]
+
+
+def unfold_kernel(at_ref, *refs):
+    parts, (code_ref, total_ref) = refs[:4], refs[4:]
+    size, lanes = parts[0].shape[2:]
+    for dx, ref in enumerate(parts):
+        for dy in range(4):
+            total_ref[
+                :,
+                part_of(lax.rem(at_ref[1], 4) + 4, -dx, size),
+                part_of(at_ref[1] // 4 + 4, -dy, lanes),
+            ] = ref[dy]
+    for i in range(3):
+        encode(total_ref[i], code_ref, i)
+
+
+def unfold(at, parts):
+    _, count, size, lanes = parts[0].shape
+    return call(
+        unfold_kernel, at, parts,
+        [
+            ((count, 4 * size + 8, 2 * lanes), jnp.int32),
+            ((count, 4 * size, 4 * lanes), jnp.float32),
+        ],
+    )[0]
+
+
+def rows_kernel(at_ref, bits_two_ref, bits_one_ref, panel_ref, code_ref, top_ref, cov_two_ref, cov_one_ref, cross_ref, tile_ref):
+    count, bw = code_ref.shape[0], tile_ref.shape[0]
+    tile_ref[...] = decode_tile(code_ref[2 * at_ref[0] + at_ref[1] // 8, 2 * (bw + 8) :], bw)
     block = 16 * at_ref[0] + at_ref[1]
     skip = bits_one_ref.shape[0] - bits_two_ref.shape[0]
     keep_two = bits_two_ref[block].astype(jnp.float32)
     keep_one = bits_one_ref[skip + block].astype(jnp.float32)
 
     def total(panel):
-        value = decode(code_ref[0, panel])
+        at = slice(panel * (bw + 8), (panel + 1) * (bw + 8))
+        value = decode(code_ref[0, at])
         for i in range(1, count):
-            value = value + decode(code_ref[i, panel])
+            value = value + decode(code_ref[i, at])
         return value
 
     cov_two = -keep_two * total(0)
     cov_two_ref[...] = cov_two
     cov_one = -keep_one * (product(cov_two, top_ref[...]) + total(1))
     cov_one_ref[...] = cov_one
-    bw = cross_ref.shape[1]
     cross_ref[...] = cov_one_ref[:, pl.ds(pl.multiple_of(panel_ref[block] * bw, bw), bw)]
 
 
@@ -244,34 +359,23 @@
     vmem = pl.BlockSpec(memory_space=pltpu.VMEM)
     return pl.pallas_call(
         rows_kernel,
-        out_shape=[jax.ShapeDtypeStruct((bw, n), jnp.float32) for n in (width, width, bw)],
+        out_shape=[jax.ShapeDtypeStruct((bw, n), jnp.float32) for n in (width, width, bw, bw)],
         in_specs=[smem] * 4 + [vmem] * 2,
-        out_specs=[vmem] * 3,
+        out_specs=[vmem] * 4,
         compiler_params=pltpu.CompilerParams(vmem_limit_bytes=ROOM),
         cost_estimate=LIGHT,
     )(at, bits_two, bits_one, panel, code, norm_top)
 
 
-def small_kernel(at_ref, own_ref, other_ref, gram_ref, top_ref, keep_ref, two_ref, top_cov_ref, one_ref, sums_ref):
-    y_count, lanes = own_ref.shape[2], own_ref.shape[-1]
-    tall = own_ref.shape[-2]
-
-    own_z, own_core = at_ref[0] // 2, lax.rem(at_ref[0], 2)
-    own_x, own_y = lax.rem(at_ref[1], 4), at_ref[1] // 4
-    for flip, ref in enumerate((own_ref, other_ref)):
-        half = lax.rem(own_core + flip, 2)
-        for dz in range(4):
-            z = lax.rem(own_z + 4 - dz, 4)
-            for dx in range(4):
-                x = lax.rem(own_x + 4 - dx, 4)
-                row = ((half * 4 + z) * 4 + x) * tall
-                for dy in range(y_count):
-                    y = lax.rem(own_y + 4 - dy, 4)
-                    sums_ref[
-                        :,
-                        pl.ds(pl.multiple_of(row, tall), tall),
-                        pl.ds(pl.multiple_of(y * lanes, lanes), lanes),
-                    ] = ref[dz, dx, dy]
+def small_kernel(at_ref, keep_ref, gram_ref, top_ref, *refs):
+    held, (two_ref, top_cov_ref, one_ref, sums_ref) = refs[:8], refs[8:]
+    size = held[0].shape[1] - 8
+    z, core = at_ref[0] // 2, lax.rem(at_ref[0], 2)
+    for i, ref in enumerate(held):
+        block = lax.rem(core + i, 2) * 4 + lax.rem(z + 4 - i // 2, 4)
+        rows = pl.ds(pl.multiple_of(block * size, size), size)
+        for j in range(3):
+            sums_ref[j, rows, :] = decode(ref[j])
     top = top_ref[...]
     two = gram_ref[0] + sums_ref[0]
     two_ref[...] = two
@@ -287,19 +391,19 @@
     one_ref[...] = gram_ref[1] + sums_ref[2] - product(top, top_cov, tdot) - product(mixed, top)
 
 
-def small(at, own, other, gram, norm_top, bits_top):
+def small(at, held, gram, norm_top, bits_top):
     width = norm_top.shape[0]
     smem = pl.BlockSpec(memory_space=pltpu.SMEM)
     vmem = pl.BlockSpec(memory_space=pltpu.VMEM)
     return pl.pallas_call(
         small_kernel,
         out_shape=[jax.ShapeDtypeStruct((width, width), jnp.float32)] * 3,
-        in_specs=[smem, vmem, vmem, vmem, vmem, smem],
+        in_specs=[smem] * 2 + [vmem] * 10,
         out_specs=[vmem] * 3,
         scratch_shapes=[pltpu.VMEM((3, width, width), jnp.float32)],
         compiler_params=pltpu.CompilerParams(vmem_limit_bytes=ROOM),
         cost_estimate=LIGHT,
-    )(at, own, other, gram, norm_top, bits_top)
+    )(at, bits_top, gram, norm_top, *held)
 
 
 def early_kernel(keep_ref, top_rows_ref, inv_two_ref, inv_one_ref, gram_ref, top_ref):
@@ -398,9 +502,6 @@
     def __init__(self, axis, size, stride, count=4):
         self.axis, self.size, self.stride, self.count = axis, size, stride, count
 
-    def place(self):
-        return lax.axis_index(self.axis) // self.stride % self.count
-
     def move(self, value, step):
         pairs = []
         for i in range(self.size):
@@ -408,21 +509,8 @@
             pairs.append((i, i + ((at + step) % self.count - at) * self.stride))
         return lax.ppermute(value, self.axis, pairs)
 
-    def scatter_sum(self, value, axis):
-        size = value.shape[axis] // self.count
-
-        def take(step):
-            at = (self.place() + step) % self.count * size
-            return lax.dynamic_slice_in_dim(value, at, size, axis)
-
-        parts = [self.move(take(step), step) for step in range(1, self.count)]
-        total = take(0)
-        for part in parts:
-            total = total + part
-        return total
-
-    def gather(self, value):
-        return jnp.stack([value] + [self.move(value, step) for step in range(1, self.count)])
+    def others(self, parts):
+        return [self.move(part, step + 1) for step, part in enumerate(parts)]
 
 
 def spread_pairs(row_count, col_count):
@@ -457,7 +545,6 @@
     total_count = row_count * col_count
     row_index = lax.axis_index("row")
     col_index = lax.axis_index("col")
-    ratio = col_count // row_count
     width = diag_inv_two.shape[0]
     bw = loadings.shape[1] // 2
     top_blocks = width // bw
@@ -475,26 +562,11 @@
     blocks = unit_block[:, 0]
     part, blocks = lax.optimization_barrier((part, blocks))
     part = lax.ppermute(part, BOTH, spread_pairs(row_count, col_count))
+
     held = []
     for step in range(4):
         piece = ring_z.move(part, step) if step else part
         held += [piece, core.move(piece, 1)]
-
-    tiles = tiles_of(at, trail_cov, row_count, bw)
-    turn = col_index % row_count
-    pairs = [
-        (r * col_count + ratio * r + h, r * col_count + h * row_count)
-        for r in range(row_count)
-        for h in range(ratio)
-    ]
-    tiles = lax.ppermute(tiles, BOTH, pairs)
-    half = row_count // 2
-    while half:
-        pairs = [(c, c + half) for c in range(0, col_count, 2 * half)]
-        handed = lax.ppermute(tiles[half:], "col", pairs)
-        tiles = jnp.where(turn // half % 2 == 1, handed, tiles[:half])
-        half //= 2
-    tile = tiles[0]
 
     capacity = 2 * loadings.shape[0] // total_count
     hits = (blocks[:, None] == jnp.arange(total_count, dtype=jnp.int32)[None, :]).astype(jnp.int32)
@@ -510,29 +582,31 @@
     code, units = lax.optimization_barrier((code, units))
     code = lax.all_to_all(code, "col", split_axis=0, concat_axis=0, tiled=True)
 
-    total = sums(
+    keep, give = sums(
         at, pattern_two, pattern_one, panel_two_rows, panel_one_rows, image_two, image_one,
         diag_inv_two, diag_inv_one, bw,
     )
-    bits_top, total = lax.optimization_barrier((bits_top, total))
+    bits_top, keep = lax.optimization_barrier((bits_top, keep))
     gram, norm_top = early(bits_top, panel_one_top, diag_inv_two, diag_inv_one)
-    total = core.scatter_sum(total, 1)
-    total = ring_z.scatter_sum(total, 1)
-    total, norm_top = lax.optimization_barrier((total, norm_top))
-    total = ring_x.scatter_sum(total, 1)
-    total = ring_y.scatter_sum(total, 2)
-    total, tile = lax.optimization_barrier((total, tile))
-    total = ring_y.gather(total)
-    total = ring_x.gather(total)
+    mine, *codes = fold_z(at, keep, core.move(give, 1))
+    mine, *parts = fold_x(at, mine, ring_z.others(codes))
+    mine, norm_top = lax.optimization_barrier((mine, norm_top))
+    mine, *parts = fold_y(at, [mine, *ring_x.others(parts)])
+    total = mine
+    for part in ring_y.others(parts):
+        total = total + part
+    total = jnp.stack([total, *ring_y.others([total] * 3)])
+    total = unfold(at, [total, *ring_x.others([total] * 3)])
     total, code = lax.optimization_barrier((total, code))
-    total = ring_z.gather(total)
-    cov_two, cov_one, cross = rows(
+    whole = []
+    for piece in [total, *ring_z.others([total] * 3)]:
+        whole += [piece, core.move(piece, 1)]
+    cov_two, cov_one, cross, tile = rows(
         at, pattern_two, pattern_one, block_panel, code, norm_top, bw
     )
     value = forms(units, tile, cross)[0].reshape(total_count, capacity)
     returned = lax.all_to_all(value, BOTH, split_axis=0, concat_axis=0, tiled=True)
-    other = core.move(total, 1)
-    diag_two, top_cov, diag_one = small(at, total, other, gram, norm_top, bits_top)
+    diag_two, top_cov, diag_one = small(at, whole, gram, norm_top, bits_top)
     own_panel = jnp.sum(hits * block_panel[None, :], axis=1, keepdims=True)
     within = inner(loadings, own_panel, diag_one)[0]
     within, returned = lax.optimization_barrier((within, returned))

time: 283 us -> 244 us (0.86)
  waiting for transfers between devices: 102 us -> 54.1 us
  starting transfers between devices: 70.5 us -> 79.4 us
  Pallas kernels: 75.8 us -> 80.1 us
  other arithmetic: 7.63 us -> 3.68 us
    ppermute x4 -> x0, waiting for transfers between devices: 65.5 us -> none  [the longest x1 65.5 us: local(): tiles = lax.ppermute(tiles, BOTH, pairs)]
    ppermute x27 -> x30, starting transfers between devices: 36.5 us -> 52.6 us  [move(): return lax.ppermute(value, self.axis, pairs)]
    ppermute x27 -> x30, waiting for transfers between devices: 32.1 us -> 45.5 us  [move(): return lax.ppermute(value, self.axis, pairs)]
    ppermute x4 -> x0, starting transfers between devices: 7.99 us -> none  [the longest x3 6.71 us: local(): handed = lax.ppermute(tiles[half:], 'col', pairs)]
    all_to_all x1, waiting for transfers between devices: 0.01 us -> 4.65 us  [local(): lax.all_to_all(packed, BOTH, split_axis=0, concat_axis=0, tiled=True)]
    pallas_call x2 -> x5, Pallas kernels: 25.5 us -> 29.3 us  [the longest x1 20.2 us: sums(): pl.pallas_call(functools.partial(sums_kernel, bw), out_shape=[jax.ShapeDt...]
    unnamed x32 -> x66, local copies, waits for them, and re-layouts: 3.74 us -> 7.11 us
    dynamic_slice x4 -> x0, local copies, waits for them, and re-layouts: 2.83 us -> none  [take(): return lax.dynamic_slice_in_dim(value, at, size, axis)]
  transfers between devices with their start and end apart: 35 -> 34, of which waited for: 20 -> 18; matrix products, arithmetic and copies ran while one was open for 9% -> 7% of each run, Pallas kernels for 26% -> 31%
where the time goes in v4:
time: 244 us; the launch traced here: 243 us
  Pallas kernels  80.1 us (33%)
  starting transfers between devices  79.4 us (33%)
  waiting for transfers between devices  54.1 us (22%)
  local copies, waits for them, and re-layouts  23.2 us (10%)
  other arithmetic  3.68 us (2%)
    ppermute x30, starting transfers between devices, move(): return lax.ppermute(value, self.axis, pairs)  52.6 us
    ppermute x30, waiting for transfers between devices, move(): return lax.ppermute(value, self.axis, pairs)  45.5 us
    pallas_call x1, Pallas kernels, image(): pl.pallas_call(functools.partial(image_kernel, bw, len(held)), out_shape=...  20.5 us
    pallas_call x1, Pallas kernels, sums(): pl.pallas_call(functools.partial(sums_kernel, bw), out_shape=[jax.ShapeDt...  20.2 us
    scatter x1, local copies, waits for them, and re-layouts, local(): jnp.zeros((total_count * capacity, 2 * bw), jnp.bfloat16).at[slot]  11.3 us
    all_to_all x1, starting transfers between devices, local(): lax.all_to_all(packed, BOTH, split_axis=0, concat_axis=0, tiled=True)  10.5 us
    pallas_call x4, Pallas kernels, call(): pl.pallas_call(kernel, out_shape=[jax.ShapeDtypeStruct(*shape) for shape...  9.1 us
    unnamed x66, local copies, waits for them, and re-layouts  7.11 us
  transfers between devices with their start and end apart: 34, of which 18 were waited for; matrix products, arithmetic and copies ran while one was open for 7% of the time, Pallas kernels for 31%

profile of v4, /device:TPU:1, one launch (start us, length us, event | category | flops | bytes accessed | tf_op | source)
XLA Modules:
  0.0 242.9 jit_solution(17607925784731552898)
XLA Ops:
  1.3 4.0 %shard_map.181 = s32[2,136,256]{2,1,0:T(8,128)} custom-call(s32[2]{0:T(128)} %pad_add_fusion.at_ref, s32[128]{0:T(128)} %bits_two_ref.5, s32[132]{0:T(256)} %bits_one_ref.5, f32[2048,512]{1,0:T(8,128)} %two_ref.3, f32[2048,512]{1,0:T(8,128)} %one_ref.3, f32[512,512]{1,0:T(8,128)} %inv_two_ref.5, f32[512,512]{1,0:T(8,128)} %inv_one_ref.5), custom_call_target="tpu_custom_call" | custom-call | flops 1 | bytes 1 | tf_op jit(solution)/shard_map/pallas_call | solution.py:88
  5.3 5.2 %collective-permute-start = (s32[2,136,256]{2,1,0:T(8,128)}, s32[2,136,256]{2,1,0:T(8,128)S(1)}, u32[]{:S(2)}, u32[]{:S(2)}) collective-permute-start(s32[2,136,256]{2,1,0:T(8,128)} %shard_map.181), channel_id=1, source_target_pairs={{0,0},{1,1},{2,17},{3,16},{4,32},{5,33},{6,49},{7,48},{8,64},{9,65... | collective-permute-start | bytes 835592 | tf_op jit(solution)/shard_map/ppermute | solution.py:564
  11.4 4.0 %collective-permute-done.refs_0_ = s32[2,136,256]{2,1,0:T(8,128)S(1)} collective-permute-done((s32[2,136,256]{2,1,0:T(8,128)}, s32[2,136,256]{2,1,0:T(8,128)S(1)}, u32[]{:S(2)}, u32[]{:S(2)}) %collective-permute-start) | collective-permute-done | bytes 278560 | tf_op jit(solution)/shard_map/ppermute | solution.py:564
  15.5 4.5 %collective-permute-start.2 = (s32[2,136,256]{2,1,0:T(8,128)S(1)}, s32[2,136,256]{2,1,0:T(8,128)S(1)}, u32[]{:S(2)}, u32[]{:S(2)}) collective-permute-start(s32[2,136,256]{2,1,0:T(8,128)S(1)} %collective-permute-done.refs_0_), channel_id=1, source_target_pairs={{0,32},{16,48},{32,64},{48,80},{64,96},{80,112},{96,0},{112,16},{1... | collective-permute-start | bytes 835592 | tf_op jit(solution)/shard_map/ppermute | solution.py:510
  20.0 7.4 %collective-permute-start.3 = (s32[2,136,256]{2,1,0:T(8,128)S(1)}, s32[2,136,256]{2,1,0:T(8,128)S(1)}, u32[]{:S(2)}, u32[]{:S(2)}) collective-permute-start(s32[2,136,256]{2,1,0:T(8,128)S(1)} %collective-permute-done.refs_0_), channel_id=1, source_target_pairs={{0,64},{16,80},{32,96},{48,112},{64,0},{80,16},{96,32},{112,48},{1... | collective-permute-start | bytes 835592 | tf_op jit(solution)/shard_map/ppermute | solution.py:510
  30.1 11.3 %scatter_custom_fusion = bf16[4096,256]{1,0:T(8,128)(2,1)} fusion(s32[2048]{0:T(1024)S(1)} %get-tuple-element.95, bf16[2048,256]{1,0:T(8,128)(2,1)} %units_ref.1, bf16[]{:T(256)} %constant.14.clone.1), kind=kCustom, calls=%fused_computation.12 | custom fusion | bytes 2097664 | tf_op jit(solution)/shard_map/scatter | solution.py:575
  41.4 10.5 %all-to-all-start = ((bf16[128,32,256]{2,1,0:T(8,128)(2,1)}), bf16[128,32,256]{2,1,0:T(8,128)(2,1)S(1)}, u32[]{:S(2)}, u32[]{:S(2)}) async-start(bf16[128,32,256]{2,1,0:T(8,128)(2,1)} %bitcast.24), calls=%async_computation | async-start | bytes 4194304 | tf_op jit(solution)/shard_map/all_to_all | solution.py:578
  56.6 20.5 %shard_map.182 = (f32[2048,512]{1,0:T(8,128)}, f32[2048,512]{1,0:T(8,128)}, s32[16,312,256]{2,1,0:T(8,128)}) custom-call(s32[2]{0:T(128)} %pad_add_fusion.at_ref, f32[2048,1024]{1,0:T(8,128)} %cov_ref.1, s32[2,136,256]{2,1,0:T(8,128)} %copy-done.3, s32[2,136,256]{2,1,0:T(8,128)} %copy-done.7, s32[2,136,256]{2,1,0:T(8,128)} %copy-done.4, ...), custom_call_target="tpu_custom_call" | custom-call | flops 1 | bytes 1 | tf_op jit(solution)/shard_map/pallas_call | solution.py:165
  77.1 4.6 %all-to-all-done = bf16[128,32,256]{2,1,0:T(8,128)(2,1)S(1)} async-done(((bf16[128,32,256]{2,1,0:T(8,128)(2,1)}), bf16[128,32,256]{2,1,0:T(8,128)(2,1)S(1)}, u32[]{:S(2)}, u32[]{:S(2)}) %all-to-all-start) | async-done | bytes 2097184 | tf_op jit(solution)/shard_map/all_to_all | solution.py:578
  83.0 4.8 %all-to-all-start.1 = ((s32[16,312,256]{2,1,0:T(8,128)}), s32[16,312,256]{2,1,0:T(8,128)}, u32[]{:S(2)}, u32[]{:S(2)}) async-start(s32[16,312,256]{2,1,0:T(8,128)} %get-tuple-element.77), calls=%async_computation.1 | async-start | bytes 10223616 | tf_op jit(solution)/shard_map/all_to_all | solution.py:583
  87.8 20.2 %shard_map.183 = (f32[3,256,512]{2,1,0:T(8,128)}, f32[3,256,512]{2,1,0:T(8,128)}) custom-call(s32[2]{0:T(128)} %pad_add_fusion.at_ref, s32[128]{0:T(128)} %bits_two_ref.5, s32[132]{0:T(256)} %bits_one_ref.5, f32[2048,512]{1,0:T(8,128)} %two_ref.3, f32[2048,512]{1,0:T(8,128)} %one_ref.3, f32[2048,512]{1,0:T(8,128)} %get-tuple-element.54.image_two_ref, ...), custom_call_target="tpu_custom_call" | custom-call | flops 1 | bytes 1 | tf_op jit(solution)/shard_map/pallas_call | solution.py:226
  113.5 3.1 %shard_map.184 = (f32[3,64,512]{2,1,0:T(8,128)}, s32[3,72,256]{2,1,0:T(8,128)}, s32[3,72,256]{2,1,0:T(8,128)}, s32[3,72,256]{2,1,0:T(8,128)}) custom-call(s32[2]{0:T(128)} %pad_add_fusion.at_ref, f32[3,256,512]{2,1,0:T(8,128)} %get-tuple-element.57.own_ref, f32[3,256,512]{2,1,0:T(8,128)} %copy-done.1), custom_call_target="tpu_custom_call" | custom-call | flops 1 | bytes 1 | tf_op jit(solution)/shard_map/pallas_call | solution.py:243
  119.5 5.5 %collective-permute-done.10.refs_1_ = s32[3,72,256]{2,1,0:T(8,128)S(1)} collective-permute-done((s32[3,72,256]{2,1,0:T(8,128)}, s32[3,72,256]{2,1,0:T(8,128)S(1)}, u32[]{:S(2)}, u32[]{:S(2)}) %collective-permute-start.10) | collective-permute-done | bytes 221216 | tf_op jit(solution)/shard_map/ppermute | solution.py:510
  125.0 3.4 %collective-permute-done.11.refs_2_ = s32[3,72,256]{2,1,0:T(8,128)S(1)} collective-permute-done((s32[3,72,256]{2,1,0:T(8,128)}, s32[3,72,256]{2,1,0:T(8,128)S(1)}, u32[]{:S(2)}, u32[]{:S(2)}) %collective-permute-start.11) | collective-permute-done | bytes 221216 | tf_op jit(solution)/shard_map/ppermute | solution.py:510
  138.7 5.9 %shard_map.186 = (f32[2,512,512]{2,1,0:T(8,128)}, f32[512,512]{1,0:T(8,128)}) custom-call(s32[4]{0:T(128)} %slice.15.keep_ref, f32[512,512]{1,0:T(8,128)} %top_rows_ref.1, f32[512,512]{1,0:T(8,128)} %inv_two_ref.5, f32[512,512]{1,0:T(8,128)} %inv_one_ref.5), custom_call_target="tpu_custom_call" | custom-call | flops 1 | bytes 1 | tf_op jit(solution)/shard_map/pallas_call | solution.py:426
  144.6 11.6 %collective-permute-done.12.refs_1_ = f32[3,16,512]{2,1,0:T(8,128)S(1)} collective-permute-done((f32[3,16,512]{2,1,0:T(8,128)}, f32[3,16,512]{2,1,0:T(8,128)S(1)}, u32[]{:S(2)}, u32[]{:S(2)}) %collective-permute-start.12) | collective-permute-done | bytes 98336 | tf_op jit(solution)/shard_map/ppermute | solution.py:510
  156.2 9.9 %collective-permute-done.13.refs_2_ = f32[3,16,512]{2,1,0:T(8,128)S(1)} collective-permute-done((f32[3,16,512]{2,1,0:T(8,128)}, f32[3,16,512]{2,1,0:T(8,128)S(1)}, u32[]{:S(2)}, u32[]{:S(2)}) %collective-permute-start.13) | collective-permute-done | bytes 98336 | tf_op jit(solution)/shard_map/ppermute | solution.py:510
  196.4 7.1 %collective-permute-start.24 = (s32[3,72,256]{2,1,0:T(8,128)}, s32[3,72,256]{2,1,0:T(8,128)S(1)}, u32[]{:S(2)}, u32[]{:S(2)}) collective-permute-start(s32[3,72,256]{2,1,0:T(8,128)} %get-tuple-element.82.refs_0_), channel_id=1, source_target_pairs={{0,16},{16,0},{32,48},{48,32},{64,80},{80,64},{96,112},{112,96},{1... | collective-permute-start | bytes 663560 | tf_op jit(solution)/shard_map/ppermute | solution.py:510
  203.4 4.9 %collective-permute-start.26 = (s32[3,72,256]{2,1,0:T(8,128)S(1)}, s32[3,72,256]{2,1,0:T(8,128)S(1)}, u32[]{:S(2)}, u32[]{:S(2)}) collective-permute-start(s32[3,72,256]{2,1,0:T(8,128)S(1)} %collective-permute-done.25.refs_2_), channel_id=1, source_target_pairs={{0,16},{16,0},{32,48},{48,32},{64,80},{80,64},{96,112},{112,96},{1... | collective-permute-start | bytes 663560 | tf_op jit(solution)/shard_map/ppermute | solution.py:510
  209.2 5.2 %shard_map.189 = (f32[128,512]{1,0:T(8,128)}, f32[128,512]{1,0:T(8,128)}, f32[128,128]{1,0:T(8,128)}, f32[128,128]{1,0:T(8,128)}) custom-call(s32[2]{0:T(128)} %pad_add_fusion.at_ref, s32[128]{0:T(128)} %bits_two_ref.5, s32[132]{0:T(256)} %bits_one_ref.5, s32[128]{0:T(128)} %panel_ref.1, s32[16,312,256]{2,1,0:T(8,128)} %all-to-all-done.1.code_ref, ...), custom_call_target="tpu_custom_call" | custom-call | flops 1 | bytes 1 | tf_op jit(solution)/shard_map/pallas_call | solution.py:360
  214.5 4.6 %shard_map.192 = f32[8,4096]{1,0:T(8,128)} custom-call(bf16[4096,256]{1,0:T(8,128)(2,1)} %bitcast.23, f32[128,128]{1,0:T(8,128)} %get-tuple-element.88.tile_ref, f32[128,128]{1,0:T(8,128)} %get-tuple-element.89.cross_ref), custom_call_target="tpu_custom_call" | custom-call | flops 1 | bytes 1 | tf_op jit(solution)/shard_map/pallas_call | solution.py:461
  220.7 6.3 %all-to-all-start.2 = ((f32[128,1,32]{2,1,0:T(1,128)}), f32[128,1,32]{2,1,0:T(1,128)S(1)}, u32[]{:S(2)}, u32[]{:S(2)}) async-start(f32[128,1,32]{2,1,0:T(1,128)} %bitcast.15), calls=%async_computation.2 | async-start | bytes 131072 | tf_op jit(solution)/shard_map/all_to_all | solution.py:608
  229.3 6.5 %shard_map.190 = (f32[512,512]{1,0:T(8,128)}, f32[512,512]{1,0:T(8,128)}, f32[512,512]{1,0:T(8,128)}) custom-call(s32[2]{0:T(128)} %pad_add_fusion.at_ref, s32[4]{0:T(128)} %slice.15.keep_ref, f32[2,512,512]{2,1,0:T(8,128)} %get-tuple-element.81.gram_ref, f32[512,512]{1,0:T(8,128)} %get-tuple-element.79.top_ref, s32[3,72,256]{2,1,0:T(8,128)} %get-tuple-element.82.refs_0_, ...), custom_call_target="tpu_custom_call" | custom-call | flops 1 | bytes 1 | tf_op jit(solution)/shard_map/pallas_call | solution.py:398
  235.9 4.0 %shard_map.191 = f32[8,2048]{1,0:T(8,128)} custom-call(bf16[2048,256]{1,0:T(8,128)(2,1)} %units_ref.1, s32[2048,1]{1,0:T(8,128)} %copy.25.panel_ref, f32[512,512]{1,0:T(8,128)} %get-tuple-element.47.diag_ref), custom_call_target="tpu_custom_call" | custom-call | flops 1 | bytes 1 | tf_op jit(solution)/shard_map/pallas_call | solution.py:486
  (142 shorter events, 66.8 us)
Async XLA Ops:
  5.3 10.2 %collective-permute-start = (s32[2,136,256]{2,1,0:T(8,128)}, s32[2,136,256]{2,1,0:T(8,128)S(1)}, u32[]{:S(2)}, u32[]{:S(2)}) collective-permute-start(s32[2,136,256]{2,1,0:T(8,128)} %shard_map.181), channel_id=1, source_target_pairs={{0,0},{1,1},{2,17},{3,16},{4,32},{5,33},{6,49},{7,48},{8,64},{9,65... | collective-permute-start | bytes 835592 | tf_op jit(solution)/shard_map/ppermute | solution.py:564
  15.5 26.0 %collective-permute-start.2 = (s32[2,136,256]{2,1,0:T(8,128)S(1)}, s32[2,136,256]{2,1,0:T(8,128)S(1)}, u32[]{:S(2)}, u32[]{:S(2)}) collective-permute-start(s32[2,136,256]{2,1,0:T(8,128)S(1)} %collective-permute-done.refs_0_), channel_id=1, source_target_pairs={{0,32},{16,48},{32,64},{48,80},{64,96},{80,112},{96,0},{112,16},{1... | collective-permute-start | bytes 835592 | tf_op jit(solution)/shard_map/ppermute | solution.py:510
  20.0 21.4 %collective-permute-start.3 = (s32[2,136,256]{2,1,0:T(8,128)S(1)}, s32[2,136,256]{2,1,0:T(8,128)S(1)}, u32[]{:S(2)}, u32[]{:S(2)}) collective-permute-start(s32[2,136,256]{2,1,0:T(8,128)S(1)} %collective-permute-done.refs_0_), channel_id=1, source_target_pairs={{0,64},{16,80},{32,96},{48,112},{64,0},{80,16},{96,32},{112,48},{1... | collective-permute-start | bytes 835592 | tf_op jit(solution)/shard_map/ppermute | solution.py:510
  27.4 14.1 %collective-permute-start.4 = (s32[2,136,256]{2,1,0:T(8,128)S(1)}, s32[2,136,256]{2,1,0:T(8,128)S(1)}, u32[]{:S(2)}, u32[]{:S(2)}) collective-permute-start(s32[2,136,256]{2,1,0:T(8,128)S(1)} %collective-permute-done.refs_0_), channel_id=1, source_target_pairs={{0,96},{16,112},{32,0},{48,16},{64,32},{80,48},{96,64},{112,80},{1... | collective-permute-start | bytes 835592 | tf_op jit(solution)/shard_map/ppermute | solution.py:510
  41.4 40.3 %all-to-all-start = ((bf16[128,32,256]{2,1,0:T(8,128)(2,1)}), bf16[128,32,256]{2,1,0:T(8,128)(2,1)S(1)}, u32[]{:S(2)}, u32[]{:S(2)}) async-start(bf16[128,32,256]{2,1,0:T(8,128)(2,1)} %bitcast.24), calls=%async_computation | async-start | bytes 4194304 | tf_op jit(solution)/shard_map/all_to_all | solution.py:578
  83.0 108.8 %all-to-all-start.1 = ((s32[16,312,256]{2,1,0:T(8,128)}), s32[16,312,256]{2,1,0:T(8,128)}, u32[]{:S(2)}, u32[]{:S(2)}) async-start(s32[16,312,256]{2,1,0:T(8,128)} %get-tuple-element.77), calls=%async_computation.1 | async-start | bytes 10223616 | tf_op jit(solution)/shard_map/all_to_all | solution.py:583
  116.6 8.5 %collective-permute-start.10 = (s32[3,72,256]{2,1,0:T(8,128)}, s32[3,72,256]{2,1,0:T(8,128)S(1)}, u32[]{:S(2)}, u32[]{:S(2)}) collective-permute-start(s32[3,72,256]{2,1,0:T(8,128)} %get-tuple-element.61), channel_id=1, source_target_pairs={{0,64},{16,80},{32,96},{48,112},{64,0},{80,16},{96,32},{112,48},{1... | collective-permute-start | bytes 663560 | tf_op jit(solution)/shard_map/ppermute | solution.py:510
  117.6 10.9 %collective-permute-start.11 = (s32[3,72,256]{2,1,0:T(8,128)}, s32[3,72,256]{2,1,0:T(8,128)S(1)}, u32[]{:S(2)}, u32[]{:S(2)}) collective-permute-start(s32[3,72,256]{2,1,0:T(8,128)} %get-tuple-element.62), channel_id=1, source_target_pairs={{0,96},{16,112},{32,0},{48,16},{64,32},{80,48},{96,64},{112,80},{1... | collective-permute-start | bytes 663560 | tf_op jit(solution)/shard_map/ppermute | solution.py:510
  119.5 11.0 %collective-permute-start.9 = (s32[3,72,256]{2,1,0:T(8,128)}, s32[3,72,256]{2,1,0:T(8,128)S(1)}, u32[]{:S(2)}, u32[]{:S(2)}) collective-permute-start(s32[3,72,256]{2,1,0:T(8,128)} %get-tuple-element.60), channel_id=1, source_target_pairs={{0,32},{16,48},{32,64},{48,80},{64,96},{80,112},{96,0},{112,16},{1... | collective-permute-start | bytes 663560 | tf_op jit(solution)/shard_map/ppermute | solution.py:510
  133.5 22.7 %collective-permute-start.12 = (f32[3,16,512]{2,1,0:T(8,128)}, f32[3,16,512]{2,1,0:T(8,128)S(1)}, u32[]{:S(2)}, u32[]{:S(2)}) collective-permute-start(f32[3,16,512]{2,1,0:T(8,128)} %get-tuple-element.67), channel_id=1, source_target_pairs={{0,1},{1,2},{2,3},{3,0},{4,5},{5,6},{6,7},{7,4},{8,9},{9,10},{10,1... | collective-permute-start | bytes 294920 | tf_op jit(solution)/shard_map/ppermute | solution.py:510
  135.1 31.1 %collective-permute-start.13 = (f32[3,16,512]{2,1,0:T(8,128)}, f32[3,16,512]{2,1,0:T(8,128)S(1)}, u32[]{:S(2)}, u32[]{:S(2)}) collective-permute-start(f32[3,16,512]{2,1,0:T(8,128)} %get-tuple-element.68), channel_id=1, source_target_pairs={{0,2},{1,3},{2,0},{3,1},{4,6},{5,7},{6,4},{7,5},{8,10},{9,11},{10,... | collective-permute-start | bytes 294920 | tf_op jit(solution)/shard_map/ppermute | solution.py:510
  137.5 28.7 %collective-permute-start.14 = (f32[3,16,512]{2,1,0:T(8,128)}, f32[3,16,512]{2,1,0:T(8,128)S(1)}, u32[]{:S(2)}, u32[]{:S(2)}) collective-permute-start(f32[3,16,512]{2,1,0:T(8,128)} %get-tuple-element.69), channel_id=1, source_target_pairs={{0,3},{1,0},{2,1},{3,2},{4,7},{5,4},{6,5},{7,6},{8,11},{9,8},{10,9... | collective-permute-start | bytes 294920 | tf_op jit(solution)/shard_map/ppermute | solution.py:510
  169.2 4.6 %collective-permute-start.15 = (f32[3,16,128]{2,1,0:T(8,128)}, f32[3,16,128]{2,1,0:T(8,128)S(1)}, u32[]{:S(2)}, u32[]{:S(2)}) collective-permute-start(f32[3,16,128]{2,1,0:T(8,128)} %get-tuple-element.71), channel_id=1, source_target_pairs={{0,4},{1,5},{2,6},{3,7},{4,8},{5,9},{6,10},{7,11},{8,12},{9,13},{1... | collective-permute-start | bytes 73736 | tf_op jit(solution)/shard_map/ppermute | solution.py:510
  182.8 5.8 %collective-permute-start.21 = (f32[4,3,16,128]{3,2,1,0:T(8,128)S(1)}, f32[4,3,16,128]{3,2,1,0:T(8,128)S(1)}, u32[]{:S(2)}, u32[]{:S(2)}) collective-permute-start(f32[4,3,16,128]{3,2,1,0:T(8,128)S(1)} %pad_maximum_fusion.refs_0_), channel_id=1, source_target_pairs={{0,1},{1,2},{2,3},{3,0},{4,5},{5,6},{6,7},{7,4},{8,9},{9,10},{10,1... | collective-permute-start | bytes 294920 | tf_op jit(solution)/shard_map/ppermute | solution.py:510
  182.9 5.7 %collective-permute-start.22 = (f32[4,3,16,128]{3,2,1,0:T(8,128)S(1)}, f32[4,3,16,128]{3,2,1,0:T(8,128)S(1)}, u32[]{:S(2)}, u32[]{:S(2)}) collective-permute-start(f32[4,3,16,128]{3,2,1,0:T(8,128)S(1)} %pad_maximum_fusion.refs_0_), channel_id=1, source_target_pairs={{0,2},{1,3},{2,0},{3,1},{4,6},{5,7},{6,4},{7,5},{8,10},{9,11},{10,... | collective-permute-start | bytes 294920 | tf_op jit(solution)/shard_map/ppermute | solution.py:510
  184.4 4.9 %collective-permute-start.23 = (f32[4,3,16,128]{3,2,1,0:T(8,128)S(1)}, f32[4,3,16,128]{3,2,1,0:T(8,128)S(1)}, u32[]{:S(2)}, u32[]{:S(2)}) collective-permute-start(f32[4,3,16,128]{3,2,1,0:T(8,128)S(1)} %pad_maximum_fusion.refs_0_), channel_id=1, source_target_pairs={{0,3},{1,0},{2,1},{3,2},{4,7},{5,4},{6,5},{7,6},{8,11},{9,8},{10,9... | collective-permute-start | bytes 294920 | tf_op jit(solution)/shard_map/ppermute | solution.py:510
  191.8 11.6 %collective-permute-start.25 = (s32[3,72,256]{2,1,0:T(8,128)}, s32[3,72,256]{2,1,0:T(8,128)S(1)}, u32[]{:S(2)}, u32[]{:S(2)}) collective-permute-start(s32[3,72,256]{2,1,0:T(8,128)} %get-tuple-element.82.refs_0_), channel_id=1, source_target_pairs={{0,32},{16,48},{32,64},{48,80},{64,96},{80,112},{96,0},{112,16},{1... | collective-permute-start | bytes 663560 | tf_op jit(solution)/shard_map/ppermute | solution.py:510
  191.9 16.5 %collective-permute-start.27 = (s32[3,72,256]{2,1,0:T(8,128)}, s32[3,72,256]{2,1,0:T(8,128)S(1)}, u32[]{:S(2)}, u32[]{:S(2)}) collective-permute-start(s32[3,72,256]{2,1,0:T(8,128)} %get-tuple-element.82.refs_0_), channel_id=1, source_target_pairs={{0,64},{16,80},{32,96},{48,112},{64,0},{80,16},{96,32},{112,48},{1... | collective-permute-start | bytes 663560 | tf_op jit(solution)/shard_map/ppermute | solution.py:510
  194.6 13.8 %collective-permute-start.29 = (s32[3,72,256]{2,1,0:T(8,128)}, s32[3,72,256]{2,1,0:T(8,128)S(1)}, u32[]{:S(2)}, u32[]{:S(2)}) collective-permute-start(s32[3,72,256]{2,1,0:T(8,128)} %get-tuple-element.82.refs_0_), channel_id=1, source_target_pairs={{0,96},{16,112},{32,0},{48,16},{64,32},{80,48},{96,64},{112,80},{1... | collective-permute-start | bytes 663560 | tf_op jit(solution)/shard_map/ppermute | solution.py:510
  196.4 32.1 %collective-permute-start.24 = (s32[3,72,256]{2,1,0:T(8,128)}, s32[3,72,256]{2,1,0:T(8,128)S(1)}, u32[]{:S(2)}, u32[]{:S(2)}) collective-permute-start(s32[3,72,256]{2,1,0:T(8,128)} %get-tuple-element.82.refs_0_), channel_id=1, source_target_pairs={{0,16},{16,0},{32,48},{48,32},{64,80},{80,64},{96,112},{112,96},{1... | collective-permute-start | bytes 663560 | tf_op jit(solution)/shard_map/ppermute | solution.py:510
  203.4 25.0 %collective-permute-start.26 = (s32[3,72,256]{2,1,0:T(8,128)S(1)}, s32[3,72,256]{2,1,0:T(8,128)S(1)}, u32[]{:S(2)}, u32[]{:S(2)}) collective-permute-start(s32[3,72,256]{2,1,0:T(8,128)S(1)} %collective-permute-done.25.refs_2_), channel_id=1, source_target_pairs={{0,16},{16,0},{32,48},{48,32},{64,80},{80,64},{96,112},{112,96},{1... | collective-permute-start | bytes 663560 | tf_op jit(solution)/shard_map/ppermute | solution.py:510
  208.3 20.1 %collective-permute-start.28 = (s32[3,72,256]{2,1,0:T(8,128)S(1)}, s32[3,72,256]{2,1,0:T(8,128)S(1)}, u32[]{:S(2)}, u32[]{:S(2)}) collective-permute-start(s32[3,72,256]{2,1,0:T(8,128)S(1)} %collective-permute-done.27.refs_4_), channel_id=1, source_target_pairs={{0,16},{16,0},{32,48},{48,32},{64,80},{80,64},{96,112},{112,96},{1... | collective-permute-start | bytes 663560 | tf_op jit(solution)/shard_map/ppermute | solution.py:510
  208.4 20.0 %collective-permute-start.30 = (s32[3,72,256]{2,1,0:T(8,128)S(1)}, s32[3,72,256]{2,1,0:T(8,128)S(1)}, u32[]{:S(2)}, u32[]{:S(2)}) collective-permute-start(s32[3,72,256]{2,1,0:T(8,128)S(1)} %collective-permute-done.29.refs_6_), channel_id=1, source_target_pairs={{0,16},{16,0},{32,48},{48,32},{64,80},{80,64},{96,112},{112,96},{1... | collective-permute-start | bytes 663560 | tf_op jit(solution)/shard_map/ppermute | solution.py:510
  220.7 20.1 %all-to-all-start.2 = ((f32[128,1,32]{2,1,0:T(1,128)}), f32[128,1,32]{2,1,0:T(1,128)S(1)}, u32[]{:S(2)}, u32[]{:S(2)}) async-start(f32[128,1,32]{2,1,0:T(1,128)} %bitcast.15), calls=%async_computation.2 | async-start | bytes 131072 | tf_op jit(solution)/shard_map/all_to_all | solution.py:608
  (43 other events, 230.6 us)

commit v5 on v4

--- a/solution.py
+++ b/solution.py
@@ -293,40 +293,35 @@
 
 
 def fold_y_kernel(at_ref, *refs):
-    parts, outs, total_ref = refs[:4], refs[4:8], refs[8]
-    total_ref[...] = (parts[0][...] + parts[1][...]) + (parts[2][...] + parts[3][...])
-    size = outs[0].shape[2]
-    for step, ref in enumerate(outs):
-        ref[...] = total_ref[:, :, part_of(at_ref[1] // 4, step, size)]
+    parts, (out_ref, held_ref) = refs[:4], refs[4:]
+    for dy, ref in enumerate(parts):
+        held_ref[lax.rem(at_ref[1] // 4 + 4 - dy, 4)] = ref[...]
+    out_ref[...] = (held_ref[0] + held_ref[1]) + (held_ref[2] + held_ref[3])
 
 
 def fold_y(at, parts):
-    count, size, width = parts[0].shape
-    part, whole = ((count, size, width // 4), jnp.float32), ((count, size, width), jnp.float32)
-    return call(fold_y_kernel, at, parts, [part] * 4 + [whole])[:4]
+    shape = parts[0].shape
+    return call(
+        fold_y_kernel, at, parts, [(shape, jnp.float32), ((4, *shape), jnp.float32)]
+    )[0]
 
 
 def unfold_kernel(at_ref, *refs):
     parts, (code_ref, total_ref) = refs[:4], refs[4:]
-    size, lanes = parts[0].shape[2:]
+    size = parts[0].shape[1]
     for dx, ref in enumerate(parts):
-        for dy in range(4):
-            total_ref[
-                :,
-                part_of(lax.rem(at_ref[1], 4) + 4, -dx, size),
-                part_of(at_ref[1] // 4 + 4, -dy, lanes),
-            ] = ref[dy]
+        total_ref[:, part_of(lax.rem(at_ref[1], 4) + 4, -dx, size), :] = ref[...]
     for i in range(3):
         encode(total_ref[i], code_ref, i)
 
 
 def unfold(at, parts):
-    _, count, size, lanes = parts[0].shape
+    count, size, width = parts[0].shape
     return call(
         unfold_kernel, at, parts,
         [
-            ((count, 4 * size + 8, 2 * lanes), jnp.int32),
-            ((count, 4 * size, 4 * lanes), jnp.float32),
+            ((count, 4 * size + 8, width // 2), jnp.int32),
+            ((count, 4 * size, width), jnp.float32),
         ],
     )[0]
 
@@ -563,18 +558,21 @@
     part, blocks = lax.optimization_barrier((part, blocks))
     part = lax.ppermute(part, BOTH, spread_pairs(row_count, col_count))
 
-    held = []
-    for step in range(4):
-        piece = ring_z.move(part, step) if step else part
-        held += [piece, core.move(piece, 1)]
-
     capacity = 2 * loadings.shape[0] // total_count
     hits = (blocks[:, None] == jnp.arange(total_count, dtype=jnp.int32)[None, :]).astype(jnp.int32)
     rank = jnp.sum(jnp.cumsum(hits, axis=0) * hits, axis=1) - 1
     slot = blocks * capacity + rank
     packed = jnp.zeros((total_count * capacity, 2 * bw), jnp.bfloat16).at[slot].set(loadings)
     packed = packed.reshape(total_count, capacity, 2 * bw)
-    packed, held[2], held[4], held[6] = lax.optimization_barrier((packed, held[2], held[4], held[6]))
+    part, packed = lax.optimization_barrier((part, packed))
+    held = []
+    for step in range(4):
+        piece = ring_z.move(part, step) if step else part
+        held += [piece, core.move(piece, 1)]
+
+    packed, held[2], held[4], held[6] = lax.optimization_barrier(
+        (packed, held[2], held[4], held[6])
+    )
     units = lax.all_to_all(packed, BOTH, split_axis=0, concat_axis=0, tiled=True)
     units = units.reshape(total_count * capacity, 2 * bw)
 
@@ -591,20 +589,21 @@
     mine, *codes = fold_z(at, keep, core.move(give, 1))
     mine, *parts = fold_x(at, mine, ring_z.others(codes))
     mine, norm_top = lax.optimization_barrier((mine, norm_top))
-    mine, *parts = fold_y(at, [mine, *ring_x.others(parts)])
     total = mine
-    for part in ring_y.others(parts):
+    for part in ring_x.others(parts):
         total = total + part
-    total = jnp.stack([total, *ring_y.others([total] * 3)])
-    total = unfold(at, [total, *ring_x.others([total] * 3)])
     total, code = lax.optimization_barrier((total, code))
+    total = fold_y(at, [total, *ring_y.others([total] * 3)])
+    cov_two, cov_one, cross, tile = rows(
+        at, pattern_two, pattern_one, block_panel, code, norm_top, bw
+    )
+    value = forms(units, tile, cross)[0].reshape(total_count, capacity)
+    total, value = lax.optimization_barrier((total, value))
+    parts = [total, *ring_x.others([total] * 3)]
+    total = unfold(at, parts)
     whole = []
     for piece in [total, *ring_z.others([total] * 3)]:
         whole += [piece, core.move(piece, 1)]
-    cov_two, cov_one, cross, tile = rows(
-        at, pattern_two, pattern_one, block_panel, code, norm_top, bw
-    )
-    value = forms(units, tile, cross)[0].reshape(total_count, capacity)
     returned = lax.all_to_all(value, BOTH, split_axis=0, concat_axis=0, tiled=True)
     diag_two, top_cov, diag_one = small(at, whole, gram, norm_top, bits_top)
     own_panel = jnp.sum(hits * block_panel[None, :], axis=1, keepdims=True)

time: 244 us -> 231 us (0.947)
  starting transfers between devices: 79.4 us -> 65.9 us
    ppermute x30 -> x27, starting transfers between devices: 52.6 us -> 40.6 us  [move(): return lax.ppermute(value, self.axis, pairs)]
    ppermute x30 -> x27, waiting for transfers between devices: 45.5 us -> 50.5 us  [move(): return lax.ppermute(value, self.axis, pairs)]
    ppermute x1, waiting for transfers between devices: 4.03 us -> 0.01 us  [local(): part = lax.ppermute(part, BOTH, spread_pairs(row_count, col_count))]
    unnamed x66 -> x68, local copies, waits for them, and re-layouts: 7.11 us -> 7.28 us
  transfers between devices with their start and end apart: 34 -> 31, of which waited for: 18 -> 16; matrix products, arithmetic and copies ran while one was open for 7% -> 8% of each run, Pallas kernels for 31% -> 32%
where the time goes in v5:
time: 231 us; the launch traced here: 230 us
  Pallas kernels  80.2 us (35%)
  starting transfers between devices  65.9 us (29%)
  waiting for transfers between devices  55.2 us (24%)
  local copies, waits for them, and re-layouts  23.4 us (10%)
  other arithmetic  2.92 us (1%)
    ppermute x27, waiting for transfers between devices, move(): return lax.ppermute(value, self.axis, pairs)  50.5 us
    ppermute x27, starting transfers between devices, move(): return lax.ppermute(value, self.axis, pairs)  40.6 us
    pallas_call x1, Pallas kernels, image(): pl.pallas_call(functools.partial(image_kernel, bw, len(held)), out_shape=...  20.5 us
    pallas_call x1, Pallas kernels, sums(): pl.pallas_call(functools.partial(sums_kernel, bw), out_shape=[jax.ShapeDt...  20.2 us
    scatter x1, local copies, waits for them, and re-layouts, local(): jnp.zeros((total_count * capacity, 2 * bw), jnp.bfloat16).at[slot]  11.2 us
    all_to_all x1, starting transfers between devices, local(): lax.all_to_all(packed, BOTH, split_axis=0, concat_axis=0, tiled=True)  9.77 us
    pallas_call x4, Pallas kernels, call(): pl.pallas_call(kernel, out_shape=[jax.ShapeDtypeStruct(*shape) for shape...  9.2 us
    unnamed x68, local copies, waits for them, and re-layouts  7.28 us
  transfers between devices with their start and end apart: 31, of which 16 were waited for; matrix products, arithmetic and copies ran while one was open for 8% of the time, Pallas kernels for 32%

profile of v5, /device:TPU:1, one launch (start us, length us, event | category | flops | bytes accessed | tf_op | source)
XLA Modules:
  0.0 229.8 jit_solution(7634739093793236142)
XLA Ops:
  1.3 4.0 %shard_map.181 = s32[2,136,256]{2,1,0:T(8,128)} custom-call(s32[2]{0:T(128)} %pad_add_fusion.at_ref, s32[128]{0:T(128)} %bits_two_ref.5, s32[132]{0:T(256)} %bits_one_ref.5, f32[2048,512]{1,0:T(8,128)} %two_ref.3, f32[2048,512]{1,0:T(8,128)} %one_ref.3, f32[512,512]{1,0:T(8,128)} %inv_two_ref.5, f32[512,512]{1,0:T(8,128)} %inv_one_ref.5), custom_call_target="tpu_custom_call" | custom-call | flops 1 | bytes 1 | tf_op jit(solution)/shard_map/pallas_call | solution.py:88
  5.2 5.2 %collective-permute-start = (s32[2,136,256]{2,1,0:T(8,128)}, s32[2,136,256]{2,1,0:T(8,128)S(1)}, u32[]{:S(2)}, u32[]{:S(2)}) collective-permute-start(s32[2,136,256]{2,1,0:T(8,128)} %shard_map.181), channel_id=1, source_target_pairs={{0,0},{1,1},{2,17},{3,16},{4,32},{5,33},{6,49},{7,48},{8,64},{9,65... | collective-permute-start | bytes 835592 | tf_op jit(solution)/shard_map/ppermute | solution.py:559
  12.7 11.2 %scatter_custom_fusion = bf16[4096,256]{1,0:T(8,128)(2,1)} fusion(s32[2048]{0:T(1024)S(1)} %get-tuple-element.97, bf16[2048,256]{1,0:T(8,128)(2,1)} %units_ref.1, bf16[]{:T(256)} %constant.14.clone.1), kind=kCustom, calls=%fused_computation.12 | custom fusion | bytes 2097664 | tf_op jit(solution)/shard_map/scatter | solution.py:565
  26.2 3.8 %collective-permute-start.3 = (s32[2,136,256]{2,1,0:T(8,128)S(1)}, s32[2,136,256]{2,1,0:T(8,128)S(1)}, u32[]{:S(2)}, u32[]{:S(2)}) collective-permute-start(s32[2,136,256]{2,1,0:T(8,128)S(1)} %collective-permute-done.refs_0_), channel_id=1, source_target_pairs={{0,64},{16,80},{32,96},{48,112},{64,0},{80,16},{96,32},{112,48},{1... | collective-permute-start | bytes 835592 | tf_op jit(solution)/shard_map/ppermute | solution.py:505
  33.2 6.6 %collective-permute-done.3.refs_4_ = s32[2,136,256]{2,1,0:T(8,128)S(1)} collective-permute-done((s32[2,136,256]{2,1,0:T(8,128)S(1)}, s32[2,136,256]{2,1,0:T(8,128)S(1)}, u32[]{:S(2)}, u32[]{:S(2)}) %collective-permute-start.3) | collective-permute-done | bytes 278560 | tf_op jit(solution)/shard_map/ppermute | solution.py:505
  41.0 9.8 %all-to-all-start = ((bf16[128,32,256]{2,1,0:T(8,128)(2,1)}), bf16[128,32,256]{2,1,0:T(8,128)(2,1)S(1)}, u32[]{:S(2)}, u32[]{:S(2)}) async-start(bf16[128,32,256]{2,1,0:T(8,128)(2,1)} %bitcast.22), calls=%async_computation | async-start | bytes 4194304 | tf_op jit(solution)/shard_map/all_to_all | solution.py:576
  55.3 20.5 %shard_map.182 = (f32[2048,512]{1,0:T(8,128)}, f32[2048,512]{1,0:T(8,128)}, s32[16,312,256]{2,1,0:T(8,128)}) custom-call(s32[2]{0:T(128)} %pad_add_fusion.at_ref, f32[2048,1024]{1,0:T(8,128)} %cov_ref.1, s32[2,136,256]{2,1,0:T(8,128)} %copy-done.3, s32[2,136,256]{2,1,0:T(8,128)} %copy-done.7, s32[2,136,256]{2,1,0:T(8,128)} %copy-done.4, ...), custom_call_target="tpu_custom_call" | custom-call | flops 1 | bytes 1 | tf_op jit(solution)/shard_map/pallas_call | solution.py:165
  75.8 4.6 %all-to-all-done = bf16[128,32,256]{2,1,0:T(8,128)(2,1)S(1)} async-done(((bf16[128,32,256]{2,1,0:T(8,128)(2,1)}), bf16[128,32,256]{2,1,0:T(8,128)(2,1)S(1)}, u32[]{:S(2)}, u32[]{:S(2)}) %all-to-all-start) | async-done | bytes 2097184 | tf_op jit(solution)/shard_map/all_to_all | solution.py:576
  81.8 4.8 %all-to-all-start.1 = ((s32[16,312,256]{2,1,0:T(8,128)}), s32[16,312,256]{2,1,0:T(8,128)}, u32[]{:S(2)}, u32[]{:S(2)}) async-start(s32[16,312,256]{2,1,0:T(8,128)} %get-tuple-element.75), calls=%async_computation.1 | async-start | bytes 10223616 | tf_op jit(solution)/shard_map/all_to_all | solution.py:581
  86.5 20.2 %shard_map.183 = (f32[3,256,512]{2,1,0:T(8,128)}, f32[3,256,512]{2,1,0:T(8,128)}) custom-call(s32[2]{0:T(128)} %pad_add_fusion.at_ref, s32[128]{0:T(128)} %bits_two_ref.5, s32[132]{0:T(256)} %bits_one_ref.5, f32[2048,512]{1,0:T(8,128)} %two_ref.3, f32[2048,512]{1,0:T(8,128)} %one_ref.3, f32[2048,512]{1,0:T(8,128)} %get-tuple-element.57.image_two_ref, ...), custom_call_target="tpu_custom_call" | custom-call | flops 1 | bytes 1 | tf_op jit(solution)/shard_map/pallas_call | solution.py:226
  112.2 3.1 %shard_map.184 = (f32[3,64,512]{2,1,0:T(8,128)}, s32[3,72,256]{2,1,0:T(8,128)}, s32[3,72,256]{2,1,0:T(8,128)}, s32[3,72,256]{2,1,0:T(8,128)}) custom-call(s32[2]{0:T(128)} %pad_add_fusion.at_ref, f32[3,256,512]{2,1,0:T(8,128)} %get-tuple-element.60.own_ref, f32[3,256,512]{2,1,0:T(8,128)} %copy-done.1), custom_call_target="tpu_custom_call" | custom-call | flops 1 | bytes 1 | tf_op jit(solution)/shard_map/pallas_call | solution.py:243
  118.3 5.5 %collective-permute-done.10.refs_1_ = s32[3,72,256]{2,1,0:T(8,128)S(1)} collective-permute-done((s32[3,72,256]{2,1,0:T(8,128)}, s32[3,72,256]{2,1,0:T(8,128)S(1)}, u32[]{:S(2)}, u32[]{:S(2)}) %collective-permute-start.10) | collective-permute-done | bytes 221216 | tf_op jit(solution)/shard_map/ppermute | solution.py:505
  123.8 3.4 %collective-permute-done.11.refs_2_ = s32[3,72,256]{2,1,0:T(8,128)S(1)} collective-permute-done((s32[3,72,256]{2,1,0:T(8,128)}, s32[3,72,256]{2,1,0:T(8,128)S(1)}, u32[]{:S(2)}, u32[]{:S(2)}) %collective-permute-start.11) | collective-permute-done | bytes 221216 | tf_op jit(solution)/shard_map/ppermute | solution.py:505
  137.4 5.9 %shard_map.186 = (f32[2,512,512]{2,1,0:T(8,128)}, f32[512,512]{1,0:T(8,128)}) custom-call(s32[4]{0:T(128)} %slice.15.keep_ref, f32[512,512]{1,0:T(8,128)} %top_rows_ref.1, f32[512,512]{1,0:T(8,128)} %inv_two_ref.5, f32[512,512]{1,0:T(8,128)} %inv_one_ref.5), custom_call_target="tpu_custom_call" | custom-call | flops 1 | bytes 1 | tf_op jit(solution)/shard_map/pallas_call | solution.py:421
  143.3 11.7 %collective-permute-done.12 = f32[3,16,512]{2,1,0:T(8,128)S(1)} collective-permute-done((f32[3,16,512]{2,1,0:T(8,128)}, f32[3,16,512]{2,1,0:T(8,128)S(1)}, u32[]{:S(2)}, u32[]{:S(2)}) %collective-permute-start.12) | collective-permute-done | bytes 98336 | tf_op jit(solution)/shard_map/ppermute | solution.py:505
  154.9 9.9 %collective-permute-done.13 = f32[3,16,512]{2,1,0:T(8,128)S(1)} collective-permute-done((f32[3,16,512]{2,1,0:T(8,128)}, f32[3,16,512]{2,1,0:T(8,128)S(1)}, u32[]{:S(2)}, u32[]{:S(2)}) %collective-permute-start.13) | collective-permute-done | bytes 98336 | tf_op jit(solution)/shard_map/ppermute | solution.py:505
  169.6 5.2 %shard_map.187 = (f32[128,512]{1,0:T(8,128)}, f32[128,512]{1,0:T(8,128)}, f32[128,128]{1,0:T(8,128)}, f32[128,128]{1,0:T(8,128)}) custom-call(s32[2]{0:T(128)} %pad_add_fusion.at_ref, s32[128]{0:T(128)} %bits_two_ref.5, s32[132]{0:T(256)} %bits_one_ref.5, s32[128]{0:T(128)} %panel_ref.1, s32[16,312,256]{2,1,0:T(8,128)} %all-to-all-done.1.code_ref, ...), custom_call_target="tpu_custom_call" | custom-call | flops 1 | bytes 1 | tf_op jit(solution)/shard_map/pallas_call | solution.py:355
  174.8 4.6 %shard_map.189 = f32[8,4096]{1,0:T(8,128)} custom-call(bf16[4096,256]{1,0:T(8,128)(2,1)} %bitcast.21, f32[128,128]{1,0:T(8,128)} %get-tuple-element.83.tile_ref, f32[128,128]{1,0:T(8,128)} %get-tuple-element.84.cross_ref), custom_call_target="tpu_custom_call" | custom-call | flops 1 | bytes 1 | tf_op jit(solution)/shard_map/pallas_call | solution.py:456
  186.9 3.3 %collective-permute-done.18.refs_1_ = f32[3,16,512]{2,1,0:T(8,128)S(1)} collective-permute-done((f32[3,16,512]{2,1,0:T(8,128)}, f32[3,16,512]{2,1,0:T(8,128)S(1)}, u32[]{:S(2)}, u32[]{:S(2)}) %collective-permute-start.18) | collective-permute-done | bytes 98336 | tf_op jit(solution)/shard_map/ppermute | solution.py:505
  193.4 2.8 %collective-permute-start.24 = (s32[3,72,256]{2,1,0:T(8,128)}, s32[3,72,256]{2,1,0:T(8,128)S(1)}, u32[]{:S(2)}, u32[]{:S(2)}) collective-permute-start(s32[3,72,256]{2,1,0:T(8,128)} %get-tuple-element.86.refs_0_), channel_id=1, source_target_pairs={{0,64},{16,80},{32,96},{48,112},{64,0},{80,16},{96,32},{112,48},{1... | collective-permute-start | bytes 663560 | tf_op jit(solution)/shard_map/ppermute | solution.py:505
  198.1 4.5 %collective-permute-start.21 = (s32[3,72,256]{2,1,0:T(8,128)}, s32[3,72,256]{2,1,0:T(8,128)S(1)}, u32[]{:S(2)}, u32[]{:S(2)}) collective-permute-start(s32[3,72,256]{2,1,0:T(8,128)} %get-tuple-element.86.refs_0_), channel_id=1, source_target_pairs={{0,16},{16,0},{32,48},{48,32},{64,80},{80,64},{96,112},{112,96},{1... | collective-permute-start | bytes 663560 | tf_op jit(solution)/shard_map/ppermute | solution.py:505
  208.4 5.5 %all-to-all-start.2 = ((f32[128,1,32]{2,1,0:T(1,128)}), f32[128,1,32]{2,1,0:T(1,128)S(1)}, u32[]{:S(2)}, u32[]{:S(2)}) async-start(f32[128,1,32]{2,1,0:T(1,128)} %bitcast.12), calls=%async_computation.2 | async-start | bytes 131072 | tf_op jit(solution)/shard_map/all_to_all | solution.py:607
  216.3 6.5 %shard_map.191 = (f32[512,512]{1,0:T(8,128)}, f32[512,512]{1,0:T(8,128)}, f32[512,512]{1,0:T(8,128)}) custom-call(s32[2]{0:T(128)} %pad_add_fusion.at_ref, s32[4]{0:T(128)} %slice.15.keep_ref, f32[2,512,512]{2,1,0:T(8,128)} %get-tuple-element.79.gram_ref, f32[512,512]{1,0:T(8,128)} %get-tuple-element.77.top_ref, s32[3,72,256]{2,1,0:T(8,128)} %get-tuple-element.86.refs_0_, ...), custom_call_target="tpu_custom_call" | custom-call | flops 1 | bytes 1 | tf_op jit(solution)/shard_map/pallas_call | solution.py:393
  222.8 4.0 %shard_map.192 = f32[8,2048]{1,0:T(8,128)} custom-call(bf16[2048,256]{1,0:T(8,128)(2,1)} %units_ref.1, s32[2048,1]{1,0:T(8,128)} %copy.25.panel_ref, f32[512,512]{1,0:T(8,128)} %get-tuple-element.48.diag_ref), custom_call_target="tpu_custom_call" | custom-call | flops 1 | bytes 1 | tf_op jit(solution)/shard_map/pallas_call | solution.py:481
  (137 shorter events, 62.2 us)
Async XLA Ops:
  5.2 18.7 %collective-permute-start = (s32[2,136,256]{2,1,0:T(8,128)}, s32[2,136,256]{2,1,0:T(8,128)S(1)}, u32[]{:S(2)}, u32[]{:S(2)}) collective-permute-start(s32[2,136,256]{2,1,0:T(8,128)} %shard_map.181), channel_id=1, source_target_pairs={{0,0},{1,1},{2,17},{3,16},{4,32},{5,33},{6,49},{7,48},{8,64},{9,65... | collective-permute-start | bytes 835592 | tf_op jit(solution)/shard_map/ppermute | solution.py:559
  24.0 9.2 %collective-permute-start.2 = (s32[2,136,256]{2,1,0:T(8,128)S(1)}, s32[2,136,256]{2,1,0:T(8,128)S(1)}, u32[]{:S(2)}, u32[]{:S(2)}) collective-permute-start(s32[2,136,256]{2,1,0:T(8,128)S(1)} %collective-permute-done.refs_0_), channel_id=1, source_target_pairs={{0,32},{16,48},{32,64},{48,80},{64,96},{80,112},{96,0},{112,16},{1... | collective-permute-start | bytes 835592 | tf_op jit(solution)/shard_map/ppermute | solution.py:505
  26.2 13.6 %collective-permute-start.3 = (s32[2,136,256]{2,1,0:T(8,128)S(1)}, s32[2,136,256]{2,1,0:T(8,128)S(1)}, u32[]{:S(2)}, u32[]{:S(2)}) collective-permute-start(s32[2,136,256]{2,1,0:T(8,128)S(1)} %collective-permute-done.refs_0_), channel_id=1, source_target_pairs={{0,64},{16,80},{32,96},{48,112},{64,0},{80,16},{96,32},{112,48},{1... | collective-permute-start | bytes 835592 | tf_op jit(solution)/shard_map/ppermute | solution.py:505
  30.0 11.0 %collective-permute-start.4 = (s32[2,136,256]{2,1,0:T(8,128)S(1)}, s32[2,136,256]{2,1,0:T(8,128)S(1)}, u32[]{:S(2)}, u32[]{:S(2)}) collective-permute-start(s32[2,136,256]{2,1,0:T(8,128)S(1)} %collective-permute-done.refs_0_), channel_id=1, source_target_pairs={{0,96},{16,112},{32,0},{48,16},{64,32},{80,48},{96,64},{112,80},{1... | collective-permute-start | bytes 835592 | tf_op jit(solution)/shard_map/ppermute | solution.py:505
  41.0 39.5 %all-to-all-start = ((bf16[128,32,256]{2,1,0:T(8,128)(2,1)}), bf16[128,32,256]{2,1,0:T(8,128)(2,1)S(1)}, u32[]{:S(2)}, u32[]{:S(2)}) async-start(bf16[128,32,256]{2,1,0:T(8,128)(2,1)} %bitcast.22), calls=%async_computation | async-start | bytes 4194304 | tf_op jit(solution)/shard_map/all_to_all | solution.py:576
  81.8 83.2 %all-to-all-start.1 = ((s32[16,312,256]{2,1,0:T(8,128)}), s32[16,312,256]{2,1,0:T(8,128)}, u32[]{:S(2)}, u32[]{:S(2)}) async-start(s32[16,312,256]{2,1,0:T(8,128)} %get-tuple-element.75), calls=%async_computation.1 | async-start | bytes 10223616 | tf_op jit(solution)/shard_map/all_to_all | solution.py:581
  115.3 8.5 %collective-permute-start.10 = (s32[3,72,256]{2,1,0:T(8,128)}, s32[3,72,256]{2,1,0:T(8,128)S(1)}, u32[]{:S(2)}, u32[]{:S(2)}) collective-permute-start(s32[3,72,256]{2,1,0:T(8,128)} %get-tuple-element.64), channel_id=1, source_target_pairs={{0,64},{16,80},{32,96},{48,112},{64,0},{80,16},{96,32},{112,48},{1... | collective-permute-start | bytes 663560 | tf_op jit(solution)/shard_map/ppermute | solution.py:505
  116.3 10.9 %collective-permute-start.11 = (s32[3,72,256]{2,1,0:T(8,128)}, s32[3,72,256]{2,1,0:T(8,128)S(1)}, u32[]{:S(2)}, u32[]{:S(2)}) collective-permute-start(s32[3,72,256]{2,1,0:T(8,128)} %get-tuple-element.65), channel_id=1, source_target_pairs={{0,96},{16,112},{32,0},{48,16},{64,32},{80,48},{96,64},{112,80},{1... | collective-permute-start | bytes 663560 | tf_op jit(solution)/shard_map/ppermute | solution.py:505
  118.3 10.9 %collective-permute-start.9 = (s32[3,72,256]{2,1,0:T(8,128)}, s32[3,72,256]{2,1,0:T(8,128)S(1)}, u32[]{:S(2)}, u32[]{:S(2)}) collective-permute-start(s32[3,72,256]{2,1,0:T(8,128)} %get-tuple-element.63), channel_id=1, source_target_pairs={{0,32},{16,48},{32,64},{48,80},{64,96},{80,112},{96,0},{112,16},{1... | collective-permute-start | bytes 663560 | tf_op jit(solution)/shard_map/ppermute | solution.py:505
  132.2 22.7 %collective-permute-start.12 = (f32[3,16,512]{2,1,0:T(8,128)}, f32[3,16,512]{2,1,0:T(8,128)S(1)}, u32[]{:S(2)}, u32[]{:S(2)}) collective-permute-start(f32[3,16,512]{2,1,0:T(8,128)} %get-tuple-element.70), channel_id=1, source_target_pairs={{0,1},{1,2},{2,3},{3,0},{4,5},{5,6},{6,7},{7,4},{8,9},{9,10},{10,1... | collective-permute-start | bytes 294920 | tf_op jit(solution)/shard_map/ppermute | solution.py:505
  133.8 31.1 %collective-permute-start.13 = (f32[3,16,512]{2,1,0:T(8,128)}, f32[3,16,512]{2,1,0:T(8,128)S(1)}, u32[]{:S(2)}, u32[]{:S(2)}) collective-permute-start(f32[3,16,512]{2,1,0:T(8,128)} %get-tuple-element.71), channel_id=1, source_target_pairs={{0,2},{1,3},{2,0},{3,1},{4,6},{5,7},{6,4},{7,5},{8,10},{9,11},{10,... | collective-permute-start | bytes 294920 | tf_op jit(solution)/shard_map/ppermute | solution.py:505
  136.2 28.7 %collective-permute-start.14 = (f32[3,16,512]{2,1,0:T(8,128)}, f32[3,16,512]{2,1,0:T(8,128)S(1)}, u32[]{:S(2)}, u32[]{:S(2)}) collective-permute-start(f32[3,16,512]{2,1,0:T(8,128)} %get-tuple-element.72), channel_id=1, source_target_pairs={{0,3},{1,0},{2,1},{3,2},{4,7},{5,4},{6,5},{7,6},{8,11},{9,8},{10,9... | collective-permute-start | bytes 294920 | tf_op jit(solution)/shard_map/ppermute | solution.py:505
  165.0 16.1 %collective-permute-start.15 = (f32[3,16,512]{2,1,0:T(8,128)S(1)}, f32[3,16,512]{2,1,0:T(8,128)S(1)}, u32[]{:S(2)}, u32[]{:S(2)}) collective-permute-start(f32[3,16,512]{2,1,0:T(8,128)S(1)} %add_add_fusion.refs_0_), channel_id=1, source_target_pairs={{0,4},{1,5},{2,6},{3,7},{4,8},{5,9},{6,10},{7,11},{8,12},{9,13},{1... | collective-permute-start | bytes 294920 | tf_op jit(solution)/shard_map/ppermute | solution.py:505
  165.0 16.0 %collective-permute-start.16 = (f32[3,16,512]{2,1,0:T(8,128)S(1)}, f32[3,16,512]{2,1,0:T(8,128)S(1)}, u32[]{:S(2)}, u32[]{:S(2)}) collective-permute-start(f32[3,16,512]{2,1,0:T(8,128)S(1)} %add_add_fusion.refs_0_), channel_id=1, source_target_pairs={{0,8},{1,9},{2,10},{3,11},{4,12},{5,13},{6,14},{7,15},{8,0},{9,1},... | collective-permute-start | bytes 294920 | tf_op jit(solution)/shard_map/ppermute | solution.py:505
  167.6 13.5 %collective-permute-start.17 = (f32[3,16,512]{2,1,0:T(8,128)S(1)}, f32[3,16,512]{2,1,0:T(8,128)S(1)}, u32[]{:S(2)}, u32[]{:S(2)}) collective-permute-start(f32[3,16,512]{2,1,0:T(8,128)S(1)} %add_add_fusion.refs_0_), channel_id=1, source_target_pairs={{0,12},{1,13},{2,14},{3,15},{4,0},{5,1},{6,2},{7,3},{8,4},{9,5},{1... | collective-permute-start | bytes 294920 | tf_op jit(solution)/shard_map/ppermute | solution.py:505
  184.2 5.9 %collective-permute-start.19 = (f32[3,16,512]{2,1,0:T(8,128)}, f32[3,16,512]{2,1,0:T(8,128)S(1)}, u32[]{:S(2)}, u32[]{:S(2)}) collective-permute-start(f32[3,16,512]{2,1,0:T(8,128)} %get-tuple-element.85.refs_0_), channel_id=1, source_target_pairs={{0,2},{1,3},{2,0},{3,1},{4,6},{5,7},{6,4},{7,5},{8,10},{9,11},{10,... | collective-permute-start | bytes 294920 | tf_op jit(solution)/shard_map/ppermute | solution.py:505
  193.4 9.2 %collective-permute-start.22 = (s32[3,72,256]{2,1,0:T(8,128)}, s32[3,72,256]{2,1,0:T(8,128)S(1)}, u32[]{:S(2)}, u32[]{:S(2)}) collective-permute-start(s32[3,72,256]{2,1,0:T(8,128)} %get-tuple-element.86.refs_0_), channel_id=1, source_target_pairs={{0,32},{16,48},{32,64},{48,80},{64,96},{80,112},{96,0},{112,16},{1... | collective-permute-start | bytes 663560 | tf_op jit(solution)/shard_map/ppermute | solution.py:505
  193.4 11.8 %collective-permute-start.24 = (s32[3,72,256]{2,1,0:T(8,128)}, s32[3,72,256]{2,1,0:T(8,128)S(1)}, u32[]{:S(2)}, u32[]{:S(2)}) collective-permute-start(s32[3,72,256]{2,1,0:T(8,128)} %get-tuple-element.86.refs_0_), channel_id=1, source_target_pairs={{0,64},{16,80},{32,96},{48,112},{64,0},{80,16},{96,32},{112,48},{1... | collective-permute-start | bytes 663560 | tf_op jit(solution)/shard_map/ppermute | solution.py:505
  196.2 11.4 %collective-permute-start.26 = (s32[3,72,256]{2,1,0:T(8,128)}, s32[3,72,256]{2,1,0:T(8,128)S(1)}, u32[]{:S(2)}, u32[]{:S(2)}) collective-permute-start(s32[3,72,256]{2,1,0:T(8,128)} %get-tuple-element.86.refs_0_), channel_id=1, source_target_pairs={{0,96},{16,112},{32,0},{48,16},{64,32},{80,48},{96,64},{112,80},{1... | collective-permute-start | bytes 663560 | tf_op jit(solution)/shard_map/ppermute | solution.py:505
  198.1 17.3 %collective-permute-start.21 = (s32[3,72,256]{2,1,0:T(8,128)}, s32[3,72,256]{2,1,0:T(8,128)S(1)}, u32[]{:S(2)}, u32[]{:S(2)}) collective-permute-start(s32[3,72,256]{2,1,0:T(8,128)} %get-tuple-element.86.refs_0_), channel_id=1, source_target_pairs={{0,16},{16,0},{32,48},{48,32},{64,80},{80,64},{96,112},{112,96},{1... | collective-permute-start | bytes 663560 | tf_op jit(solution)/shard_map/ppermute | solution.py:505
  202.6 12.8 %collective-permute-start.23 = (s32[3,72,256]{2,1,0:T(8,128)S(1)}, s32[3,72,256]{2,1,0:T(8,128)S(1)}, u32[]{:S(2)}, u32[]{:S(2)}) collective-permute-start(s32[3,72,256]{2,1,0:T(8,128)S(1)} %collective-permute-done.22.refs_2_), channel_id=1, source_target_pairs={{0,16},{16,0},{32,48},{48,32},{64,80},{80,64},{96,112},{112,96},{1... | collective-permute-start | bytes 663560 | tf_op jit(solution)/shard_map/ppermute | solution.py:505
  205.2 10.2 %collective-permute-start.25 = (s32[3,72,256]{2,1,0:T(8,128)S(1)}, s32[3,72,256]{2,1,0:T(8,128)S(1)}, u32[]{:S(2)}, u32[]{:S(2)}) collective-permute-start(s32[3,72,256]{2,1,0:T(8,128)S(1)} %collective-permute-done.24.refs_4_), channel_id=1, source_target_pairs={{0,16},{16,0},{32,48},{48,32},{64,80},{80,64},{96,112},{112,96},{1... | collective-permute-start | bytes 663560 | tf_op jit(solution)/shard_map/ppermute | solution.py:505
  207.6 7.8 %collective-permute-start.27 = (s32[3,72,256]{2,1,0:T(8,128)S(1)}, s32[3,72,256]{2,1,0:T(8,128)S(1)}, u32[]{:S(2)}, u32[]{:S(2)}) collective-permute-start(s32[3,72,256]{2,1,0:T(8,128)S(1)} %collective-permute-done.26.refs_6_), channel_id=1, source_target_pairs={{0,16},{16,0},{32,48},{48,32},{64,80},{80,64},{96,112},{112,96},{1... | collective-permute-start | bytes 663560 | tf_op jit(solution)/shard_map/ppermute | solution.py:505
  208.4 19.3 %all-to-all-start.2 = ((f32[128,1,32]{2,1,0:T(1,128)}), f32[128,1,32]{2,1,0:T(1,128)S(1)}, u32[]{:S(2)}, u32[]{:S(2)}) async-start(f32[128,1,32]{2,1,0:T(1,128)} %bitcast.12), calls=%async_computation.2 | async-start | bytes 131072 | tf_op jit(solution)/shard_map/all_to_all | solution.py:607
  (41 other events, 243.3 us)
